TPU v7x, 128 devices: a whole 4x4x4 slice. The times are simulated.
128 devices in a mesh: node: 2 (over z_lo), tm: 16 (over z_hi, x, core), space: 4 (over y).
Axes of the slice: x: 4, y: 4, z: 4 (z_hi: 2, z_lo: 2; z = z_hi * 2 + z_lo), core: 2. Of those that a mesh axis runs over, the one named last changes fastest.
Arguments:
- nodes: float32 [16, 4, 32, 256, 256], P('tm', 'node', 'space'), may hold values from -1.5 to 1.5
- prev_final: float32 [16, 32, 256, 256], P('tm', 'space'), may hold values from -6 to 6
- u_init: float32 [32, 256, 256], P('space'), may hold values from -6 to 6
- conductivity: float32 [32, 256, 256], P('space'), may hold values from 0.25 to 16
Outputs:
- new_nodes: float32 [16, 4, 32, 256, 256], P('tm', 'node', 'space')
All inputs are finite; a program needn't handle non-finite values.
Results may differ from a plain program's by a relative error of at most 0.0003.
Values sent between devices are 32-bit elements; how exact they have to be, the bound alone decides.
No kernel may reach another device: no remote copies, remote signals or barrier semaphores. Data moves between devices by JAX's collectives and lax.ppermute only.
A program may use at most 128 MiB of HBM per device.

v0:
```python
import jax
import jax.numpy as jnp
from jax import lax
from jax.sharding import PartitionSpec as P

SWEEPS = 8


radau_points = [0.08858795951270394, 0.4094668644407347, 0.787659461760847, 1.0]


def extended(cells, sides, width):
    for axis, dim in sides:
        count = lax.axis_size(axis)
        ends = count - 1
        head = lax.slice_in_dim(cells, 0, width, axis=dim)
        tail = lax.slice_in_dim(cells, cells.shape[dim] - width, cells.shape[dim], axis=dim)
        cells = jnp.concatenate(
            [
                lax.ppermute(tail, axis, [(i, (i + 1) % count) for i in range(ends)]),
                cells,
                lax.ppermute(head, axis, [((i + 1) % count, i) for i in range(ends)]),
            ],
            axis=dim,
        )
    return cells


def shifted_2(x, axis, by):
    devices = lax.axis_size(axis)
    pairs = [(i, i + by) for i in range(devices) if 0 <= i + by < devices]
    return lax.ppermute(x, axis, pairs)


def mixing_table():
    count_nodes = len(radau_points)
    table = [[0.0] * count_nodes for row_index in range(count_nodes)]
    for column in range(count_nodes):
        coefs = [1.0]
        for other in range(count_nodes):
            if other != column:
                scale = 1.0 / (radau_points[column] - radau_points[other])
                shifted = [0.0] + coefs
                lowered = [value * radau_points[other] for value in coefs] + [0.0]
                coefs = [(shifted[k] - lowered[k]) * scale for k in range(len(shifted))]
        for row_index in range(count_nodes):
            point = radau_points[row_index]
            integral = 0.0
            for power in range(len(coefs)):
                integral = integral + coefs[power] * point ** (power + 1) / (power + 1)
            table[row_index][column] = integral
        table[column][column] = table[column][column] - radau_points[column]
    return table


def from_lower(values, axis):
    axis = axis % values.ndim
    widths = [(0, 0)] * values.ndim
    widths[axis] = (1, 0)
    return lax.slice_in_dim(jnp.pad(values, widths), 0, values.shape[axis], axis=axis)


def from_upper(values, axis):
    axis = axis % values.ndim
    widths = [(0, 0)] * values.ndim
    widths[axis] = (0, 1)
    return lax.slice_in_dim(jnp.pad(values, widths), 1, values.shape[axis] + 1, axis=axis)


def coefficients(conduct_ext):
    centre = conduct_ext[1:-1]
    face_xl = 0.5 * (centre + conduct_ext[:-2])
    face_xr = 0.5 * (centre + conduct_ext[2:])
    padded_y = jnp.pad(centre, ((0, 0), (1, 1), (0, 0)), mode="edge")
    face_yl = 0.5 * (centre + padded_y[:, :-2])
    face_yr = 0.5 * (centre + padded_y[:, 2:])
    padded_z = jnp.pad(centre, ((0, 0), (0, 0), (1, 1)), mode="edge")
    face_zl = 0.5 * (centre + padded_z[:, :, :-2])
    face_zr = 0.5 * (centre + padded_z[:, :, 2:])
    summed = face_xl + face_xr + face_yl + face_yr + face_zl + face_zr
    return (face_xl, face_xr, face_yl, face_yr, face_zl, face_zr, summed)


def neighbours(padded, faces):
    centre = padded[..., 1:-1, :, :]
    result = faces[0] * padded[..., :-2, :, :] + faces[1] * padded[..., 2:, :, :]
    result = result + faces[2] * from_lower(centre, -2) + faces[3] * from_upper(centre, -2)
    result = result + faces[4] * from_lower(centre, -1) + faces[5] * from_upper(centre, -1)
    return result


def fix_edges(conduct_ext, conductivity, margin, position, bricks):
    brick_cells = conductivity.shape[0]
    x_index = jnp.arange(conduct_ext.shape[0])[:, None, None]
    lower_rim = (x_index < margin) & (position == 0)
    upper_rim = (x_index >= margin + brick_cells) & (position == bricks - 1)
    result = jnp.where(lower_rim, conductivity[0:1], conduct_ext)
    return jnp.where(upper_rim, conductivity[-1:], result)


def body(nodes, prev_final, u_init, conductivity):
    own_nodes = nodes[0]
    per_device = own_nodes.shape[0]
    position = lax.axis_index("space")
    bricks = lax.axis_size("space")
    first_node = lax.axis_index("node") * per_device
    weights = jnp.asarray(mixing_table(), jnp.float32)
    own_weights = lax.dynamic_slice_in_dim(weights, first_node, per_device, 1)
    node_diag = lax.dynamic_slice_in_dim(
        jnp.asarray(radau_points, jnp.float32), first_node, per_device, 0
    )[:, None, None, None]
    margin = 1
    conduct_ext = extended(conductivity, (("space", 0),), margin)
    conduct_ext = fix_edges(conduct_ext, conductivity, margin, position, bricks)
    faces_inner = coefficients(conduct_ext)
    padded_nodes = extended(own_nodes, (("space", 1),), margin)
    fluxes = neighbours(padded_nodes, faces_inner) - faces_inner[6] * own_nodes
    partial_value = jnp.einsum(
        "mj,jxyz->mxyz", own_weights, fluxes, precision=lax.Precision.HIGHEST
    )
    summed = lax.psum(partial_value, "node")
    own_sums = lax.dynamic_slice_in_dim(summed, first_node, per_device, 0)
    shifted = shifted_2(prev_final[0], "tm", 1)
    block_start = jnp.where(lax.axis_index("tm") == 0, u_init, shifted)
    right_side = block_start[None] + own_sums
    divisor = 1.0 + node_diag * faces_inner[6]
    iterate = own_nodes
    for repeat_index in range(SWEEPS):
        if repeat_index == 0:
            padded = padded_nodes
        else:
            padded = extended(iterate, (("space", 1),), 1)
        iterate = (right_side + node_diag * neighbours(padded, faces_inner)) / divisor
    return iterate[None]


def solution(mesh):
    in_specs = (
        P("tm", "node", "space", None, None),
        P("tm", "space", None, None),
        P("space", None, None),
        P("space", None, None),
    )
    out_specs = P("tm", "node", "space", None, None)
    return jax.shard_map(body, mesh=mesh, in_specs=in_specs, out_specs=out_specs, check_vma=False)
```

profile of v0, /device:TPU:14, one launch (start us, length us, event | category | flops | bytes accessed | tf_op | source)
XLA Modules:
  0.0 600.6 jit_solution(17579852292148792878)
XLA Ops:
  8.4 3.5 collective-permute-start.1
  14.4 5.4 copy.17
  23.2 3.5 collective-permute-start.3
  26.6 3.4 collective-permute-start.4
  33.4 5.1 collective-permute-done.3
  38.5 3.2 collective-permute-done.4
  41.7 42.8 %fusion.89 = f32[4,8,256,256]{3,0,2,1:T(4,128)} fusion(f32[8,256,256]{2,1,0:T(8,128)S(1)} %get-tuple-element.7, f32[4,4]{0,1:T(4,128)S(1)} %copy-done.12, s32[]{:T(128)S(6)} %select_n.22, f32[1,2,8,256,256]{4,3,2,1,0:T(8,128)} %param.6, f32[2,8,256,256]{3,0,2,1:T(2,128)} %bitcast.25, f32[2,1,256,256]{3,0,2,1:T(2,128)} %collective-permute-done.4, ...), kind=kOutput, calls=%fused_computation.147 | convolution fusion | flops 66060288 | bytes 32506884 | tf_op jit(solution)/shard_map/mj,jxyz->mxyz/dot_general | solution.py:118
  86.8 25.4 %collective-permute-done = f32[8,256,256]{2,1,0:T(8,128)} collective-permute-done((f32[8,256,256]{2,1,0:T(8,128)}, f32[8,256,256]{2,1,0:T(8,128)}, u32[]{:S(2)}, u32[]{:S(2)}) %collective-permute-start) | collective-permute-done | bytes 2097184 | tf_op jit(solution)/shard_map/ppermute | solution.py:32
  112.2 3.2 broadcast_select_fusion
  115.4 191.0 %all-reduce.34.cloned.1.call-done = f32[4,8,256,256]{3,0,2,1:T(4,128)} async-done(((f32[4,8,256,256]{3,0,2,1:T(4,128)}), f32[4,8,256,256]{3,0,2,1:T(4,128)}) %all-reduce.34.cloned.1.call-update) | async-done | bytes 8388624 | tf_op jit(solution)/shard_map/psum | solution.py:121
  306.4 22.7 %fusion.88 = (f32[2,8,256,256]{3,0,2,1:T(2,128)}, f32[2,8,256,256]{3,0,2,1:T(2,128)}) fusion(f32[8,256,256]{2,1,0:T(8,128)S(1)} %get-tuple-element.7, f32[2]{0:T(128)S(1)} %dynamic_slice.11, f32[4,8,256,256]{3,0,2,1:T(4,128)} %all-reduce.34.cloned.1.call-done, s32[]{:T(128)S(6)} %select_n.22, f32[8,256,256]{2,1,0:T(8,128)} %broadcast_select_fusion, ...), kind=kLoop, calls=%fused_computation.145 | loop fusion | flops 19922944 | bytes 34603020 | tf_op jit(solution)/shard_map/div | solution.py:133
  330.7 3.4 collective-permute-start.5
  336.6 9.7 %collective-permute-done.5 = f32[2,1,256,256]{3,0,2,1:T(2,128)S(1)} collective-permute-done((f32[2,1,256,256]{3,0,2,1:T(2,128)S(1)}, f32[2,1,256,256]{3,0,2,1:T(2,128)S(1)}, u32[]{:S(2)}, u32[]{:S(2)}) %collective-permute-start.5) | collective-permute-done | bytes 524320 | tf_op jit(solution)/shard_map/ppermute | solution.py:20
  346.2 3.1 collective-permute-done.6
  350.2 20.3 %add_divide_fusion.6 = f32[2,8,256,256]{3,0,2,1:T(2,128)} fusion(f32[2,8,256,256]{3,0,2,1:T(2,128)} %get-tuple-element.6, f32[2,8,256,256]{3,0,2,1:T(2,128)} %get-tuple-element.5, f32[2,1,256,256]{3,0,2,1:T(2,128)} %copy-done.10, f32[2,1,256,256]{3,0,2,1:T(2,128)S(1)} %collective-permute-done.5, f32[8,256,256]{2,1,0:T(8,128)} %copy-done.1, ...), kind=kLoop, calls=%fused_computation.143 | loop fusion | flops 18874368 | bytes 28311560 | tf_op jit(solution)/shard_map/div | solution.py:133
  372.0 3.1 collective-permute-start.7
  377.9 8.5 %collective-permute-done.7 = f32[2,1,256,256]{3,0,2,1:T(2,128)S(1)} collective-permute-done((f32[2,1,256,256]{3,0,2,1:T(2,128)S(1)}, f32[2,1,256,256]{3,0,2,1:T(2,128)S(1)}, u32[]{:S(2)}, u32[]{:S(2)}) %collective-permute-start.7) | collective-permute-done | bytes 524320 | tf_op jit(solution)/shard_map/ppermute | solution.py:20
  389.3 20.1 %add_divide_fusion.5 = f32[2,8,256,256]{3,0,2,1:T(2,128)} fusion(f32[2,8,256,256]{3,0,2,1:T(2,128)S(1)} %copy-done, f32[2,8,256,256]{3,0,2,1:T(2,128)} %add_divide_fusion.6, f32[2,1,256,256]{3,0,2,1:T(2,128)} %collective-permute-done.8, f32[2,1,256,256]{3,0,2,1:T(2,128)S(1)} %collective-permute-done.7, f32[8,256,256]{2,1,0:T(8,128)} %copy-done.1, ...), kind=kLoop, calls=%fused_computation.142 | loop fusion | flops 18874368 | bytes 28311560 | tf_op jit(solution)/shard_map/div | solution.py:133
  416.8 7.3 %collective-permute-done.10 = f32[2,1,256,256]{3,0,2,1:T(2,128)S(1)} collective-permute-done((f32[2,1,256,256]{3,0,2,1:T(2,128)S(1)}, f32[2,1,256,256]{3,0,2,1:T(2,128)S(1)}, u32[]{:S(2)}, u32[]{:S(2)}) %collective-permute-start.10) | collective-permute-done | bytes 524320 | tf_op jit(solution)/shard_map/ppermute | solution.py:22
  426.7 20.3 %add_divide_fusion.4 = f32[2,8,256,256]{3,0,2,1:T(2,128)} fusion(f32[2,8,256,256]{3,0,2,1:T(2,128)S(1)} %copy-done, f32[2,8,256,256]{3,0,2,1:T(2,128)} %add_divide_fusion.5, f32[2,1,256,256]{3,0,2,1:T(2,128)S(1)} %collective-permute-done.10, f32[2,1,256,256]{3,0,2,1:T(2,128)} %collective-permute-done.9, f32[8,256,256]{2,1,0:T(8,128)} %copy-done.1, ...), kind=kLoop, calls=%fused_computation.141 | loop fusion | flops 18874368 | bytes 28311560 | tf_op jit(solution)/shard_map/div | solution.py:133
  454.5 6.1 %collective-permute-done.11 = f32[2,1,256,256]{3,0,2,1:T(2,128)S(1)} collective-permute-done((f32[2,1,256,256]{3,0,2,1:T(2,128)S(1)}, f32[2,1,256,256]{3,0,2,1:T(2,128)S(1)}, u32[]{:S(2)}, u32[]{:S(2)}) %collective-permute-start.11) | collective-permute-done | bytes 524320 | tf_op jit(solution)/shard_map/ppermute | solution.py:20
  463.5 20.1 %add_divide_fusion.3 = f32[2,8,256,256]{3,0,2,1:T(2,128)} fusion(f32[2,8,256,256]{3,0,2,1:T(2,128)S(1)} %copy-done, f32[2,8,256,256]{3,0,2,1:T(2,128)} %add_divide_fusion.4, f32[2,1,256,256]{3,0,2,1:T(2,128)} %collective-permute-done.12, f32[2,1,256,256]{3,0,2,1:T(2,128)S(1)} %collective-permute-done.11, f32[8,256,256]{2,1,0:T(8,128)} %copy-done.1, ...), kind=kLoop, calls=%fused_computation.140 | loop fusion | flops 18874368 | bytes 28311560 | tf_op jit(solution)/shard_map/div | solution.py:133
  487.9 3.1 collective-permute-start.14
  491.0 5.2 collective-permute-done.13
  499.1 20.3 %add_divide_fusion.2 = f32[2,8,256,256]{3,0,2,1:T(2,128)} fusion(f32[2,8,256,256]{3,0,2,1:T(2,128)S(1)} %copy-done, f32[2,8,256,256]{3,0,2,1:T(2,128)} %add_divide_fusion.3, f32[2,1,256,256]{3,0,2,1:T(2,128)} %collective-permute-done.14, f32[2,1,256,256]{3,0,2,1:T(2,128)S(1)} %collective-permute-done.13, f32[8,256,256]{2,1,0:T(8,128)} %copy-done.1, ...), kind=kLoop, calls=%fused_computation.139 | loop fusion | flops 18874368 | bytes 28311560 | tf_op jit(solution)/shard_map/div | solution.py:133
  522.9 4.2 collective-permute-start.16
  527.1 4.9 collective-permute-done.15
  534.1 20.1 %add_divide_fusion.1 = f32[2,8,256,256]{3,0,2,1:T(2,128)} fusion(f32[2,8,256,256]{3,0,2,1:T(2,128)S(1)} %copy-done, f32[2,8,256,256]{3,0,2,1:T(2,128)} %add_divide_fusion.2, f32[2,1,256,256]{3,0,2,1:T(2,128)} %collective-permute-done.16, f32[2,1,256,256]{3,0,2,1:T(2,128)S(1)} %collective-permute-done.15, f32[8,256,256]{2,1,0:T(8,128)} %copy-done.1, ...), kind=kLoop, calls=%fused_computation.138 | loop fusion | flops 18874368 | bytes 28311560 | tf_op jit(solution)/shard_map/div | solution.py:133
  557.6 4.0 collective-permute-start.18
  561.6 5.2 collective-permute-done.17
  568.8 20.3 %fusion.92 = f32[1,2,8,256,256]{4,1,3,2,0:T(2,128)} fusion(f32[2,8,256,256]{3,0,2,1:T(2,128)S(1)} %copy-done, f32[2,8,256,256]{3,0,2,1:T(2,128)} %add_divide_fusion.1, f32[2,1,256,256]{3,0,2,1:T(2,128)} %collective-permute-done.18, f32[2,1,256,256]{3,0,2,1:T(2,128)S(1)} %collective-permute-done.17, f32[8,256,256]{2,1,0:T(8,128)} %copy-done.1, ...), kind=kLoop, calls=%fused_computation.150 | loop fusion | flops 18874368 | bytes 28311560 | tf_op jit(solution)/shard_map/broadcast_in_dim | solution.py:134
  589.1 4.7 copy.8
  (63 shorter events, 63.9 us)
Async XLA Ops:
  6.5 299.8 %all-reduce.34.cloned.1.call-start = ((), (), s32[]{:S(2)}) async-start(), calls=%async_computation | async-start | bytes 16777216 | tf_op jit(solution)/shard_map/psum | solution.py:121
  8.4 21.7 %collective-permute-start.1 = (f32[1,256,256]{2,1,0:T(8,128)}, f32[1,256,256]{2,1,0:T(8,128)S(1)}, u32[]{:S(2)}, u32[]{:S(2)}) collective-permute-start(f32[1,256,256]{2,1,0:T(8,128)} %get-tuple-element.36), channel_id=1, source_target_pairs={{0,1},{1,2},{2,3},{4,5},{5,6},{6,7},{8,9},{9,10},{10,11},{12,13},{... | collective-permute-start | bytes 786440 | tf_op jit(solution)/shard_map/ppermute | solution.py:20
  11.8 18.2 %copy-start.9 = (f32[8,256,256]{2,1,0:T(8,128)S(1)}, f32[8,256,256]{2,1,0:T(8,128)}, u32[]{:S(2)}) copy-start(f32[8,256,256]{2,1,0:T(8,128)} %param.9) | copy-start | bytes 6291460
  11.9 18.2 %collective-permute-start.2 = (f32[1,256,256]{2,1,0:T(8,128)S(1)}, f32[1,256,256]{2,1,0:T(8,128)S(1)}, u32[]{:S(2)}, u32[]{:S(2)}) collective-permute-start(f32[1,256,256]{2,1,0:T(8,128)S(1)} %get-tuple-element.37), channel_id=1, source_target_pairs={{1,0},{2,1},{3,2},{5,4},{6,5},{7,6},{9,8},{10,9},{11,10},{13,12},{... | collective-permute-start | bytes 786440 | tf_op jit(solution)/shard_map/ppermute | solution.py:22
  19.8 2.0 copy-start.8
  23.2 15.3 %collective-permute-start.3 = (f32[2,1,256,256]{3,0,2,1:T(2,128)}, f32[2,1,256,256]{3,0,2,1:T(2,128)}, u32[]{:S(2)}, u32[]{:S(2)}) collective-permute-start(f32[2,1,256,256]{3,0,2,1:T(2,128)} %get-tuple-element.28), channel_id=1, source_target_pairs={{0,1},{1,2},{2,3},{4,5},{5,6},{6,7},{8,9},{9,10},{10,11},{12,13},{... | collective-permute-start | bytes 1572872 | tf_op jit(solution)/shard_map/ppermute | solution.py:20
  26.6 15.0 %collective-permute-start.4 = (f32[2,1,256,256]{3,0,2,1:T(2,128)}, f32[2,1,256,256]{3,0,2,1:T(2,128)}, u32[]{:S(2)}, u32[]{:S(2)}) collective-permute-start(f32[2,1,256,256]{3,0,2,1:T(2,128)} %get-tuple-element.29), channel_id=1, source_target_pairs={{1,0},{2,1},{3,2},{5,4},{6,5},{7,6},{9,8},{10,9},{11,10},{13,12},{... | collective-permute-start | bytes 1572872 | tf_op jit(solution)/shard_map/ppermute | solution.py:22
  30.9 10.8 %copy-start.12 = (f32[4,4]{0,1:T(4,128)S(1)}, f32[4,4]{0,1:T(4,128)}, u32[]{:S(2)}) copy-start(f32[4,4]{0,1:T(4,128)} %constant.37.clone) | copy-start | bytes 196
  33.3 8.4 %copy-start.2 = (f32[8,256,256]{2,1,0:T(8,128)}, f32[8,256,256]{2,1,0:T(8,128)S(1)}, u32[]{:S(2)}) copy-start(f32[8,256,256]{2,1,0:T(8,128)S(1)} %get-tuple-element.8) | copy-start | bytes 6291460
  33.3 8.4 %copy-start.3 = (f32[8,256,256]{2,1,0:T(8,128)}, f32[8,256,256]{2,1,0:T(8,128)S(1)}, u32[]{:S(2)}) copy-start(f32[8,256,256]{2,1,0:T(8,128)S(1)} %get-tuple-element.9) | copy-start | bytes 6291460
  33.3 8.4 %copy-start.4 = (f32[8,256,256]{2,1,0:T(8,128)}, f32[8,256,256]{2,1,0:T(8,128)S(1)}, u32[]{:S(2)}) copy-start(f32[8,256,256]{2,1,0:T(8,128)S(1)} %get-tuple-element.10) | copy-start | bytes 6291460
  33.3 8.4 %copy-start.5 = (f32[8,256,256]{2,1,0:T(8,128)}, f32[8,256,256]{2,1,0:T(8,128)S(1)}, u32[]{:S(2)}) copy-start(f32[8,256,256]{2,1,0:T(8,128)S(1)} %get-tuple-element.11) | copy-start | bytes 6291460
  33.3 8.4 %copy-start.6 = (f32[8,256,256]{2,1,0:T(8,128)}, f32[8,256,256]{2,1,0:T(8,128)S(1)}, u32[]{:S(2)}) copy-start(f32[8,256,256]{2,1,0:T(8,128)S(1)} %get-tuple-element.12) | copy-start | bytes 6291460
  33.3 8.4 %copy-start.7 = (f32[8,256,256]{2,1,0:T(8,128)}, f32[8,256,256]{2,1,0:T(8,128)S(1)}, u32[]{:S(2)}) copy-start(f32[8,256,256]{2,1,0:T(8,128)S(1)} %get-tuple-element.13) | copy-start | bytes 6291460
  33.4 273.0 %copy-start.1 = (f32[8,256,256]{2,1,0:T(8,128)}, f32[8,256,256]{2,1,0:T(8,128)S(1)}, u32[]{:S(2)}) copy-start(f32[8,256,256]{2,1,0:T(8,128)S(1)} %get-tuple-element.7) | copy-start | bytes 6291460
  84.5 2.2 copy-start.11
  84.5 27.7 %collective-permute-start = (f32[8,256,256]{2,1,0:T(8,128)}, f32[8,256,256]{2,1,0:T(8,128)}, u32[]{:S(2)}, u32[]{:S(2)}) collective-permute-start(f32[8,256,256]{2,1,0:T(8,128)} %bitcast.27), channel_id=1, source_target_pairs={{0,4},{4,8},{8,12},{12,16},{16,20},{20,24},{24,28},{28,32},{32,36}... | collective-permute-start | bytes 6291464 | tf_op jit(solution)/shard_map/ppermute | solution.py:32
  330.7 15.6 %collective-permute-start.5 = (f32[2,1,256,256]{3,0,2,1:T(2,128)S(1)}, f32[2,1,256,256]{3,0,2,1:T(2,128)S(1)}, u32[]{:S(2)}, u32[]{:S(2)}) collective-permute-start(f32[2,1,256,256]{3,0,2,1:T(2,128)S(1)} %get-tuple-element.26), channel_id=1, source_target_pairs={{0,1},{1,2},{2,3},{4,5},{5,6},{6,7},{8,9},{9,10},{10,11},{12,13},{... | collective-permute-start | bytes 1572872 | tf_op jit(solution)/shard_map/ppermute | solution.py:20
  334.1 15.3 %collective-permute-start.6 = (f32[2,1,256,256]{3,0,2,1:T(2,128)S(1)}, f32[2,1,256,256]{3,0,2,1:T(2,128)S(1)}, u32[]{:S(2)}, u32[]{:S(2)}) collective-permute-start(f32[2,1,256,256]{3,0,2,1:T(2,128)S(1)} %get-tuple-element.27), channel_id=1, source_target_pairs={{1,0},{2,1},{3,2},{5,4},{6,5},{7,6},{9,8},{10,9},{11,10},{13,12},{... | collective-permute-start | bytes 1572872 | tf_op jit(solution)/shard_map/ppermute | solution.py:22
  350.2 39.2 %copy-start = (f32[2,8,256,256]{3,0,2,1:T(2,128)S(1)}, f32[2,8,256,256]{3,0,2,1:T(2,128)}, u32[]{:S(2)}) copy-start(f32[2,8,256,256]{3,0,2,1:T(2,128)} %get-tuple-element.6) | copy-start | bytes 12582916
  372.0 14.4 %collective-permute-start.7 = (f32[2,1,256,256]{3,0,2,1:T(2,128)S(1)}, f32[2,1,256,256]{3,0,2,1:T(2,128)S(1)}, u32[]{:S(2)}, u32[]{:S(2)}) collective-permute-start(f32[2,1,256,256]{3,0,2,1:T(2,128)S(1)} %get-tuple-element.24), channel_id=1, source_target_pairs={{0,1},{1,2},{2,3},{4,5},{5,6},{6,7},{8,9},{9,10},{10,11},{12,13},{... | collective-permute-start | bytes 1572872 | tf_op jit(solution)/shard_map/ppermute | solution.py:20
  375.1 14.2 %collective-permute-start.8 = (f32[2,1,256,256]{3,0,2,1:T(2,128)S(1)}, f32[2,1,256,256]{3,0,2,1:T(2,128)}, u32[]{:S(2)}, u32[]{:S(2)}) collective-permute-start(f32[2,1,256,256]{3,0,2,1:T(2,128)S(1)} %get-tuple-element.25), channel_id=1, source_target_pairs={{1,0},{2,1},{3,2},{5,4},{6,5},{7,6},{9,8},{10,9},{11,10},{13,12},{... | collective-permute-start | bytes 1572872 | tf_op jit(solution)/shard_map/ppermute | solution.py:22
  411.0 13.2 %collective-permute-start.10 = (f32[2,1,256,256]{3,0,2,1:T(2,128)S(1)}, f32[2,1,256,256]{3,0,2,1:T(2,128)S(1)}, u32[]{:S(2)}, u32[]{:S(2)}) collective-permute-start(f32[2,1,256,256]{3,0,2,1:T(2,128)S(1)} %get-tuple-element.23), channel_id=1, source_target_pairs={{1,0},{2,1},{3,2},{5,4},{6,5},{7,6},{9,8},{10,9},{11,10},{13,12},{... | collective-permute-start | bytes 1572872 | tf_op jit(solution)/shard_map/ppermute | solution.py:22
  413.7 13.0 %collective-permute-start.9 = (f32[2,1,256,256]{3,0,2,1:T(2,128)S(1)}, f32[2,1,256,256]{3,0,2,1:T(2,128)}, u32[]{:S(2)}, u32[]{:S(2)}) collective-permute-start(f32[2,1,256,256]{3,0,2,1:T(2,128)S(1)} %get-tuple-element.22), channel_id=1, source_target_pairs={{0,1},{1,2},{2,3},{4,5},{5,6},{6,7},{8,9},{9,10},{10,11},{12,13},{... | collective-permute-start | bytes 1572872 | tf_op jit(solution)/shard_map/ppermute | solution.py:20
  448.6 12.0 %collective-permute-start.11 = (f32[2,1,256,256]{3,0,2,1:T(2,128)S(1)}, f32[2,1,256,256]{3,0,2,1:T(2,128)S(1)}, u32[]{:S(2)}, u32[]{:S(2)}) collective-permute-start(f32[2,1,256,256]{3,0,2,1:T(2,128)S(1)} %get-tuple-element.20), channel_id=1, source_target_pairs={{0,1},{1,2},{2,3},{4,5},{5,6},{6,7},{8,9},{9,10},{10,11},{12,13},{... | collective-permute-start | bytes 1572872 | tf_op jit(solution)/shard_map/ppermute | solution.py:20
  451.7 11.8 %collective-permute-start.12 = (f32[2,1,256,256]{3,0,2,1:T(2,128)S(1)}, f32[2,1,256,256]{3,0,2,1:T(2,128)}, u32[]{:S(2)}, u32[]{:S(2)}) collective-permute-start(f32[2,1,256,256]{3,0,2,1:T(2,128)S(1)} %get-tuple-element.21), channel_id=1, source_target_pairs={{1,0},{2,1},{3,2},{5,4},{6,5},{7,6},{9,8},{10,9},{11,10},{13,12},{... | collective-permute-start | bytes 1572872 | tf_op jit(solution)/shard_map/ppermute | solution.py:22
  485.1 11.1 %collective-permute-start.13 = (f32[2,1,256,256]{3,0,2,1:T(2,128)S(1)}, f32[2,1,256,256]{3,0,2,1:T(2,128)S(1)}, u32[]{:S(2)}, u32[]{:S(2)}) collective-permute-start(f32[2,1,256,256]{3,0,2,1:T(2,128)S(1)} %get-tuple-element.18), channel_id=1, source_target_pairs={{0,1},{1,2},{2,3},{4,5},{5,6},{6,7},{8,9},{9,10},{10,11},{12,13},{... | collective-permute-start | bytes 1572872 | tf_op jit(solution)/shard_map/ppermute | solution.py:20
  487.9 11.2 %collective-permute-start.14 = (f32[2,1,256,256]{3,0,2,1:T(2,128)S(1)}, f32[2,1,256,256]{3,0,2,1:T(2,128)}, u32[]{:S(2)}, u32[]{:S(2)}) collective-permute-start(f32[2,1,256,256]{3,0,2,1:T(2,128)S(1)} %get-tuple-element.19), channel_id=1, source_target_pairs={{1,0},{2,1},{3,2},{5,4},{6,5},{7,6},{9,8},{10,9},{11,10},{13,12},{... | collective-permute-start | bytes 1572872 | tf_op jit(solution)/shard_map/ppermute | solution.py:22
  521.0 11.1 %collective-permute-start.15 = (f32[2,1,256,256]{3,0,2,1:T(2,128)S(1)}, f32[2,1,256,256]{3,0,2,1:T(2,128)S(1)}, u32[]{:S(2)}, u32[]{:S(2)}) collective-permute-start(f32[2,1,256,256]{3,0,2,1:T(2,128)S(1)} %get-tuple-element.16), channel_id=1, source_target_pairs={{0,1},{1,2},{2,3},{4,5},{5,6},{6,7},{8,9},{9,10},{10,11},{12,13},{... | collective-permute-start | bytes 1572872 | tf_op jit(solution)/shard_map/ppermute | solution.py:20
  522.9 11.2 %collective-permute-start.16 = (f32[2,1,256,256]{3,0,2,1:T(2,128)S(1)}, f32[2,1,256,256]{3,0,2,1:T(2,128)}, u32[]{:S(2)}, u32[]{:S(2)}) collective-permute-start(f32[2,1,256,256]{3,0,2,1:T(2,128)S(1)} %get-tuple-element.17), channel_id=1, source_target_pairs={{1,0},{2,1},{3,2},{5,4},{6,5},{7,6},{9,8},{10,9},{11,10},{13,12},{... | collective-permute-start | bytes 1572872 | tf_op jit(solution)/shard_map/ppermute | solution.py:22
  555.7 11.1 %collective-permute-start.17 = (f32[2,1,256,256]{3,0,2,1:T(2,128)S(1)}, f32[2,1,256,256]{3,0,2,1:T(2,128)S(1)}, u32[]{:S(2)}, u32[]{:S(2)}) collective-permute-start(f32[2,1,256,256]{3,0,2,1:T(2,128)S(1)} %get-tuple-element.14), channel_id=1, source_target_pairs={{0,1},{1,2},{2,3},{4,5},{5,6},{6,7},{8,9},{9,10},{10,11},{12,13},{... | collective-permute-start | bytes 1572872 | tf_op jit(solution)/shard_map/ppermute | solution.py:20
  557.6 11.2 %collective-permute-start.18 = (f32[2,1,256,256]{3,0,2,1:T(2,128)S(1)}, f32[2,1,256,256]{3,0,2,1:T(2,128)}, u32[]{:S(2)}, u32[]{:S(2)}) collective-permute-start(f32[2,1,256,256]{3,0,2,1:T(2,128)S(1)} %get-tuple-element.15), channel_id=1, source_target_pairs={{1,0},{2,1},{3,2},{5,4},{6,5},{7,6},{9,8},{10,9},{11,10},{13,12},{... | collective-permute-start | bytes 1572872 | tf_op jit(solution)/shard_map/ppermute | solution.py:22
  (1 other events, 0.8 us)
Sparse Core Ops, SparseCore 0:
  84.6 221.6 all-reduce.33
where the time goes:
time: 603 us; the launch traced here: 601 us
  waiting for transfers between devices  290 us (48%)
  other arithmetic  170 us (28%)
  starting transfers between devices  56.3 us (9%)
  matrix products  42.8 us (7%)
  local copies, waits for them, and re-layouts  27.7 us (5%)
  between operations  13.8 us (2%)
    psum x1, waiting for transfers between devices, body(): summed = lax.psum(partial_value, 'node')  191 us
    div x7, other arithmetic, body(): (right_side + node_diag * neighbours(padded, faces_inner)) / divisor  144 us
    ppermute x9, waiting for transfers between devices, extended(): lax.ppermute(tail, axis, [(i, (i + 1) % count) for i in range(ends)])  47.2 us
    dot_general x1, matrix products, body(): jnp.einsum('mj,jxyz->mxyz', own_weights, fluxes, precision=lax.Precision....  42.8 us
    ppermute x9, starting transfers between devices, extended(): lax.ppermute(head, axis, [((i + 1) % count, i) for i in range(ends)])  27.9 us
    ppermute x9, waiting for transfers between devices, extended(): lax.ppermute(head, axis, [((i + 1) % count, i) for i in range(ends)])  26.4 us
    ppermute x9, starting transfers between devices, extended(): lax.ppermute(tail, axis, [(i, (i + 1) % count) for i in range(ends)])  26.2 us
    ppermute x1, waiting for transfers between devices, shifted_2(): return lax.ppermute(x, axis, pairs)  25.4 us
  transfers between devices with their start and end apart: 20, of which 18 were waited for; matrix products, arithmetic and copies ran while one was open for 2% of the time, Pallas kernels for 0%

commit v1 on v0

v1 whole, which is shorter than its diff:
```python
import functools

import jax
import jax.numpy as jnp
from jax import lax
from jax.experimental import pallas as pl
from jax.experimental.pallas import tpu as pltpu
from jax.sharding import PartitionSpec as P

radau_points = [0.08858795951270394, 0.4094668644407347, 0.787659461760847, 1.0]

Q = 17
ROWS = 8 * Q
PARTS = ((0, 0, 128), (120, 8, 128))
NY = 256
NZ = 256
PLANES = 8
F32 = jnp.float32


def mixing_table():
    count_nodes = len(radau_points)
    table = [[0.0] * count_nodes for row_index in range(count_nodes)]
    for column in range(count_nodes):
        coefs = [1.0]
        for other in range(count_nodes):
            if other != column:
                scale = 1.0 / (radau_points[column] - radau_points[other])
                shifted = [0.0] + coefs
                lowered = [value * radau_points[other] for value in coefs] + [0.0]
                coefs = [(shifted[k] - lowered[k]) * scale for k in range(len(shifted))]
        for row_index in range(count_nodes):
            point = radau_points[row_index]
            integral = 0.0
            for power in range(len(coefs)):
                integral = integral + coefs[power] * point ** (power + 1) / (power + 1)
            table[row_index][column] = integral
        table[column][column] = table[column][column] - radau_points[column]
    return table


WEIGHTS = mixing_table()

ANY = pl.BlockSpec(memory_space=pl.ANY)
VM = pl.BlockSpec(memory_space=pltpu.VMEM)


def vshape(planes):
    return pltpu.VMEM((planes, Q, 8, NZ), F32)


HB = pl.BlockSpec(memory_space=pltpu.HBM)


def pin(x):
    return pltpu.with_memory_space_constraint(x, pltpu.VMEM)


def place(x, where):
    if where is False:
        return x
    return pin(x) if where else pltpu.with_memory_space_constraint(x, pltpu.HBM)


TOKEN = pltpu.VMEM((8, 128), F32)


def with_token(kernel):
    def run(before, *refs):
        ins = refs[: run.ins]
        rest = refs[run.ins + run.skip :]
        rest[run.outs][...] = before[...]
        kernel(*ins, *rest[: run.outs], *rest[run.outs + 1 :])

    return run


class Order:
    def __init__(self):
        self.token = jnp.zeros((8, 128), F32)

    def call(self, name, kernel, outs, ins, scratch, limit_mib, us, aliases=None, after=()):
        run = with_token(kernel)
        run.ins, run.outs, run.skip = len(ins), len(outs), len(after)
        ins = ins + [(a, False) for a in after]
        operands = [pin(self.token)] + [place(a, where) for a, where in ins]
        *results, self.token = pl.pallas_call(
            run,
            out_shape=[o if s is VM else jax.ShapeDtypeStruct(o, F32) for o, s in outs] + [TOKEN],
            in_specs=[VM] + [{True: VM, None: HB, False: ANY}[where] for a, where in ins],
            out_specs=[s for o, s in outs] + [VM],
            scratch_shapes=scratch,
            input_output_aliases={k + 1: v for k, v in (aliases or {}).items()},
            compiler_params=pltpu.CompilerParams(vmem_limit_bytes=limit_mib << 20),
            cost_estimate=pl.CostEstimate(flops=int(us * 1e9), bytes_accessed=0, transcendentals=0),
            name=name,
        )(*operands)
        return results


SCALE = 1_500_000


def zprev(v):
    return pltpu.roll(v, 1, axis=1)


def znext(v):
    return pltpu.roll(v, NZ - 1, axis=1)


def sdown(v):
    return pltpu.roll(v, 1, axis=0)


def sup(v):
    return pltpu.roll(v, 7, axis=0)


def rows_of(buf, plane, r):
    return jnp.concatenate([buf[lane, plane, pl.ds(r, 8, stride=Q), :] for lane in range(2)], axis=-1)


def lane_copies(src_plane, dst_plane, sems):
    return [
        pltpu.make_async_copy(src_plane.at[:, pl.ds(128 * lane, 128)], dst_plane(lane), sems.at[lane])
        for lane in range(2)
    ]


def pick(table_low, table_high, node):
    return jnp.where(node == 0, jnp.float32(table_low), jnp.float32(table_high))


def own_scale(m, node):
    return pick(radau_points[m], radau_points[2 + m], node)


def inv_scale(m, node):
    return pick(1.0 / radau_points[m], 1.0 / radau_points[2 + m], node)


def weights_for(node):
    remote = [[pick(WEIGHTS[2 + m][j], WEIGHTS[m][2 + j], node) for j in range(2)] for m in range(2)]
    local = [[pick(WEIGHTS[m][j], WEIGHTS[2 + m][2 + j], node) for j in range(2)] for m in range(2)]
    return remote, local


class Rows:
    def __init__(self, k_at, y0):
        self.k_at = k_at
        self.first = y0 == 0
        self.last = y0 + ROWS == NY
        sub = lax.broadcasted_iota(jnp.int32, (8, NZ), 0)
        lane = lax.broadcasted_iota(jnp.int32, (8, NZ), 1)
        self.top = sub == 0
        self.bottom = sub == 7
        self.left = lane == 0
        self.right = lane == NZ - 1
        kc = k_at(0)
        kb = sdown(k_at(Q - 1))
        face = 0.5 * (kb + kc)
        if self.first:
            self.prev_sum = jnp.where(self.top, kc, face)
            self.prev = jnp.where(self.top, 0.0, face)
        else:
            self.prev_sum = face
            self.prev = face
        self.kc = kc

    def step(self, r):
        kc = self.kc
        kn = self.k_at(r + 1) if r < Q - 1 else sup(self.k_at(0))
        face = 0.5 * (kc + kn)
        face_sum = face
        if r == Q - 1:
            if self.last:
                face_sum = jnp.where(self.bottom, kc, face)
            face = jnp.where(self.bottom, 0.0, face)
        zface = 0.5 * (kc + znext(kc))
        zsum = jnp.where(self.right, kc, zface) + jnp.where(self.left, kc, zprev(zface))
        zface = jnp.where(self.right, 0.0, zface)
        total = self.prev_sum + face_sum + zsum
        below = self.prev
        self.prev = face
        self.prev_sum = face_sum
        self.kc = kn
        return kc, below, face, zface, total


def flux_rows(k_at, k_low, k_up, us, u_low, u_up, y0, emit):
    rows = Rows(k_at, y0)
    state = [(u(0), sdown(u(Q - 1))) for u in us]
    for r in range(Q):
        kc, below, face, zface, total = rows.step(r)
        fxl = 0.5 * (kc + k_low(r))
        fxu = 0.5 * (kc + k_up(r))
        total = total + (fxl + fxu)
        fluxes = []
        for j in range(2):
            uc, ub = state[j]
            un = us[j](r + 1) if r < Q - 1 else sup(us[j](0))
            n = fxl * u_low[j](r) + fxu * u_up[j](r)
            n = n + below * ub + face * un
            n = n + zface * znext(uc) + zprev(zface * uc)
            fluxes.append(n - total * uc)
            state[j] = (un, uc)
        emit(r, fluxes)


def inner_kernel(y0, offset0, offset1, nodes, cond, u0, kp, rem0, rem1, loc0, loc1, buf, sems):
    node = lax.axis_index("node")
    remote, local = weights_for(node)
    sources = [nodes.at[0, 0], nodes.at[0, 1], cond]

    def copies(p):
        out = []
        for a in range(3):
            out += lane_copies(
                sources[a].at[p, pl.ds(y0, ROWS), :], lambda lane, a=a: buf.at[lane, 3 * p + a], sems.at[p, a]
            )
        return out

    for p in range(PLANES):
        for c in copies(p):
            c.start()

    def convert(p, carry):
        for c in copies(p):
            c.wait()
        for r in range(Q):
            u0[p, r] = rows_of(buf, 3 * p, r)
            u0[PLANES + p, r] = rows_of(buf, 3 * p + 1, r)
            kp[p, r] = rows_of(buf, 3 * p + 2, r)
        return carry

    lax.fori_loop(0, PLANES, convert, 0)

    def plane(i, carry):
        p = i + 1

        def emit(r, f):
            rem0[i + offset0, r] = remote[0][0] * f[0] + remote[0][1] * f[1]
            rem1[i + offset1, r] = remote[1][0] * f[0] + remote[1][1] * f[1]
            loc0[i, r] = local[0][0] * f[0] + local[0][1] * f[1]
            loc1[i, r] = local[1][0] * f[0] + local[1][1] * f[1]

        at = lambda j, d: (lambda r: u0[j * PLANES + p + d, r])
        flux_rows(
            lambda r: kp[p, r],
            lambda r: kp[p - 1, r],
            lambda r: kp[p + 1, r],
            [at(0, 0), at(1, 0)],
            [at(0, -1), at(1, -1)],
            [at(0, 1), at(1, 1)],
            y0,
            emit,
        )
        return carry

    lax.fori_loop(0, PLANES - 2, plane, 0)


def faces_kernel(nodes, cond, na, nb, fa, fb, sems):
    even = lax.rem(lax.axis_index("space"), 2) == 0

    def copies(high_near, high_far, low_near, low_far):
        pairs = []
        for (near, far), (first, second) in (((high_near, high_far), (PLANES - 1, PLANES - 2)), ((low_near, low_far), (0, 1))):
            pairs += [(cond.at[first], near.at[0]), (cond.at[second], far.at[0])]
            for j in range(2):
                pairs += [(nodes.at[0, j, first], near.at[1 + j]), (nodes.at[0, j, second], far.at[1 + j])]
        return [pltpu.make_async_copy(src, dst, sems.at[i]) for i, (src, dst) in enumerate(pairs)]

    @pl.when(even)
    def _():
        for c in copies(na, fa, nb, fb):
            c.start()

    @pl.when(jnp.logical_not(even))
    def _():
        for c in copies(nb, fb, na, fa):
            c.start()

    for c in copies(na, fa, nb, fb):
        c.wait()


def halo_copies(near, planes, y0, buf, base, sems):
    out = []
    for i, p in enumerate(planes):
        out += lane_copies(
            near.at[p, pl.ds(y0, ROWS), :], lambda lane, i=i: buf.at[lane, base + i], sems.at[base + i]
        )
    return out


def begin_halos(na, nb, planes, y0, buf, sems):
    even = lax.rem(lax.axis_index("space"), 2) == 0
    n = len(planes)

    @pl.when(even)
    def _():
        for c in halo_copies(nb, planes, y0, buf, 0, sems) + halo_copies(na, planes, y0, buf, n, sems):
            c.start()

    @pl.when(jnp.logical_not(even))
    def _():
        for c in halo_copies(na, planes, y0, buf, 0, sems) + halo_copies(nb, planes, y0, buf, n, sems):
            c.start()


def end_halos(na, nb, planes, y0, buf, sems):
    for c in halo_copies(na, planes, y0, buf, 0, sems) + halo_copies(nb, planes, y0, buf, len(planes), sems):
        c.wait()


def edge_kernel(y0, at0, at1, u0, kp, na, nb, *refs):
    rem0, rem1, loc0, loc1, buf, hu, sems = refs[-7:]
    node = lax.axis_index("node")
    pos = lax.axis_index("space")
    remote, local = weights_for(node)
    planes = (0, 1, 2)
    begin_halos(na, nb, planes, y0, buf, sems)
    end_halos(na, nb, planes, y0, buf, sems)

    def convert(i, carry):
        for r in range(Q):
            hu[i, r] = rows_of(buf, i, r)
        return carry

    lax.fori_loop(0, 6, convert, 0)

    @pl.when(pos == 0)
    def _():
        hu[0] = kp[0]

    @pl.when(pos == 3)
    def _():
        hu[3] = kp[PLANES - 1]

    for e in range(2):
        p = 7 * e

        def emit(r, f, e=e):
            rem0[at0[e], r] = remote[0][0] * f[0] + remote[0][1] * f[1]
            rem1[at1[e], r] = remote[1][0] * f[0] + remote[1][1] * f[1]
            loc0[e, r] = local[0][0] * f[0] + local[0][1] * f[1]
            loc1[e, r] = local[1][0] * f[0] + local[1][1] * f[1]

        at = lambda j, d, p=p: (lambda r: u0[j * PLANES + p + d, r])
        kat = lambda d, p=p: (lambda r: kp[p + d, r])
        halo = lambda i, e=e: (lambda r: hu[3 * e + i, r])
        flux_rows(
            kat(0),
            kat(-1) if e else halo(0),
            halo(0) if e else kat(1),
            [at(0, 0), at(1, 0)],
            [at(0, -1), at(1, -1)] if e else [halo(1), halo(2)],
            [halo(1), halo(2)] if e else [at(0, 1), at(1, 1)],
            y0,
            emit,
        )


def coef_kernel(y0, kp, na, nb, fa, fb, fx, fy, fz, a0, a1, buf, far, kx, sems, far_sems):
    node = lax.axis_index("node")
    pos = lax.axis_index("space")
    begin_halos(na, nb, (0,), y0, buf, sems)
    begin_halos(fa, fb, (0,), y0, far, far_sems)

    def keep(p, carry):
        kx[p + 2] = kp[p]
        return carry

    lax.fori_loop(0, PLANES, keep, 0)
    end_halos(na, nb, (0,), y0, buf, sems)
    end_halos(fa, fb, (0,), y0, far, far_sems)

    @pl.when(pos > 0)
    def _():
        for r in range(Q):
            kx[0, r] = rows_of(far, 0, r)
            kx[1, r] = rows_of(buf, 0, r)

    @pl.when(pos == 0)
    def _():
        kx[0] = kp[0]
        kx[1] = kp[0]

    @pl.when(pos < 3)
    def _():
        for r in range(Q):
            kx[10, r] = rows_of(buf, 1, r)
            kx[11, r] = rows_of(far, 1, r)

    @pl.when(pos == 3)
    def _():
        kx[10] = kp[7]
        kx[11] = kp[7]

    inv0, inv1 = inv_scale(0, node), inv_scale(1, node)

    def coef(i, carry):
        rim = jnp.logical_or(jnp.logical_and(i == 1, pos == 0), jnp.logical_and(i == 9, pos == 3))
        open_face = jnp.where(rim, jnp.float32(0.0), jnp.float32(0.5))
        rows = Rows(lambda r: kx[i + 1, r], y0)
        for r in range(Q):
            kc, below, face, zface, total = rows.step(r)
            low = kc + kx[i, r]
            total = total + 0.5 * (low + (kc + kx[i + 2, r]))
            fx[i, r] = open_face * low
            fy[i, r] = face
            fz[i, r] = zface
            a0[i, r] = 1.0 / (inv0 + total)
            a1[i, r] = 1.0 / (inv1 + total)
        return carry

    lax.fori_loop(0, PLANES + 2, coef, 0)
    for r in range(Q):
        fx[10, r] = 0.5 * (kx[10, r] + kx[11, r])


def start_copies(src, planes, y0, buf, sems):
    out = []
    for i, p in enumerate(planes):
        out += lane_copies(src.at[p, pl.ds(y0, ROWS), :], lambda lane, i=i: buf.at[lane, i], sems.at[i])
    return out


def begin_start(prev, init, planes, y0, buf, sems):
    first = lax.axis_index("tm") == 0

    @pl.when(first)
    def _():
        for c in start_copies(init, planes, y0, buf, sems):
            c.start()

    @pl.when(jnp.logical_not(first))
    def _():
        for c in start_copies(prev, planes, y0, buf, sems):
            c.start()


def rim_kernel(where, at, *refs):
    n = len(where)
    zs, locs = refs[:n], refs[n : 2 * n]
    prev, init, rim, sa, sb, buf, sems = refs[2 * n :]
    even = lax.rem(lax.axis_index("space"), 2) == 0
    for i, y0 in enumerate(where):
        begin_start(prev, init, (0, 7), y0, buf.at[i], sems.at[i])
    for i, y0 in enumerate(where):
        for c in start_copies(prev, (0, 7), y0, buf.at[i], sems.at[i]):
            c.wait()
        for e in range(2):
            for r in range(Q):
                rim[2 * i + e, r] = rows_of(buf.at[i], e, r) + (locs[i][e, r] + zs[i][at[i][e], r])
    top = jnp.where(even, 1, 0)
    for i in range(n):
        for r in range(Q):
            sa[i, r] = rim[2 * i + top, r]
            sb[i, r] = rim[2 * i + 1 - top, r]


def sweep(src, rhs, a, fx, fy, fz, shift, count, store):
    G = 2

    def pair(t, carry):
        b = t * G
        uc = [src[b + g + 1, 0] for g in range(G)]
        last = [src[b + g + 1, Q - 1] for g in range(G)]
        flow = [sdown(fy[b + g + shift, Q - 1] * last[g]) for g in range(G)]
        for r in range(Q):
            low = src[b, r]
            high = src[b + G + 1, r]
            faces = [fx[b + g + shift, r] for g in range(G + 1)]
            column = [low] + uc + [high]
            nxt = []
            for g in range(G):
                un = src[b + g + 1, r + 1] if r < Q - 1 else sup(src[b + g + 1, 0])
                d = b + g + shift
                face = fy[d, r]
                zface = fz[d, r]
                n = faces[g] * column[g] + faces[g + 1] * column[g + 2]
                n = n + (flow[g] + face * un)
                n = n + (zface * znext(uc[g]) + zprev(zface * uc[g]))
                flow[g] = face * uc[g]
                store(b + g, r, rhs[d, r] + a[d, r] * n)
                nxt.append(un)
            uc = nxt
        return carry

    lax.fori_loop(0, count // G, pair, 0)


def two_sweeps(ub, mid, rhs, a, fx, fy, fz, store):
    def keep(d, r, value):
        mid[d, r] = value

    sweep(ub, rhs, a, fx, fy, fz, 0, PLANES + 2, keep)
    sweep(mid, rhs, a, fx, fy, fz, 1, PLANES, store)


def send_faces(u, sa, sb):
    even = lax.rem(lax.axis_index("space"), 2) == 0
    top = jnp.where(even, PLANES - 2, 0)

    def one(i, carry):
        sa[i] = u[top + i]
        sb[i] = u[PLANES - 2 - top + i]
        return carry

    lax.fori_loop(0, 2, one, 0)


def place_halo(ub, ha, hb):
    even = lax.rem(lax.axis_index("space"), 2) == 0

    def fill(low, high):
        for i in range(2):
            ub[i] = low[i]
            ub[10 + i] = high[i]

    @pl.when(even)
    def _():
        fill(hb, ha)

    @pl.when(jnp.logical_not(even))
    def _():
        fill(ha, hb)


def first_kernel(m, y0, slot, offset, z, loc, rim, ra, rb, a, fx, fy, fz, u0, prev, init, na, nb, fa, fb, rhs, u, sa, sb, ub, mid, buf, hbuf, fbuf, sems, hsems, fsems):
    node = lax.axis_index("node")
    even = lax.rem(lax.axis_index("space"), 2) == 0
    planes = tuple(range(1, PLANES - 1))
    begin_start(prev, init, planes, y0, buf, sems)
    begin_halos(na, nb, (1 + m,), y0, hbuf, hsems)
    begin_halos(fa, fb, (1 + m,), y0, fbuf, fsems)
    inv = inv_scale(m, node)

    def scaled(dst, src, at):
        for r in range(Q):
            dst[at, r] = src[r] * (a[at, r] * inv)

    @pl.when(even)
    def _():
        scaled(rhs, rb.at[slot], 0)
        scaled(rhs, ra.at[slot], 9)

    @pl.when(jnp.logical_not(even))
    def _():
        scaled(rhs, ra.at[slot], 0)
        scaled(rhs, rb.at[slot], 9)

    scaled(rhs, rim.at[2 * slot], 1)
    scaled(rhs, rim.at[2 * slot + 1], 8)

    def keep(p, carry):
        ub[p + 2] = u0[m * PLANES + p]
        return carry

    lax.fori_loop(0, PLANES, keep, 0)
    end_halos(na, nb, (1 + m,), y0, hbuf, hsems)
    end_halos(fa, fb, (1 + m,), y0, fbuf, fsems)

    def convert(i, carry):
        for r in range(Q):
            ub[1 + 9 * i, r] = rows_of(hbuf, i, r)
            ub[11 * i, r] = rows_of(fbuf, i, r)
        return carry

    lax.fori_loop(0, 2, convert, 0)
    for c in start_copies(prev, planes, y0, buf, sems):
        c.wait()

    def right(i, carry):
        for r in range(Q):
            rhs[i + 2, r] = (rows_of(buf, i, r) + (loc[i, r] + z[i + offset, r])) * (a[i + 2, r] * inv)
        return carry

    lax.fori_loop(0, PLANES - 2, right, 0)

    def store(d, r, value):
        u[d, r] = value

    two_sweeps(ub, mid, rhs, a, fx, fy, fz, store)
    send_faces(u, sa, sb)


def next_kernel(u, ha, hb, rhs, a, fx, fy, fz, unew, sa, sb, ub, mid):
    place_halo(ub, ha, hb)

    def keep(p, carry):
        ub[p + 2] = u[p]
        return carry

    lax.fori_loop(0, PLANES, keep, 0)

    def store(d, r, value):
        unew[d, r] = value

    two_sweeps(ub, mid, rhs, a, fx, fy, fz, store)
    send_faces(unew, sa, sb)


def last_kernel(m, part, aliased, u, ha, hb, rhs, a, fx, fy, fz, *rest):
    out, ub, mid, obuf, sems = rest[1:] if aliased else rest
    y0, first, kept = PARTS[part]
    place_halo(ub, ha, hb)

    def keep(p, carry):
        ub[p + 2] = u[p]
        return carry

    lax.fori_loop(0, PLANES, keep, 0)

    def store(d, r, value):
        for lane in range(2):
            obuf[lane, d, pl.ds(r, 8, stride=Q), :] = value[:, 128 * lane : 128 * lane + 128]

    two_sweeps(ub, mid, rhs, a, fx, fy, fz, store)
    cs = [
        pltpu.make_async_copy(
            obuf.at[lane, p, pl.ds(first, kept), :],
            out.at[0, m, p, pl.ds(y0 + first, kept), pl.ds(128 * lane, 128)],
            sems.at[lane, p],
        )
        for lane in range(2)
        for p in range(PLANES)
    ]
    for c in cs:
        c.start()
    for c in cs:
        c.wait()


DMA = pltpu.SemaphoreType.DMA
SWAP_A = [(0, 1), (1, 0), (2, 3), (3, 2)]
SWAP_B = [(1, 2), (2, 1)]


def to_a(x):
    return lax.ppermute(x, "space", SWAP_A)


def to_b(x):
    return lax.ppermute(x, "space", SWAP_B)


def swap_nodes(x):
    return lax.ppermute(x, "node", [(0, 1), (1, 0)])


def body(nodes, prev_final, u_init, cond):
    order = Order()
    plane_shape = lambda n: pltpu.VMEM((n, NY, NZ), F32)
    na, nb, fa, fb = order.call(
        "faces",
        faces_kernel,
        [(plane_shape(3), VM)] * 4,
        [(nodes, None), (cond, None)],
        [DMA((12,))],
        4,
        1.0,
    )
    na, nb, fa, fb = to_a(na), to_b(nb), to_a(fa), to_b(fb)
    half = lax.axis_size("tm") // 2
    blocks = 2 * half
    pairs = [
        (n * blocks + t, (1 - n if t == half - 1 else n) * blocks + t + 1)
        for n in range(2)
        for t in range(blocks - 1)
    ]
    prev = lax.ppermute(prev_final[0], ("node", "tm"), pairs)

    inner, edges, coef = [], [], {}
    for part, (y0, first, kept) in enumerate(PARTS):
        inner.append(
            order.call(
                "inner%d" % part,
                functools.partial(inner_kernel, y0, part, 1 - part),
                [(vshape(n), VM) for n in (2 * PLANES, PLANES, 8 if part else 6, 6 if part else 10, 6, 6)],
                [(nodes, None), (cond, None)],
                [pltpu.VMEM((2, 3 * PLANES, ROWS, 128), F32), DMA((PLANES, 3, 2))],
                12,
                5.0,
            )
        )
    def edge_step(part):
        y0 = PARTS[part][0]
        u0, kp = inner[part][:2]
        args = [(u0, True), (kp, True), (na, False), (nb, False)]
        if part:
            args += [(inner[1][2], True), (edges[0][1], True)]
        else:
            args += [(inner[0][3], True)]
        edges.append(
            order.call(
                "edge%d" % part,
                functools.partial(edge_kernel, y0, (0, 7) if part else (0, 1), (8, 9) if part else (0, 7)),
                [(vshape(8 if part else 2), VM), (vshape(10), VM), (vshape(2), VM), (vshape(2), VM)],
                args,
                [pltpu.VMEM((2, 6, ROWS, 128), F32), pltpu.VMEM((6, Q, 8, NZ), F32), DMA((6, 2))],
                8,
                2.5,
                {4: 0, 5: 1} if part else {4: 1},
                [prev, z_start] if part else [],
            )
        )

    def coef_step(part):
        coef[part] = order.call(
            "coef%d" % part,
            functools.partial(coef_kernel, PARTS[part][0]),
            [(vshape(11), VM)] + [(vshape(10), VM)] * 4,
            [(inner[part][1], True)] + [(x, False) for x in (na, nb, fa, fb)],
            [pltpu.VMEM((2, 2, ROWS, 128), F32)] * 2 + [pltpu.VMEM((12, Q, 8, NZ), F32), DMA((2, 2)), DMA((2, 2))],
            8,
            3.5,
        )

    z_start = swap_nodes(inner[0][2])
    edge_step(0)
    edge_step(1)
    coef_step(0)

    units = [(m, part) for m in range(2) for part in range(2)]
    z_inner = [z_start] + [swap_nodes(x) for x in (edges[1][0], edges[1][1], inner[1][3])]
    z_edge = [(swap_nodes(edges[0][0]), (0, 1)), (z_inner[1], (0, 7)), (z_inner[2], (0, 7)), (z_inner[2], (8, 9))]
    state = {}
    out = [None]

    def coefs(unit):
        m, part = units[unit]
        return [(x, True) for x in [coef[part][3 + m]] + coef[part][:3]]

    def rim_step(which):
        n = len(which)
        parts = [units[unit][1] for unit in which]
        rim, ra, rb = order.call(
            "rim%d" % which[0],
            functools.partial(rim_kernel, tuple(PARTS[part][0] for part in parts), tuple(z_edge[unit][1] for unit in which)),
            [(vshape(2 * n), VM), (vshape(n), VM), (vshape(n), VM)],
            [(z_edge[unit][0], True) for unit in which]
            + [(edges[units[unit][1]][2 + units[unit][0]], True) for unit in which]
            + [(prev, False), (u_init, False)],
            [pltpu.VMEM((n, 2, 2, ROWS, 128), F32), DMA((n, 2, 2))],
            4,
            0.5,
        )
        ra, rb = to_a(ra), to_b(rb)
        for slot, unit in enumerate(which):
            state[unit] = (slot, rim, ra, rb)

    def first_step(unit):
        m, part = units[unit]
        slot, rim, ra, rb = state[unit]
        rhs, u, sa, sb = order.call(
            "first%d" % unit,
            functools.partial(first_kernel, m, PARTS[part][0], slot, 1 if unit in (1, 2) else 0),
            [(vshape(10), VM), (vshape(8), VM), (vshape(2), VM), (vshape(2), VM)],
            [(x, True) for x in (z_inner[unit], inner[part][4 + m], rim, ra, rb)]
            + coefs(unit)
            + [(inner[part][0], True)]
            + [(x, False) for x in (prev, u_init, na, nb, fa, fb)],
            [
                pltpu.VMEM((12, Q, 8, NZ), F32),
                pltpu.VMEM((10, Q, 8, NZ), F32),
                pltpu.VMEM((2, 6, ROWS, 128), F32),
                pltpu.VMEM((2, 2, ROWS, 128), F32),
                pltpu.VMEM((2, 2, ROWS, 128), F32),
                DMA((6, 2)),
                DMA((2, 2)),
                DMA((2, 2)),
            ],
            12,
            3.0,
        )
        state[unit] = (rhs, u, to_a(sa), to_b(sb))

    def next_step(unit, index):
        rhs, u, ha, hb = state[unit]
        u, sa, sb = order.call(
            "next%d_%d" % (unit, index),
            next_kernel,
            [(vshape(8), VM), (vshape(2), VM), (vshape(2), VM)],
            [(x, True) for x in (u, ha, hb, rhs)] + coefs(unit),
            [pltpu.VMEM((12, Q, 8, NZ), F32), pltpu.VMEM((10, Q, 8, NZ), F32)],
            8,
            2.5,
        )
        state[unit] = (rhs, u, to_a(sa), to_b(sb))

    def last_step(unit):
        m, part = units[unit]
        rhs, u, ha, hb = state[unit]
        args = [(x, True) for x in (u, ha, hb, rhs)] + coefs(unit)
        aliased = out[0] is not None
        if aliased:
            args.append((out[0], False))
        (out[0],) = order.call(
            "last%d" % unit,
            functools.partial(last_kernel, m, part, aliased),
            [((1, 2, PLANES, NY, NZ), ANY)],
            args,
            [
                pltpu.VMEM((12, Q, 8, NZ), F32),
                pltpu.VMEM((10, Q, 8, NZ), F32),
                pltpu.VMEM((2, 8, ROWS, 128), F32),
                DMA((2, 8)),
            ],
            8,
            3.5,
            {8: 0} if aliased else None,
        )

    C, R, S, N, M, L = range(6)
    plan = (
        (R, 0), (C, 1), (S, 0), (N, 0), (R, 1), (M, 0), (S, 1), (L, 0), (N, 1), (R, 2),
        (M, 1), (S, 2), (L, 1), (S, 3), (N, 2), (N, 3), (M, 2), (M, 3), (L, 2), (L, 3),
    )
    for kind, unit in plan:
        if kind == C:
            coef_step(unit)
        elif kind == R:
            rim_step((2, 3) if unit == 2 else (unit,))
        elif kind == S:
            first_step(unit)
        elif kind == L:
            last_step(unit)
        else:
            next_step(unit, kind)
    return out[0]


def solution(mesh):
    in_specs = (
        P("tm", "node", "space", None, None),
        P("tm", "space", None, None),
        P("space", None, None),
        P("space", None, None),
    )
    out_specs = P("tm", "node", "space", None, None)
    return jax.shard_map(body, mesh=mesh, in_specs=in_specs, out_specs=out_specs, check_vma=False)
```

time: 603 us -> 172 us (0.29)
  waiting for transfers between devices: 290 us -> 25.7 us
  other arithmetic: 170 us -> 0 us
  Pallas kernels: 0 us -> 71.4 us
  matrix products: 42.8 us -> 0 us
  local copies, waits for them, and re-layouts: 27.7 us -> 0.01 us
  starting transfers between devices: 56.3 us -> 72.5 us
  between operations: 13.8 us -> 0.77 us
    psum x1 -> x0, waiting for transfers between devices: 191 us -> none  [body(): summed = lax.psum(partial_value, 'node')]
    div x7 -> x0, other arithmetic: 144 us -> none  [body(): (right_side + node_diag * neighbours(padded, faces_inner)) / divisor]
    ppermute x19 -> x40, waiting for transfers between devices: 99.1 us -> 25.7 us  [the longest x17 9.71 us: to_a(): return lax.ppermute(x, 'space', SWAP_A)]
    pallas_call x0 -> x26, Pallas kernels: none -> 71.4 us  [call(): pl.pallas_call(run, out_shape=[o if s is VM else jax.ShapeDtypeStruct(o,...]
    dot_general x1 -> x0, matrix products: 42.8 us -> none  [body(): jnp.einsum('mj,jxyz->mxyz', own_weights, fluxes, precision=lax.Precision....]
    broadcast_in_dim x1 -> x0, other arithmetic: 20.3 us -> none  [body(): return iterate[None]]
    ppermute x19 -> x40, starting transfers between devices: 56.3 us -> 72.5 us  [the longest x17 52.2 us: to_b(): return lax.ppermute(x, 'space', SWAP_B)]
    slice x11 -> x0, local copies, waits for them, and re-layouts: 12.8 us -> none  [the longest x8 12.3 us: extended(): lax.slice_in_dim(cells, cells.shape[dim] - width, cells.shape[dim], axis=...]
  transfers between devices with their start and end apart: 20 -> 40, of which waited for: 18 -> 14; matrix products, arithmetic and copies ran while one was open for 2% -> 0% of each run, Pallas kernels for 0% -> 40%
where the time goes in v1:
time: 172 us; the launch traced here: 170 us
  starting transfers between devices  72.5 us (42%)
  Pallas kernels  71.4 us (42%)
  waiting for transfers between devices  25.7 us (15%)
    pallas_call x26, Pallas kernels, call(): pl.pallas_call(run, out_shape=[o if s is VM else jax.ShapeDtypeStruct(o,...  71.4 us
    ppermute x17, starting transfers between devices, to_b(): return lax.ppermute(x, 'space', SWAP_B)  52.2 us
    ppermute x5, starting transfers between devices, swap_nodes(): return lax.ppermute(x, 'node', [(0, 1), (1, 0)])  16.1 us
    ppermute x17, waiting for transfers between devices, to_a(): return lax.ppermute(x, 'space', SWAP_A)  9.71 us
    ppermute x17, waiting for transfers between devices, to_b(): return lax.ppermute(x, 'space', SWAP_B)  9.51 us
    ppermute x5, waiting for transfers between devices, swap_nodes(): return lax.ppermute(x, 'node', [(0, 1), (1, 0)])  6.48 us
  transfers between devices with their start and end apart: 40, of which 14 were waited for; matrix products, arithmetic and copies ran while one was open for 0% of the time, Pallas kernels for 40%

profile of v1, /device:TPU:14, one launch (start us, length us, event | category | flops | bytes accessed | tf_op | source)
XLA Modules:
  0.0 170.4 jit_solution(11270321787204011766)
XLA Ops:
  4.4 4.3 %collective-permute-start.1 = (f32[3,256,256]{2,1,0:T(8,128)S(1)}, f32[3,256,256]{2,1,0:T(8,128)S(1)}, u32[]{:S(2)}, u32[]{:S(2)}) collective-permute-start(f32[3,256,256]{2,1,0:T(8,128)S(1)} %get-tuple-element.123), channel_id=1, source_target_pairs={{1,2},{2,1},{5,6},{6,5},{9,10},{10,9},{13,14},{14,13},{17,18},{18,... | collective-permute-start | bytes 2359304 | tf_op jit(solution)/shard_map/ppermute | solution.py:648
  8.7 7.2 %inner0.1 = (f32[16,17,8,256]{3,2,1,0:T(8,128)S(1)}, f32[8,17,8,256]{3,2,1,0:T(8,128)S(1)}, f32[6,17,8,256]{3,2,1,0:T(8,128)S(1)}, f32[10,17,8,256]{3,2,1,0:T(8,...) custom-call(f32[8,128]{1,0:T(8,128)S(1)} %get-tuple-element.117.before, ...), custom_call_target="tpu_custom_call" | custom-call | flops 5000000000 | tf_op jit(solution)/shard_map/inner0/pallas_call | solution.py:87
  17.9 3.3 %collective-permute-done.refs_2_.refs_1_.refs_12_ = f32[3,256,256]{2,1,0:T(8,128)S(1)} collective-permute-done((f32[3,256,256]{2,1,0:T(8,128)S(1)}, f32[3,256,256]{2,1,0:T(8,128)S(1)}, u32[]{:S(2)}, u32[]{:S(2)}) %collective-permute-start) | collective-permute-done | bytes 786464 | tf_op jit(solution)/shard_map/ppermute | solution.py:644
  21.2 3.5 %collective-permute-start.5 = (f32[3,256,256]{2,1,0:T(8,128)S(1)}, f32[3,256,256]{2,1,0:T(8,128)S(1)}, u32[]{:S(2)}, u32[]{:S(2)}) collective-permute-start(f32[3,256,256]{2,1,0:T(8,128)S(1)} %get-tuple-element.133), channel_id=1, source_target_pairs={{1,2},{2,1},{5,6},{6,5},{9,10},{10,9},{13,14},{14,13},{17,18},{18,... | collective-permute-start | bytes 2359304 | tf_op jit(solution)/shard_map/ppermute | solution.py:648
  24.7 7.2 %inner1.1 = (f32[16,17,8,256]{3,2,1,0:T(8,128)S(1)}, f32[8,17,8,256]{3,2,1,0:T(8,128)S(1)}, f32[8,17,8,256]{3,2,1,0:T(8,128)S(1)}, f32[6,17,8,256]{3,2,1,0:T(8,1...) custom-call(f32[8,128]{1,0:T(8,128)S(1)} %get-tuple-element.118.before, ...), custom_call_target="tpu_custom_call" | custom-call | flops 5000000000 | tf_op jit(solution)/shard_map/inner1/pallas_call | solution.py:87
  34.4 4.2 %collective-permute-start.6 = (f32[2,17,8,256]{3,2,1,0:T(8,128)S(1)}, f32[2,17,8,256]{3,2,1,0:T(8,128)S(1)}, u32[]{:S(2)}, u32[]{:S(2)}) collective-permute-start(f32[2,17,8,256]{3,2,1,0:T(8,128)S(1)} %get-tuple-element.135), channel_id=1, source_target_pairs={{0,64},{64,0},{1,65},{65,1},{2,66},{66,2},{3,67},{67,3},{4,68},{68... | collective-permute-start | bytes 835592 | tf_op jit(solution)/shard_map/ppermute | solution.py:652
  44.5 2.6 %collective-permute-start.8 = (f32[1,17,8,256]{3,2,1,0:T(8,128)S(1)}, f32[1,17,8,256]{3,2,1,0:T(8,128)S(1)}, u32[]{:S(2)}, u32[]{:S(2)}) collective-permute-start(f32[1,17,8,256]{3,2,1,0:T(8,128)S(1)} %get-tuple-element.142), channel_id=1, source_target_pairs={{1,2},{2,1},{5,6},{6,5},{9,10},{10,9},{13,14},{14,13},{17,18},{18,... | collective-permute-start | bytes 417800 | tf_op jit(solution)/shard_map/ppermute | solution.py:648
  51.5 3.0 %first0.1 = (f32[10,17,8,256]{3,2,1,0:T(8,128)S(1)}, f32[8,17,8,256]{3,2,1,0:T(8,128)S(1)}, f32[2,17,8,256]{3,2,1,0:T(8,128)S(1)}, f32[2,17,8,256]{3,2,1,0:T(8,128)S(1)}, f32[8,128]{1,0:T(8,128)S(1)}) custom-call(f32[8,128]{1,0:T(8,128)S(1)} %get-tuple-element.138.before, f32[6,17,8,256]{3,2,1,0:T(8,128)S(1)} %collective-permute-done.3.refs_7_.refs_0_, ...), custom_call_target="tpu_custom_call" | custom-call | flops 3000000000 | tf_op jit(solution)/shard_map/first0/pallas_call | solution.py:87
  54.6 2.6 %collective-permute-start.10 = (f32[2,17,8,256]{3,2,1,0:T(8,128)S(1)}, f32[2,17,8,256]{3,2,1,0:T(8,128)S(1)}, u32[]{:S(2)}, u32[]{:S(2)}) collective-permute-start(f32[2,17,8,256]{3,2,1,0:T(8,128)S(1)} %get-tuple-element.150), channel_id=1, source_target_pairs={{1,2},{2,1},{5,6},{6,5},{9,10},{10,9},{13,14},{14,13},{17,18},{18,... | collective-permute-start | bytes 835592 | tf_op jit(solution)/shard_map/ppermute | solution.py:648
  57.1 5.3 %collective-permute-done.9.refs_1_ = f32[2,17,8,256]{3,2,1,0:T(8,128)S(1)} collective-permute-done((f32[2,17,8,256]{3,2,1,0:T(8,128)S(1)}, f32[2,17,8,256]{3,2,1,0:T(8,128)S(1)}, u32[]{:S(2)}, u32[]{:S(2)}) %collective-permute-start.9) | collective-permute-done | bytes 278560 | tf_op jit(solution)/shard_map/ppermute | solution.py:644
  66.7 2.6 %collective-permute-start.13 = (f32[2,17,8,256]{3,2,1,0:T(8,128)S(1)}, f32[2,17,8,256]{3,2,1,0:T(8,128)S(1)}, u32[]{:S(2)}, u32[]{:S(2)}) collective-permute-start(f32[2,17,8,256]{3,2,1,0:T(8,128)S(1)} %get-tuple-element.158), channel_id=1, source_target_pairs={{1,2},{2,1},{5,6},{6,5},{9,10},{10,9},{13,14},{14,13},{17,18},{18,... | collective-permute-start | bytes 835592 | tf_op jit(solution)/shard_map/ppermute | solution.py:648
  69.3 7.9 %collective-permute-start.20 = (f32[10,17,8,256]{3,2,1,0:T(8,128)S(1)}, f32[10,17,8,256]{3,2,1,0:T(8,128)S(1)}, u32[]{:S(2)}, u32[]{:S(2)}) collective-permute-start(f32[10,17,8,256]{3,2,1,0:T(8,128)S(1)} %get-tuple-element.178), channel_id=1, source_target_pairs={{0,64},{64,0},{1,65},{65,1},{2,66},{66,2},{3,67},{67,3},{4,68},{68... | collective-permute-start | bytes 4177928 | tf_op jit(solution)/shard_map/ppermute | solution.py:652
  77.4 2.7 %collective-permute-start.15 = (f32[1,17,8,256]{3,2,1,0:T(8,128)S(1)}, f32[1,17,8,256]{3,2,1,0:T(8,128)S(1)}, u32[]{:S(2)}, u32[]{:S(2)}) collective-permute-start(f32[1,17,8,256]{3,2,1,0:T(8,128)S(1)} %get-tuple-element.163), channel_id=1, source_target_pairs={{1,2},{2,1},{5,6},{6,5},{9,10},{10,9},{13,14},{14,13},{17,18},{18,... | collective-permute-start | bytes 417800 | tf_op jit(solution)/shard_map/ppermute | solution.py:648
  82.5 3.2 %collective-permute-start.17 = (f32[2,17,8,256]{3,2,1,0:T(8,128)S(1)}, f32[2,17,8,256]{3,2,1,0:T(8,128)S(1)}, u32[]{:S(2)}, u32[]{:S(2)}) collective-permute-start(f32[2,17,8,256]{3,2,1,0:T(8,128)S(1)} %get-tuple-element.171), channel_id=1, source_target_pairs={{1,2},{2,1},{5,6},{6,5},{9,10},{10,9},{13,14},{14,13},{17,18},{18,... | collective-permute-start | bytes 835592 | tf_op jit(solution)/shard_map/ppermute | solution.py:648
  85.8 3.1 %first1.1 = (f32[10,17,8,256]{3,2,1,0:T(8,128)S(1)}, f32[8,17,8,256]{3,2,1,0:T(8,128)S(1)}, f32[2,17,8,256]{3,2,1,0:T(8,128)S(1)}, f32[2,17,8,256]{3,2,1,0:T(8,128)S(1)}, f32[8,128]{1,0:T(8,128)S(1)}) custom-call(f32[8,128]{1,0:T(8,128)S(1)} %get-tuple-element.159.before, f32[8,17,8,256]{3,2,1,0:T(8,128)S(1)} %collective-permute-done.11.refs_0_, ...), custom_call_target="tpu_custom_call" | custom-call | flops 3000000000 | tf_op jit(solution)/shard_map/first1/pallas_call | solution.py:87
  89.1 2.7 %collective-permute-start.19 = (f32[2,17,8,256]{3,2,1,0:T(8,128)S(1)}, f32[2,17,8,256]{3,2,1,0:T(8,128)S(1)}, u32[]{:S(2)}, u32[]{:S(2)}) collective-permute-start(f32[2,17,8,256]{3,2,1,0:T(8,128)S(1)} %get-tuple-element.175), channel_id=1, source_target_pairs={{1,2},{2,1},{5,6},{6,5},{9,10},{10,9},{13,14},{14,13},{17,18},{18,... | collective-permute-start | bytes 835592 | tf_op jit(solution)/shard_map/ppermute | solution.py:648
  91.8 3.4 %last0.1 = (f32[1,2,8,256,256]{4,3,2,1,0:T(8,128)}, f32[8,128]{1,0:T(8,128)S(1)}) custom-call(f32[8,128]{1,0:T(8,128)S(1)} %get-tuple-element.168.before, f32[8,17,8,256]{3,2,1,0:T(8,128)S(1)} %get-tuple-element.169.refs_0_, f32[2,17,8,256]{3,2,1,0:T(8,128)S(1)} %collective-permute-done.16.refs_1_, f32[2,17,8,256]{3,2,1,0:T(8,128)S(1)} %collective-permute-done.17.refs_2_, ...), custom_call_target="tpu_custom_call" | custom-call | flops 3500000000 | tf_op jit(solution)/shard_map/last0/pallas_call | solution.py:87
  100.5 2.8 %collective-permute-start.22 = (f32[2,17,8,256]{3,2,1,0:T(8,128)S(1)}, f32[2,17,8,256]{3,2,1,0:T(8,128)S(1)}, u32[]{:S(2)}, u32[]{:S(2)}) collective-permute-start(f32[2,17,8,256]{3,2,1,0:T(8,128)S(1)} %get-tuple-element.184), channel_id=1, source_target_pairs={{1,2},{2,1},{5,6},{6,5},{9,10},{10,9},{13,14},{14,13},{17,18},{18,... | collective-permute-start | bytes 835592 | tf_op jit(solution)/shard_map/ppermute | solution.py:648
  103.3 3.8 %collective-permute-done.20.refs_0_.refs_1_ = f32[10,17,8,256]{3,2,1,0:T(8,128)S(1)} collective-permute-done((f32[10,17,8,256]{3,2,1,0:T(8,128)S(1)}, f32[10,17,8,256]{3,2,1,0:T(8,128)S(1)}, u32[]{:S(2)}, u32[]{:S(2)}) %collective-permute-start.20) | collective-permute-done | bytes 1392672 | tf_op jit(solution)/shard_map/ppermute | solution.py:652
  107.5 2.7 %collective-permute-start.24 = (f32[2,17,8,256]{3,2,1,0:T(8,128)S(1)}, f32[2,17,8,256]{3,2,1,0:T(8,128)S(1)}, u32[]{:S(2)}, u32[]{:S(2)}) collective-permute-start(f32[2,17,8,256]{3,2,1,0:T(8,128)S(1)} %get-tuple-element.189), channel_id=1, source_target_pairs={{1,2},{2,1},{5,6},{6,5},{9,10},{10,9},{13,14},{14,13},{17,18},{18,... | collective-permute-start | bytes 835592 | tf_op jit(solution)/shard_map/ppermute | solution.py:648
  114.5 3.2 %collective-permute-start.26 = (f32[2,17,8,256]{3,2,1,0:T(8,128)S(1)}, f32[2,17,8,256]{3,2,1,0:T(8,128)S(1)}, u32[]{:S(2)}, u32[]{:S(2)}) collective-permute-start(f32[2,17,8,256]{3,2,1,0:T(8,128)S(1)} %get-tuple-element.194), channel_id=1, source_target_pairs={{1,2},{2,1},{5,6},{6,5},{9,10},{10,9},{13,14},{14,13},{17,18},{18,... | collective-permute-start | bytes 835592 | tf_op jit(solution)/shard_map/ppermute | solution.py:648
  117.7 2.9 %first2.1 = (f32[10,17,8,256]{3,2,1,0:T(8,128)S(1)}, f32[8,17,8,256]{3,2,1,0:T(8,128)S(1)}, f32[2,17,8,256]{3,2,1,0:T(8,128)S(1)}, f32[2,17,8,256]{3,2,1,0:T(8,128)S(1)}, f32[8,128]{1,0:T(8,128)S(1)}) custom-call(f32[8,128]{1,0:T(8,128)S(1)} %get-tuple-element.185.before, f32[10,17,8,256]{3,2,1,0:T(8,128)S(1)} %collective-permute-done.20.refs_0_.refs_1_, ...), custom_call_target="tpu_custom_call" | custom-call | flops 3000000000 | tf_op jit(solution)/shard_map/first2/pallas_call | solution.py:87
  120.7 2.7 %collective-permute-start.29 = (f32[2,17,8,256]{3,2,1,0:T(8,128)S(1)}, f32[2,17,8,256]{3,2,1,0:T(8,128)S(1)}, u32[]{:S(2)}, u32[]{:S(2)}) collective-permute-start(f32[2,17,8,256]{3,2,1,0:T(8,128)S(1)} %get-tuple-element.203), channel_id=1, source_target_pairs={{1,2},{2,1},{5,6},{6,5},{9,10},{10,9},{13,14},{14,13},{17,18},{18,... | collective-permute-start | bytes 835592 | tf_op jit(solution)/shard_map/ppermute | solution.py:648
  123.4 3.4 %last1.1 = (f32[1,2,8,256,256]{4,3,2,1,0:T(8,128)}, f32[8,128]{1,0:T(8,128)S(1)}) custom-call(f32[8,128]{1,0:T(8,128)S(1)} %get-tuple-element.191.before, f32[8,17,8,256]{3,2,1,0:T(8,128)S(1)} %get-tuple-element.192.refs_0_, f32[2,17,8,256]{3,2,1,0:T(8,128)S(1)} %collective-permute-done.25.refs_1_, ...), custom_call_target="tpu_custom_call", output_to_operand_aliasing={{0}: (9, {})} | custom-call | flops 3500000000 | tf_op jit(solution)/shard_map/last1/pallas_call | solution.py:87
  128.8 3.0 %first3.1 = (f32[10,17,8,256]{3,2,1,0:T(8,128)S(1)}, f32[8,17,8,256]{3,2,1,0:T(8,128)S(1)}, f32[2,17,8,256]{3,2,1,0:T(8,128)S(1)}, f32[2,17,8,256]{3,2,1,0:T(8,128)S(1)}, f32[8,128]{1,0:T(8,128)S(1)}) custom-call(f32[8,128]{1,0:T(8,128)S(1)} %get-tuple-element.196.before, f32[6,17,8,256]{3,2,1,0:T(8,128)S(1)} %collective-permute-done.27.refs_0_, ...), custom_call_target="tpu_custom_call" | custom-call | flops 3000000000 | tf_op jit(solution)/shard_map/first3/pallas_call | solution.py:87
  132.2 3.2 %collective-permute-start.31 = (f32[2,17,8,256]{3,2,1,0:T(8,128)S(1)}, f32[2,17,8,256]{3,2,1,0:T(8,128)S(1)}, u32[]{:S(2)}, u32[]{:S(2)}) collective-permute-start(f32[2,17,8,256]{3,2,1,0:T(8,128)S(1)} %get-tuple-element.208), channel_id=1, source_target_pairs={{1,2},{2,1},{5,6},{6,5},{9,10},{10,9},{13,14},{14,13},{17,18},{18,... | collective-permute-start | bytes 835592 | tf_op jit(solution)/shard_map/ppermute | solution.py:648
  137.8 2.7 %collective-permute-start.33 = (f32[2,17,8,256]{3,2,1,0:T(8,128)S(1)}, f32[2,17,8,256]{3,2,1,0:T(8,128)S(1)}, u32[]{:S(2)}, u32[]{:S(2)}) collective-permute-start(f32[2,17,8,256]{3,2,1,0:T(8,128)S(1)} %get-tuple-element.213), channel_id=1, source_target_pairs={{1,2},{2,1},{5,6},{6,5},{9,10},{10,9},{13,14},{14,13},{17,18},{18,... | collective-permute-start | bytes 835592 | tf_op jit(solution)/shard_map/ppermute | solution.py:648
  144.2 4.1 %collective-permute-start.35 = (f32[2,17,8,256]{3,2,1,0:T(8,128)S(1)}, f32[2,17,8,256]{3,2,1,0:T(8,128)S(1)}, u32[]{:S(2)}, u32[]{:S(2)}) collective-permute-start(f32[2,17,8,256]{3,2,1,0:T(8,128)S(1)} %get-tuple-element.217), channel_id=1, source_target_pairs={{1,2},{2,1},{5,6},{6,5},{9,10},{10,9},{13,14},{14,13},{17,18},{18,... | collective-permute-start | bytes 835592 | tf_op jit(solution)/shard_map/ppermute | solution.py:648
  151.5 2.8 %collective-permute-start.37 = (f32[2,17,8,256]{3,2,1,0:T(8,128)S(1)}, f32[2,17,8,256]{3,2,1,0:T(8,128)S(1)}, u32[]{:S(2)}, u32[]{:S(2)}) collective-permute-start(f32[2,17,8,256]{3,2,1,0:T(8,128)S(1)} %get-tuple-element.221), channel_id=1, source_target_pairs={{1,2},{2,1},{5,6},{6,5},{9,10},{10,9},{13,14},{14,13},{17,18},{18,... | collective-permute-start | bytes 835592 | tf_op jit(solution)/shard_map/ppermute | solution.py:648
  157.1 4.2 %collective-permute-start.39 = (f32[2,17,8,256]{3,2,1,0:T(8,128)S(1)}, f32[2,17,8,256]{3,2,1,0:T(8,128)S(1)}, u32[]{:S(2)}, u32[]{:S(2)}) collective-permute-start(f32[2,17,8,256]{3,2,1,0:T(8,128)S(1)} %get-tuple-element.226), channel_id=1, source_target_pairs={{1,2},{2,1},{5,6},{6,5},{9,10},{10,9},{13,14},{14,13},{17,18},{18,... | collective-permute-start | bytes 835592 | tf_op jit(solution)/shard_map/ppermute | solution.py:648
  162.8 3.3 %last2.1 = (f32[1,2,8,256,256]{4,3,2,1,0:T(8,128)}, f32[8,128]{1,0:T(8,128)S(1)}) custom-call(f32[8,128]{1,0:T(8,128)S(1)} %get-tuple-element.218.before, f32[8,17,8,256]{3,2,1,0:T(8,128)S(1)} %get-tuple-element.219.refs_0_, f32[2,17,8,256]{3,2,1,0:T(8,128)S(1)} %collective-permute-done.36.refs_1_, ...), custom_call_target="tpu_custom_call", output_to_operand_aliasing={{0}: (9, {})} | custom-call | flops 3500000000 | tf_op jit(solution)/shard_map/last2/pallas_call | solution.py:87
  166.2 4.0 %last3.1 = (f32[1,2,8,256,256]{4,3,2,1,0:T(8,128)}, f32[8,128]{1,0:T(8,128)}) custom-call(f32[8,128]{1,0:T(8,128)S(1)} %get-tuple-element.223.before, f32[8,17,8,256]{3,2,1,0:T(8,128)S(1)} %get-tuple-element.224.refs_0_, f32[2,17,8,256]{3,2,1,0:T(8,128)S(1)} %collective-permute-done.38.refs_1_, ...), custom_call_target="tpu_custom_call", output_to_operand_aliasing={{0}: (9, {})} | custom-call | flops 3500000000 | tf_op jit(solution)/shard_map/last3/pallas_call | solution.py:87
  (77 shorter events, 52.3 us)
Async XLA Ops:
  0.0 38.6 %collective-permute-start.2 = (f32[8,256,256]{2,1,0:T(8,128)}, f32[8,256,256]{2,1,0:T(8,128)S(1)}, u32[]{:S(2)}, u32[]{:S(2)}) collective-permute-start(f32[8,256,256]{2,1,0:T(8,128)} %bitcast.1), channel_id=1, source_target_pairs={{0,4},{4,8},{8,12},{12,16},{16,20},{20,24},{24,28},{28,96},{32,36}... | collective-permute-start | bytes 6291464 | tf_op jit(solution)/shard_map/ppermute | solution.py:675
  3.9 17.3 %collective-permute-start = (f32[3,256,256]{2,1,0:T(8,128)S(1)}, f32[3,256,256]{2,1,0:T(8,128)S(1)}, u32[]{:S(2)}, u32[]{:S(2)}) collective-permute-start(f32[3,256,256]{2,1,0:T(8,128)S(1)} %get-tuple-element.122), channel_id=1, source_target_pairs={{0,1},{1,0},{2,3},{3,2},{4,5},{5,4},{6,7},{7,6},{8,9},{9,8},{10,11... | collective-permute-start | bytes 2359304 | tf_op jit(solution)/shard_map/ppermute | solution.py:644
  4.4 27.5 %collective-permute-start.1 = (f32[3,256,256]{2,1,0:T(8,128)S(1)}, f32[3,256,256]{2,1,0:T(8,128)S(1)}, u32[]{:S(2)}, u32[]{:S(2)}) collective-permute-start(f32[3,256,256]{2,1,0:T(8,128)S(1)} %get-tuple-element.123), channel_id=1, source_target_pairs={{1,2},{2,1},{5,6},{6,5},{9,10},{10,9},{13,14},{14,13},{17,18},{18,... | collective-permute-start | bytes 2359304 | tf_op jit(solution)/shard_map/ppermute | solution.py:648
  15.9 22.7 %collective-permute-start.3 = (f32[6,17,8,256]{3,2,1,0:T(8,128)S(1)}, f32[6,17,8,256]{3,2,1,0:T(8,128)S(1)}, u32[]{:S(2)}, u32[]{:S(2)}) collective-permute-start(f32[6,17,8,256]{3,2,1,0:T(8,128)S(1)} %get-tuple-element.130), channel_id=1, source_target_pairs={{0,64},{64,0},{1,65},{65,1},{2,66},{66,2},{3,67},{67,3},{4,68},{68... | collective-permute-start | bytes 2506760 | tf_op jit(solution)/shard_map/ppermute | solution.py:652
  17.9 23.3 %collective-permute-start.4 = (f32[3,256,256]{2,1,0:T(8,128)S(1)}, f32[3,256,256]{2,1,0:T(8,128)S(1)}, u32[]{:S(2)}, u32[]{:S(2)}) collective-permute-start(f32[3,256,256]{2,1,0:T(8,128)S(1)} %get-tuple-element.132), channel_id=1, source_target_pairs={{0,1},{1,0},{2,3},{3,2},{4,5},{5,4},{6,7},{7,6},{8,9},{9,8},{10,11... | collective-permute-start | bytes 2359304 | tf_op jit(solution)/shard_map/ppermute | solution.py:644
  21.2 20.0 %collective-permute-start.5 = (f32[3,256,256]{2,1,0:T(8,128)S(1)}, f32[3,256,256]{2,1,0:T(8,128)S(1)}, u32[]{:S(2)}, u32[]{:S(2)}) collective-permute-start(f32[3,256,256]{2,1,0:T(8,128)S(1)} %get-tuple-element.133), channel_id=1, source_target_pairs={{1,2},{2,1},{5,6},{6,5},{9,10},{10,9},{13,14},{14,13},{17,18},{18,... | collective-permute-start | bytes 2359304 | tf_op jit(solution)/shard_map/ppermute | solution.py:648
  34.4 9.9 %collective-permute-start.6 = (f32[2,17,8,256]{3,2,1,0:T(8,128)S(1)}, f32[2,17,8,256]{3,2,1,0:T(8,128)S(1)}, u32[]{:S(2)}, u32[]{:S(2)}) collective-permute-start(f32[2,17,8,256]{3,2,1,0:T(8,128)S(1)} %get-tuple-element.135), channel_id=1, source_target_pairs={{0,64},{64,0},{1,65},{65,1},{2,66},{66,2},{3,67},{67,3},{4,68},{68... | collective-permute-start | bytes 835592 | tf_op jit(solution)/shard_map/ppermute | solution.py:652
  41.1 36.1 %collective-permute-start.11 = (f32[8,17,8,256]{3,2,1,0:T(8,128)S(1)}, f32[8,17,8,256]{3,2,1,0:T(8,128)S(1)}, u32[]{:S(2)}, u32[]{:S(2)}) collective-permute-start(f32[8,17,8,256]{3,2,1,0:T(8,128)S(1)} %get-tuple-element.153), channel_id=1, source_target_pairs={{0,64},{64,0},{1,65},{65,1},{2,66},{66,2},{3,67},{67,3},{4,68},{68... | collective-permute-start | bytes 3342344 | tf_op jit(solution)/shard_map/ppermute | solution.py:652
  54.6 9.7 %collective-permute-start.10 = (f32[2,17,8,256]{3,2,1,0:T(8,128)S(1)}, f32[2,17,8,256]{3,2,1,0:T(8,128)S(1)}, u32[]{:S(2)}, u32[]{:S(2)}) collective-permute-start(f32[2,17,8,256]{3,2,1,0:T(8,128)S(1)} %get-tuple-element.150), channel_id=1, source_target_pairs={{1,2},{2,1},{5,6},{6,5},{9,10},{10,9},{13,14},{14,13},{17,18},{18,... | collective-permute-start | bytes 835592 | tf_op jit(solution)/shard_map/ppermute | solution.py:648
  66.6 13.5 %collective-permute-start.12 = (f32[2,17,8,256]{3,2,1,0:T(8,128)S(1)}, f32[2,17,8,256]{3,2,1,0:T(8,128)S(1)}, u32[]{:S(2)}, u32[]{:S(2)}) collective-permute-start(f32[2,17,8,256]{3,2,1,0:T(8,128)S(1)} %get-tuple-element.157), channel_id=1, source_target_pairs={{0,1},{1,0},{2,3},{3,2},{4,5},{5,4},{6,7},{7,6},{8,9},{9,8},{10,11... | collective-permute-start | bytes 835592 | tf_op jit(solution)/shard_map/ppermute | solution.py:644
  66.7 13.4 %collective-permute-start.13 = (f32[2,17,8,256]{3,2,1,0:T(8,128)S(1)}, f32[2,17,8,256]{3,2,1,0:T(8,128)S(1)}, u32[]{:S(2)}, u32[]{:S(2)}) collective-permute-start(f32[2,17,8,256]{3,2,1,0:T(8,128)S(1)} %get-tuple-element.158), channel_id=1, source_target_pairs={{1,2},{2,1},{5,6},{6,5},{9,10},{10,9},{13,14},{14,13},{17,18},{18,... | collective-permute-start | bytes 835592 | tf_op jit(solution)/shard_map/ppermute | solution.py:648
  69.3 37.9 %collective-permute-start.20 = (f32[10,17,8,256]{3,2,1,0:T(8,128)S(1)}, f32[10,17,8,256]{3,2,1,0:T(8,128)S(1)}, u32[]{:S(2)}, u32[]{:S(2)}) collective-permute-start(f32[10,17,8,256]{3,2,1,0:T(8,128)S(1)} %get-tuple-element.178), channel_id=1, source_target_pairs={{0,64},{64,0},{1,65},{65,1},{2,66},{66,2},{3,67},{67,3},{4,68},{68... | collective-permute-start | bytes 4177928 | tf_op jit(solution)/shard_map/ppermute | solution.py:652
  82.4 9.4 %collective-permute-start.16 = (f32[2,17,8,256]{3,2,1,0:T(8,128)S(1)}, f32[2,17,8,256]{3,2,1,0:T(8,128)S(1)}, u32[]{:S(2)}, u32[]{:S(2)}) collective-permute-start(f32[2,17,8,256]{3,2,1,0:T(8,128)S(1)} %get-tuple-element.170), channel_id=1, source_target_pairs={{0,1},{1,0},{2,3},{3,2},{4,5},{5,4},{6,7},{7,6},{8,9},{9,8},{10,11... | collective-permute-start | bytes 835592 | tf_op jit(solution)/shard_map/ppermute | solution.py:644
  82.5 9.3 %collective-permute-start.17 = (f32[2,17,8,256]{3,2,1,0:T(8,128)S(1)}, f32[2,17,8,256]{3,2,1,0:T(8,128)S(1)}, u32[]{:S(2)}, u32[]{:S(2)}) collective-permute-start(f32[2,17,8,256]{3,2,1,0:T(8,128)S(1)} %get-tuple-element.171), channel_id=1, source_target_pairs={{1,2},{2,1},{5,6},{6,5},{9,10},{10,9},{13,14},{14,13},{17,18},{18,... | collective-permute-start | bytes 835592 | tf_op jit(solution)/shard_map/ppermute | solution.py:648
  100.4 11.6 %collective-permute-start.21 = (f32[2,17,8,256]{3,2,1,0:T(8,128)S(1)}, f32[2,17,8,256]{3,2,1,0:T(8,128)S(1)}, u32[]{:S(2)}, u32[]{:S(2)}) collective-permute-start(f32[2,17,8,256]{3,2,1,0:T(8,128)S(1)} %get-tuple-element.183), channel_id=1, source_target_pairs={{0,1},{1,0},{2,3},{3,2},{4,5},{5,4},{6,7},{7,6},{8,9},{9,8},{10,11... | collective-permute-start | bytes 835592 | tf_op jit(solution)/shard_map/ppermute | solution.py:644
  100.5 11.5 %collective-permute-start.22 = (f32[2,17,8,256]{3,2,1,0:T(8,128)S(1)}, f32[2,17,8,256]{3,2,1,0:T(8,128)S(1)}, u32[]{:S(2)}, u32[]{:S(2)}) collective-permute-start(f32[2,17,8,256]{3,2,1,0:T(8,128)S(1)} %get-tuple-element.184), channel_id=1, source_target_pairs={{1,2},{2,1},{5,6},{6,5},{9,10},{10,9},{13,14},{14,13},{17,18},{18,... | collective-permute-start | bytes 835592 | tf_op jit(solution)/shard_map/ppermute | solution.py:648
  107.4 10.3 %collective-permute-start.23 = (f32[2,17,8,256]{3,2,1,0:T(8,128)S(1)}, f32[2,17,8,256]{3,2,1,0:T(8,128)S(1)}, u32[]{:S(2)}, u32[]{:S(2)}) collective-permute-start(f32[2,17,8,256]{3,2,1,0:T(8,128)S(1)} %get-tuple-element.188), channel_id=1, source_target_pairs={{0,1},{1,0},{2,3},{3,2},{4,5},{5,4},{6,7},{7,6},{8,9},{9,8},{10,11... | collective-permute-start | bytes 835592 | tf_op jit(solution)/shard_map/ppermute | solution.py:644
  107.5 10.2 %collective-permute-start.24 = (f32[2,17,8,256]{3,2,1,0:T(8,128)S(1)}, f32[2,17,8,256]{3,2,1,0:T(8,128)S(1)}, u32[]{:S(2)}, u32[]{:S(2)}) collective-permute-start(f32[2,17,8,256]{3,2,1,0:T(8,128)S(1)} %get-tuple-element.189), channel_id=1, source_target_pairs={{1,2},{2,1},{5,6},{6,5},{9,10},{10,9},{13,14},{14,13},{17,18},{18,... | collective-permute-start | bytes 835592 | tf_op jit(solution)/shard_map/ppermute | solution.py:648
  110.1 18.6 %collective-permute-start.27 = (f32[6,17,8,256]{3,2,1,0:T(8,128)S(1)}, f32[6,17,8,256]{3,2,1,0:T(8,128)S(1)}, u32[]{:S(2)}, u32[]{:S(2)}) collective-permute-start(f32[6,17,8,256]{3,2,1,0:T(8,128)S(1)} %get-tuple-element.197), channel_id=1, source_target_pairs={{0,64},{64,0},{1,65},{65,1},{2,66},{66,2},{3,67},{67,3},{4,68},{68... | collective-permute-start | bytes 2506760 | tf_op jit(solution)/shard_map/ppermute | solution.py:652
  114.4 9.0 %collective-permute-start.25 = (f32[2,17,8,256]{3,2,1,0:T(8,128)S(1)}, f32[2,17,8,256]{3,2,1,0:T(8,128)S(1)}, u32[]{:S(2)}, u32[]{:S(2)}) collective-permute-start(f32[2,17,8,256]{3,2,1,0:T(8,128)S(1)} %get-tuple-element.193), channel_id=1, source_target_pairs={{0,1},{1,0},{2,3},{3,2},{4,5},{5,4},{6,7},{7,6},{8,9},{9,8},{10,11... | collective-permute-start | bytes 835592 | tf_op jit(solution)/shard_map/ppermute | solution.py:644
  114.5 8.9 %collective-permute-start.26 = (f32[2,17,8,256]{3,2,1,0:T(8,128)S(1)}, f32[2,17,8,256]{3,2,1,0:T(8,128)S(1)}, u32[]{:S(2)}, u32[]{:S(2)}) collective-permute-start(f32[2,17,8,256]{3,2,1,0:T(8,128)S(1)} %get-tuple-element.194), channel_id=1, source_target_pairs={{1,2},{2,1},{5,6},{6,5},{9,10},{10,9},{13,14},{14,13},{17,18},{18,... | collective-permute-start | bytes 835592 | tf_op jit(solution)/shard_map/ppermute | solution.py:648
  120.6 14.7 %collective-permute-start.28 = (f32[2,17,8,256]{3,2,1,0:T(8,128)S(1)}, f32[2,17,8,256]{3,2,1,0:T(8,128)S(1)}, u32[]{:S(2)}, u32[]{:S(2)}) collective-permute-start(f32[2,17,8,256]{3,2,1,0:T(8,128)S(1)} %get-tuple-element.202), channel_id=1, source_target_pairs={{0,1},{1,0},{2,3},{3,2},{4,5},{5,4},{6,7},{7,6},{8,9},{9,8},{10,11... | collective-permute-start | bytes 835592 | tf_op jit(solution)/shard_map/ppermute | solution.py:644
  120.7 14.7 %collective-permute-start.29 = (f32[2,17,8,256]{3,2,1,0:T(8,128)S(1)}, f32[2,17,8,256]{3,2,1,0:T(8,128)S(1)}, u32[]{:S(2)}, u32[]{:S(2)}) collective-permute-start(f32[2,17,8,256]{3,2,1,0:T(8,128)S(1)} %get-tuple-element.203), channel_id=1, source_target_pairs={{1,2},{2,1},{5,6},{6,5},{9,10},{10,9},{13,14},{14,13},{17,18},{18,... | collective-permute-start | bytes 835592 | tf_op jit(solution)/shard_map/ppermute | solution.py:648
  132.2 9.5 %collective-permute-start.31 = (f32[2,17,8,256]{3,2,1,0:T(8,128)S(1)}, f32[2,17,8,256]{3,2,1,0:T(8,128)S(1)}, u32[]{:S(2)}, u32[]{:S(2)}) collective-permute-start(f32[2,17,8,256]{3,2,1,0:T(8,128)S(1)} %get-tuple-element.208), channel_id=1, source_target_pairs={{1,2},{2,1},{5,6},{6,5},{9,10},{10,9},{13,14},{14,13},{17,18},{18,... | collective-permute-start | bytes 835592 | tf_op jit(solution)/shard_map/ppermute | solution.py:648
  137.7 10.6 %collective-permute-start.32 = (f32[2,17,8,256]{3,2,1,0:T(8,128)S(1)}, f32[2,17,8,256]{3,2,1,0:T(8,128)S(1)}, u32[]{:S(2)}, u32[]{:S(2)}) collective-permute-start(f32[2,17,8,256]{3,2,1,0:T(8,128)S(1)} %get-tuple-element.212), channel_id=1, source_target_pairs={{0,1},{1,0},{2,3},{3,2},{4,5},{5,4},{6,7},{7,6},{8,9},{9,8},{10,11... | collective-permute-start | bytes 835592 | tf_op jit(solution)/shard_map/ppermute | solution.py:644
  137.8 11.3 %collective-permute-start.33 = (f32[2,17,8,256]{3,2,1,0:T(8,128)S(1)}, f32[2,17,8,256]{3,2,1,0:T(8,128)S(1)}, u32[]{:S(2)}, u32[]{:S(2)}) collective-permute-start(f32[2,17,8,256]{3,2,1,0:T(8,128)S(1)} %get-tuple-element.213), channel_id=1, source_target_pairs={{1,2},{2,1},{5,6},{6,5},{9,10},{10,9},{13,14},{14,13},{17,18},{18,... | collective-permute-start | bytes 835592 | tf_op jit(solution)/shard_map/ppermute | solution.py:648
  144.1 10.3 %collective-permute-start.34 = (f32[2,17,8,256]{3,2,1,0:T(8,128)S(1)}, f32[2,17,8,256]{3,2,1,0:T(8,128)S(1)}, u32[]{:S(2)}, u32[]{:S(2)}) collective-permute-start(f32[2,17,8,256]{3,2,1,0:T(8,128)S(1)} %get-tuple-element.216), channel_id=1, source_target_pairs={{0,1},{1,0},{2,3},{3,2},{4,5},{5,4},{6,7},{7,6},{8,9},{9,8},{10,11... | collective-permute-start | bytes 835592 | tf_op jit(solution)/shard_map/ppermute | solution.py:644
  144.2 10.4 %collective-permute-start.35 = (f32[2,17,8,256]{3,2,1,0:T(8,128)S(1)}, f32[2,17,8,256]{3,2,1,0:T(8,128)S(1)}, u32[]{:S(2)}, u32[]{:S(2)}) collective-permute-start(f32[2,17,8,256]{3,2,1,0:T(8,128)S(1)} %get-tuple-element.217), channel_id=1, source_target_pairs={{1,2},{2,1},{5,6},{6,5},{9,10},{10,9},{13,14},{14,13},{17,18},{18,... | collective-permute-start | bytes 835592 | tf_op jit(solution)/shard_map/ppermute | solution.py:648
  151.4 9.9 %collective-permute-start.36 = (f32[2,17,8,256]{3,2,1,0:T(8,128)S(1)}, f32[2,17,8,256]{3,2,1,0:T(8,128)S(1)}, u32[]{:S(2)}, u32[]{:S(2)}) collective-permute-start(f32[2,17,8,256]{3,2,1,0:T(8,128)S(1)} %get-tuple-element.220), channel_id=1, source_target_pairs={{0,1},{1,0},{2,3},{3,2},{4,5},{5,4},{6,7},{7,6},{8,9},{9,8},{10,11... | collective-permute-start | bytes 835592 | tf_op jit(solution)/shard_map/ppermute | solution.py:644
  151.5 11.3 %collective-permute-start.37 = (f32[2,17,8,256]{3,2,1,0:T(8,128)S(1)}, f32[2,17,8,256]{3,2,1,0:T(8,128)S(1)}, u32[]{:S(2)}, u32[]{:S(2)}) collective-permute-start(f32[2,17,8,256]{3,2,1,0:T(8,128)S(1)} %get-tuple-element.221), channel_id=1, source_target_pairs={{1,2},{2,1},{5,6},{6,5},{9,10},{10,9},{13,14},{14,13},{17,18},{18,... | collective-permute-start | bytes 835592 | tf_op jit(solution)/shard_map/ppermute | solution.py:648
  157.0 9.1 %collective-permute-start.38 = (f32[2,17,8,256]{3,2,1,0:T(8,128)S(1)}, f32[2,17,8,256]{3,2,1,0:T(8,128)S(1)}, u32[]{:S(2)}, u32[]{:S(2)}) collective-permute-start(f32[2,17,8,256]{3,2,1,0:T(8,128)S(1)} %get-tuple-element.225), channel_id=1, source_target_pairs={{0,1},{1,0},{2,3},{3,2},{4,5},{5,4},{6,7},{7,6},{8,9},{9,8},{10,11... | collective-permute-start | bytes 835592 | tf_op jit(solution)/shard_map/ppermute | solution.py:644
  157.1 9.0 %collective-permute-start.39 = (f32[2,17,8,256]{3,2,1,0:T(8,128)S(1)}, f32[2,17,8,256]{3,2,1,0:T(8,128)S(1)}, u32[]{:S(2)}, u32[]{:S(2)}) collective-permute-start(f32[2,17,8,256]{3,2,1,0:T(8,128)S(1)} %get-tuple-element.226), channel_id=1, source_target_pairs={{1,2},{2,1},{5,6},{6,5},{9,10},{10,9},{13,14},{14,13},{17,18},{18,... | collective-permute-start | bytes 835592 | tf_op jit(solution)/shard_map/ppermute | solution.py:648
  (9 other events, 64.5 us)

commit v2 on v1

--- a/solution.py
+++ b/solution.py
@@ -92,13 +92,13 @@
             scratch_shapes=scratch,
             input_output_aliases={k + 1: v for k, v in (aliases or {}).items()},
             compiler_params=pltpu.CompilerParams(vmem_limit_bytes=limit_mib << 20),
-            cost_estimate=pl.CostEstimate(flops=int(us * 1e9), bytes_accessed=0, transcendentals=0),
+            cost_estimate=pl.CostEstimate(flops=int(us * FLOPS), bytes_accessed=0, transcendentals=0),
             name=name,
         )(*operands)
         return results
 
 
-SCALE = 1_500_000
+FLOPS = 7e8
 
 
 def zprev(v):
@@ -234,10 +234,11 @@
             kp[p, r] = rows_of(buf, 3 * p + 2, r)
         return carry
 
-    lax.fori_loop(0, PLANES, convert, 0)
+    lax.fori_loop(0, 2, convert, 0)
 
     def plane(i, carry):
         p = i + 1
+        convert(p + 1, carry)
 
         def emit(r, f):
             rem0[i + offset0, r] = remote[0][0] * f[0] + remote[0][1] * f[1]
@@ -261,28 +262,26 @@
     lax.fori_loop(0, PLANES - 2, plane, 0)
 
 
-def faces_kernel(nodes, cond, na, nb, fa, fb, sems):
+def faces_kernel(depth, nodes, cond, sa, sb, sems):
     even = lax.rem(lax.axis_index("space"), 2) == 0
 
-    def copies(high_near, high_far, low_near, low_far):
+    def copies(high, low):
         pairs = []
-        for (near, far), (first, second) in (((high_near, high_far), (PLANES - 1, PLANES - 2)), ((low_near, low_far), (0, 1))):
-            pairs += [(cond.at[first], near.at[0]), (cond.at[second], far.at[0])]
-            for j in range(2):
-                pairs += [(nodes.at[0, j, first], near.at[1 + j]), (nodes.at[0, j, second], far.at[1 + j])]
+        for dst, p in ((high, PLANES - 1 - depth), (low, depth)):
+            pairs += [(cond.at[p], dst.at[0])] + [(nodes.at[0, j, p], dst.at[1 + j]) for j in range(2)]
         return [pltpu.make_async_copy(src, dst, sems.at[i]) for i, (src, dst) in enumerate(pairs)]
 
     @pl.when(even)
     def _():
-        for c in copies(na, fa, nb, fb):
+        for c in copies(sa, sb):
             c.start()
 
     @pl.when(jnp.logical_not(even))
     def _():
-        for c in copies(nb, fb, na, fa):
+        for c in copies(sb, sa):
             c.start()
 
-    for c in copies(na, fa, nb, fb):
+    for c in copies(sa, sb):
         c.wait()
 
 
@@ -654,17 +653,20 @@
 
 def body(nodes, prev_final, u_init, cond):
     order = Order()
-    plane_shape = lambda n: pltpu.VMEM((n, NY, NZ), F32)
-    na, nb, fa, fb = order.call(
-        "faces",
-        faces_kernel,
-        [(plane_shape(3), VM)] * 4,
-        [(nodes, None), (cond, None)],
-        [DMA((12,))],
-        4,
-        1.0,
-    )
-    na, nb, fa, fb = to_a(na), to_b(nb), to_a(fa), to_b(fb)
+
+    def faces(depth):
+        sa, sb = order.call(
+            "faces%d" % depth,
+            functools.partial(faces_kernel, depth),
+            [(pltpu.VMEM((3, NY, NZ), F32), VM)] * 2,
+            [(nodes, None), (cond, None)],
+            [DMA((6,))],
+            4,
+            0.7,
+        )
+        return to_a(sa), to_b(sb)
+
+    na, nb = faces(0)
     half = lax.axis_size("tm") // 2
     blocks = 2 * half
     pairs = [
@@ -720,10 +722,10 @@
             3.5,
         )
 
+    fa, fb = faces(1)
     z_start = swap_nodes(inner[0][2])
     edge_step(0)
     edge_step(1)
-    coef_step(0)
 
     units = [(m, part) for m in range(2) for part in range(2)]
     z_inner = [z_start] + [swap_nodes(x) for x in (edges[1][0], edges[1][1], inner[1][3])]
@@ -817,7 +819,7 @@
 
     C, R, S, N, M, L = range(6)
     plan = (
-        (R, 0), (C, 1), (S, 0), (N, 0), (R, 1), (M, 0), (S, 1), (L, 0), (N, 1), (R, 2),
+        (R, 0), (C, 0), (C, 1), (S, 0), (N, 0), (R, 1), (M, 0), (S, 1), (L, 0), (N, 1), (R, 2),
         (M, 1), (S, 2), (L, 1), (S, 3), (N, 2), (N, 3), (M, 2), (M, 3), (L, 2), (L, 3),
     )
     for kind, unit in plan:

time: 172 us -> 169 us (0.983)
  starting transfers between devices: 72.5 us -> 57.9 us
  waiting for transfers between devices: 25.7 us -> 38.7 us
    ppermute x5, starting transfers between devices: 16.1 us -> 6.27 us  [swap_nodes(): return lax.ppermute(x, 'node', [(0, 1), (1, 0)])]
    ppermute x17, waiting for transfers between devices: 9.51 us -> 18.2 us  [to_b(): return lax.ppermute(x, 'space', SWAP_B)]
    ppermute x17, starting transfers between devices: 52.2 us -> 46.4 us  [to_b(): return lax.ppermute(x, 'space', SWAP_B)]
    ppermute x17, waiting for transfers between devices: 9.71 us -> 12.9 us  [to_a(): return lax.ppermute(x, 'space', SWAP_A)]
    pallas_call x26 -> x27, Pallas kernels: 71.4 us -> 70.9 us  [call(): pl.pallas_call(run, out_shape=[o if s is VM else jax.ShapeDtypeStruct(o,...]
  transfers between devices with their start and end apart: 40 -> 40, of which waited for: 14 -> 22; matrix products, arithmetic and copies ran while one was open for 0% -> 0% of each run, Pallas kernels for 40% -> 40%
where the time goes in v2:
time: 169 us; the launch traced here: 168 us
  Pallas kernels  70.9 us (42%)
  starting transfers between devices  57.9 us (34%)
  waiting for transfers between devices  38.7 us (23%)
    pallas_call x27, Pallas kernels, call(): pl.pallas_call(run, out_shape=[o if s is VM else jax.ShapeDtypeStruct(o,...  70.9 us
    ppermute x17, starting transfers between devices, to_b(): return lax.ppermute(x, 'space', SWAP_B)  46.4 us
    ppermute x17, waiting for transfers between devices, to_b(): return lax.ppermute(x, 'space', SWAP_B)  18.2 us
    ppermute x17, waiting for transfers between devices, to_a(): return lax.ppermute(x, 'space', SWAP_A)  12.9 us
    ppermute x5, waiting for transfers between devices, swap_nodes(): return lax.ppermute(x, 'node', [(0, 1), (1, 0)])  7.64 us
    ppermute x5, starting transfers between devices, swap_nodes(): return lax.ppermute(x, 'node', [(0, 1), (1, 0)])  6.27 us
  transfers between devices with their start and end apart: 40, of which 22 were waited for; matrix products, arithmetic and copies ran while one was open for 0% of the time, Pallas kernels for 40%

profile of v2, /device:TPU:14, one launch (start us, length us, event | category | flops | bytes accessed | tf_op | source)
XLA Modules:
  0.0 168.3 jit_solution(5098823631708355234)
XLA Ops:
  3.9 4.3 %collective-permute-start.1 = (f32[3,256,256]{2,1,0:T(8,128)S(1)}, f32[3,256,256]{2,1,0:T(8,128)S(1)}, u32[]{:S(2)}, u32[]{:S(2)}) collective-permute-start(f32[3,256,256]{2,1,0:T(8,128)S(1)} %get-tuple-element.125), channel_id=1, source_target_pairs={{1,2},{2,1},{5,6},{6,5},{9,10},{10,9},{13,14},{14,13},{17,18},{18,... | collective-permute-start | bytes 2359304 | tf_op jit(solution)/shard_map/ppermute | solution.py:647
  8.2 6.6 %inner0.1 = (f32[16,17,8,256]{3,2,1,0:T(8,128)S(1)}, f32[8,17,8,256]{3,2,1,0:T(8,128)S(1)}, f32[6,17,8,256]{3,2,1,0:T(8,128)S(1)}, f32[10,17,8,256]{3,2,1,0:T(8,...) custom-call(f32[8,128]{1,0:T(8,128)S(1)} %get-tuple-element.118.before, ...), custom_call_target="tpu_custom_call" | custom-call | flops 3500000000 | tf_op jit(solution)/shard_map/inner0/pallas_call | solution.py:87
  16.8 6.5 %inner1.1 = (f32[16,17,8,256]{3,2,1,0:T(8,128)S(1)}, f32[8,17,8,256]{3,2,1,0:T(8,128)S(1)}, f32[8,17,8,256]{3,2,1,0:T(8,128)S(1)}, f32[6,17,8,256]{3,2,1,0:T(8,1...) custom-call(f32[8,128]{1,0:T(8,128)S(1)} %get-tuple-element.119.before, ...), custom_call_target="tpu_custom_call" | custom-call | flops 3500000000 | tf_op jit(solution)/shard_map/inner1/pallas_call | solution.py:87
  26.8 2.5 %edge0.1 = (f32[2,17,8,256]{3,2,1,0:T(8,128)S(1)}, f32[10,17,8,256]{3,2,1,0:T(8,128)S(1)}, f32[2,17,8,256]{3,2,1,0:T(8,128)S(1)}, f32[2,17,8,256]{3,2,1,0:T(8,128)S(1)}, f32[8,128]{1,0:T(8,128)S(1)}) custom-call(f32[8,128]{1,0:T(8,128)S(1)} %get-tuple-element.121.before, ...), custom_call_target="tpu_custom_call", output_to_operand_aliasing={{1}: (5, {})} | custom-call | flops 1750000000 | tf_op jit(solution)/shard_map/edge0/pallas_call | solution.py:87
  30.9 4.0 %collective-permute-done.3.refs_7_.refs_0_ = f32[6,17,8,256]{3,2,1,0:T(8,128)S(1)} collective-permute-done((f32[6,17,8,256]{3,2,1,0:T(8,128)S(1)}, f32[6,17,8,256]{3,2,1,0:T(8,128)S(1)}, u32[]{:S(2)}, u32[]{:S(2)}) %collective-permute-start.3) | collective-permute-done | bytes 835616 | tf_op jit(solution)/shard_map/ppermute | solution.py:651
  34.9 2.5 %edge1.1 = (f32[8,17,8,256]{3,2,1,0:T(8,128)S(1)}, f32[10,17,8,256]{3,2,1,0:T(8,128)S(1)}, f32[2,17,8,256]{3,2,1,0:T(8,128)S(1)}, f32[2,17,8,256]{3,2,1,0:T(8,128)S(1)}, f32[8,128]{1,0:T(8,128)S(1)}) custom-call(f32[8,128]{1,0:T(8,128)S(1)} %get-tuple-element.127.before, ...), custom_call_target="tpu_custom_call", output_to_operand_aliasing={{0}: (5, {}), {1}: (6, {})} | custom-call | flops 1750000000 | tf_op jit(solution)/shard_map/edge1/pallas_call | solution.py:87
  37.3 3.5 %collective-permute-done.4.refs_0_ = f32[2,17,8,256]{3,2,1,0:T(8,128)S(1)} collective-permute-done((f32[2,17,8,256]{3,2,1,0:T(8,128)S(1)}, f32[2,17,8,256]{3,2,1,0:T(8,128)S(1)}, u32[]{:S(2)}, u32[]{:S(2)}) %collective-permute-start.4) | collective-permute-done | bytes 278560 | tf_op jit(solution)/shard_map/ppermute | solution.py:651
  43.1 2.5 %collective-permute-start.11 = (f32[8,17,8,256]{3,2,1,0:T(8,128)S(1)}, f32[8,17,8,256]{3,2,1,0:T(8,128)S(1)}, u32[]{:S(2)}, u32[]{:S(2)}) collective-permute-start(f32[8,17,8,256]{3,2,1,0:T(8,128)S(1)} %get-tuple-element.155), channel_id=1, source_target_pairs={{0,64},{64,0},{1,65},{65,1},{2,66},{66,2},{3,67},{67,3},{4,68},{68... | collective-permute-start | bytes 3342344 | tf_op jit(solution)/shard_map/ppermute | solution.py:651
  51.1 3.0 %first0.1 = (f32[10,17,8,256]{3,2,1,0:T(8,128)S(1)}, f32[8,17,8,256]{3,2,1,0:T(8,128)S(1)}, f32[2,17,8,256]{3,2,1,0:T(8,128)S(1)}, f32[2,17,8,256]{3,2,1,0:T(8,128)S(1)}, f32[8,128]{1,0:T(8,128)S(1)}) custom-call(f32[8,128]{1,0:T(8,128)S(1)} %get-tuple-element.140.before, f32[6,17,8,256]{3,2,1,0:T(8,128)S(1)} %collective-permute-done.3.refs_7_.refs_0_, ...), custom_call_target="tpu_custom_call" | custom-call | flops 2100000000 | tf_op jit(solution)/shard_map/first0/pallas_call | solution.py:87
  54.2 2.9 %collective-permute-start.10 = (f32[2,17,8,256]{3,2,1,0:T(8,128)S(1)}, f32[2,17,8,256]{3,2,1,0:T(8,128)S(1)}, u32[]{:S(2)}, u32[]{:S(2)}) collective-permute-start(f32[2,17,8,256]{3,2,1,0:T(8,128)S(1)} %get-tuple-element.152), channel_id=1, source_target_pairs={{1,2},{2,1},{5,6},{6,5},{9,10},{10,9},{13,14},{14,13},{17,18},{18,... | collective-permute-start | bytes 835592 | tf_op jit(solution)/shard_map/ppermute | solution.py:647
  57.3 6.1 %collective-permute-done.9.refs_1_ = f32[2,17,8,256]{3,2,1,0:T(8,128)S(1)} collective-permute-done((f32[2,17,8,256]{3,2,1,0:T(8,128)S(1)}, f32[2,17,8,256]{3,2,1,0:T(8,128)S(1)}, u32[]{:S(2)}, u32[]{:S(2)}) %collective-permute-start.9) | collective-permute-done | bytes 278560 | tf_op jit(solution)/shard_map/ppermute | solution.py:643
  67.7 2.8 %collective-permute-start.13 = (f32[2,17,8,256]{3,2,1,0:T(8,128)S(1)}, f32[2,17,8,256]{3,2,1,0:T(8,128)S(1)}, u32[]{:S(2)}, u32[]{:S(2)}) collective-permute-start(f32[2,17,8,256]{3,2,1,0:T(8,128)S(1)} %get-tuple-element.160), channel_id=1, source_target_pairs={{1,2},{2,1},{5,6},{6,5},{9,10},{10,9},{13,14},{14,13},{17,18},{18,... | collective-permute-start | bytes 835592 | tf_op jit(solution)/shard_map/ppermute | solution.py:647
  71.9 3.2 %collective-permute-start.15 = (f32[1,17,8,256]{3,2,1,0:T(8,128)S(1)}, f32[1,17,8,256]{3,2,1,0:T(8,128)S(1)}, u32[]{:S(2)}, u32[]{:S(2)}) collective-permute-start(f32[1,17,8,256]{3,2,1,0:T(8,128)S(1)} %get-tuple-element.165), channel_id=1, source_target_pairs={{1,2},{2,1},{5,6},{6,5},{9,10},{10,9},{13,14},{14,13},{17,18},{18,... | collective-permute-start | bytes 417800 | tf_op jit(solution)/shard_map/ppermute | solution.py:647
  81.5 2.7 %collective-permute-start.17 = (f32[2,17,8,256]{3,2,1,0:T(8,128)S(1)}, f32[2,17,8,256]{3,2,1,0:T(8,128)S(1)}, u32[]{:S(2)}, u32[]{:S(2)}) collective-permute-start(f32[2,17,8,256]{3,2,1,0:T(8,128)S(1)} %get-tuple-element.173), channel_id=1, source_target_pairs={{1,2},{2,1},{5,6},{6,5},{9,10},{10,9},{13,14},{14,13},{17,18},{18,... | collective-permute-start | bytes 835592 | tf_op jit(solution)/shard_map/ppermute | solution.py:647
  84.2 3.1 %first1.1 = (f32[10,17,8,256]{3,2,1,0:T(8,128)S(1)}, f32[8,17,8,256]{3,2,1,0:T(8,128)S(1)}, f32[2,17,8,256]{3,2,1,0:T(8,128)S(1)}, f32[2,17,8,256]{3,2,1,0:T(8,128)S(1)}, f32[8,128]{1,0:T(8,128)S(1)}) custom-call(f32[8,128]{1,0:T(8,128)S(1)} %get-tuple-element.161.before, f32[8,17,8,256]{3,2,1,0:T(8,128)S(1)} %collective-permute-done.11.refs_0_, ...), custom_call_target="tpu_custom_call" | custom-call | flops 2100000000 | tf_op jit(solution)/shard_map/first1/pallas_call | solution.py:87
  87.5 3.2 %collective-permute-start.19 = (f32[2,17,8,256]{3,2,1,0:T(8,128)S(1)}, f32[2,17,8,256]{3,2,1,0:T(8,128)S(1)}, u32[]{:S(2)}, u32[]{:S(2)}) collective-permute-start(f32[2,17,8,256]{3,2,1,0:T(8,128)S(1)} %get-tuple-element.177), channel_id=1, source_target_pairs={{1,2},{2,1},{5,6},{6,5},{9,10},{10,9},{13,14},{14,13},{17,18},{18,... | collective-permute-start | bytes 835592 | tf_op jit(solution)/shard_map/ppermute | solution.py:647
  91.5 3.3 %last0.1 = (f32[1,2,8,256,256]{4,3,2,1,0:T(8,128)}, f32[8,128]{1,0:T(8,128)S(1)}) custom-call(f32[8,128]{1,0:T(8,128)S(1)} %get-tuple-element.170.before, f32[8,17,8,256]{3,2,1,0:T(8,128)S(1)} %get-tuple-element.171.refs_0_, f32[2,17,8,256]{3,2,1,0:T(8,128)S(1)} %collective-permute-done.16.refs_1_, f32[2,17,8,256]{3,2,1,0:T(8,128)S(1)} %collective-permute-done.17.refs_2_, ...), custom_call_target="tpu_custom_call" | custom-call | flops 2449999872 | tf_op jit(solution)/shard_map/last0/pallas_call | solution.py:87
  99.5 3.0 %collective-permute-start.22 = (f32[2,17,8,256]{3,2,1,0:T(8,128)S(1)}, f32[2,17,8,256]{3,2,1,0:T(8,128)S(1)}, u32[]{:S(2)}, u32[]{:S(2)}) collective-permute-start(f32[2,17,8,256]{3,2,1,0:T(8,128)S(1)} %get-tuple-element.186), channel_id=1, source_target_pairs={{1,2},{2,1},{5,6},{6,5},{9,10},{10,9},{13,14},{14,13},{17,18},{18,... | collective-permute-start | bytes 835592 | tf_op jit(solution)/shard_map/ppermute | solution.py:647
  103.0 2.9 %collective-permute-start.24 = (f32[2,17,8,256]{3,2,1,0:T(8,128)S(1)}, f32[2,17,8,256]{3,2,1,0:T(8,128)S(1)}, u32[]{:S(2)}, u32[]{:S(2)}) collective-permute-start(f32[2,17,8,256]{3,2,1,0:T(8,128)S(1)} %get-tuple-element.191), channel_id=1, source_target_pairs={{1,2},{2,1},{5,6},{6,5},{9,10},{10,9},{13,14},{14,13},{17,18},{18,... | collective-permute-start | bytes 835592 | tf_op jit(solution)/shard_map/ppermute | solution.py:647
  105.9 3.1 %collective-permute-done.21.refs_1_ = f32[2,17,8,256]{3,2,1,0:T(8,128)S(1)} collective-permute-done((f32[2,17,8,256]{3,2,1,0:T(8,128)S(1)}, f32[2,17,8,256]{3,2,1,0:T(8,128)S(1)}, u32[]{:S(2)}, u32[]{:S(2)}) %collective-permute-start.21) | collective-permute-done | bytes 278560 | tf_op jit(solution)/shard_map/ppermute | solution.py:643
  115.8 2.9 %first2.1 = (f32[10,17,8,256]{3,2,1,0:T(8,128)S(1)}, f32[8,17,8,256]{3,2,1,0:T(8,128)S(1)}, f32[2,17,8,256]{3,2,1,0:T(8,128)S(1)}, f32[2,17,8,256]{3,2,1,0:T(8,128)S(1)}, f32[8,128]{1,0:T(8,128)S(1)}) custom-call(f32[8,128]{1,0:T(8,128)S(1)} %get-tuple-element.187.before, f32[10,17,8,256]{3,2,1,0:T(8,128)S(1)} %collective-permute-done.20.refs_0_.refs_1_, ...), custom_call_target="tpu_custom_call" | custom-call | flops 2100000000 | tf_op jit(solution)/shard_map/first2/pallas_call | solution.py:87
  118.8 2.7 %collective-permute-start.29 = (f32[2,17,8,256]{3,2,1,0:T(8,128)S(1)}, f32[2,17,8,256]{3,2,1,0:T(8,128)S(1)}, u32[]{:S(2)}, u32[]{:S(2)}) collective-permute-start(f32[2,17,8,256]{3,2,1,0:T(8,128)S(1)} %get-tuple-element.205), channel_id=1, source_target_pairs={{1,2},{2,1},{5,6},{6,5},{9,10},{10,9},{13,14},{14,13},{17,18},{18,... | collective-permute-start | bytes 835592 | tf_op jit(solution)/shard_map/ppermute | solution.py:647
  122.2 3.4 %last1.1 = (f32[1,2,8,256,256]{4,3,2,1,0:T(8,128)}, f32[8,128]{1,0:T(8,128)S(1)}) custom-call(f32[8,128]{1,0:T(8,128)S(1)} %get-tuple-element.193.before, f32[8,17,8,256]{3,2,1,0:T(8,128)S(1)} %get-tuple-element.194.refs_0_, f32[2,17,8,256]{3,2,1,0:T(8,128)S(1)} %collective-permute-done.25.refs_1_, ...), custom_call_target="tpu_custom_call", output_to_operand_aliasing={{0}: (9, {})} | custom-call | flops 2449999872 | tf_op jit(solution)/shard_map/last1/pallas_call | solution.py:87
  125.7 3.1 %first3.1 = (f32[10,17,8,256]{3,2,1,0:T(8,128)S(1)}, f32[8,17,8,256]{3,2,1,0:T(8,128)S(1)}, f32[2,17,8,256]{3,2,1,0:T(8,128)S(1)}, f32[2,17,8,256]{3,2,1,0:T(8,128)S(1)}, f32[8,128]{1,0:T(8,128)S(1)}) custom-call(f32[8,128]{1,0:T(8,128)S(1)} %get-tuple-element.198.before, f32[6,17,8,256]{3,2,1,0:T(8,128)S(1)} %collective-permute-done.27.refs_0_, ...), custom_call_target="tpu_custom_call" | custom-call | flops 2100000000 | tf_op jit(solution)/shard_map/first3/pallas_call | solution.py:87
  128.8 2.5 %collective-permute-start.31 = (f32[2,17,8,256]{3,2,1,0:T(8,128)S(1)}, f32[2,17,8,256]{3,2,1,0:T(8,128)S(1)}, u32[]{:S(2)}, u32[]{:S(2)}) collective-permute-start(f32[2,17,8,256]{3,2,1,0:T(8,128)S(1)} %get-tuple-element.210), channel_id=1, source_target_pairs={{1,2},{2,1},{5,6},{6,5},{9,10},{10,9},{13,14},{14,13},{17,18},{18,... | collective-permute-start | bytes 835592 | tf_op jit(solution)/shard_map/ppermute | solution.py:647
  133.9 3.2 %collective-permute-start.33 = (f32[2,17,8,256]{3,2,1,0:T(8,128)S(1)}, f32[2,17,8,256]{3,2,1,0:T(8,128)S(1)}, u32[]{:S(2)}, u32[]{:S(2)}) collective-permute-start(f32[2,17,8,256]{3,2,1,0:T(8,128)S(1)} %get-tuple-element.215), channel_id=1, source_target_pairs={{1,2},{2,1},{5,6},{6,5},{9,10},{10,9},{13,14},{14,13},{17,18},{18,... | collective-permute-start | bytes 835592 | tf_op jit(solution)/shard_map/ppermute | solution.py:647
  140.3 2.4 %next3_3.1 = (f32[8,17,8,256]{3,2,1,0:T(8,128)S(1)}, f32[2,17,8,256]{3,2,1,0:T(8,128)S(1)}, f32[2,17,8,256]{3,2,1,0:T(8,128)S(1)}, f32[8,128]{1,0:T(8,128)S(1)}) custom-call(f32[8,128]{1,0:T(8,128)S(1)} %get-tuple-element.207.before, f32[8,17,8,256]{3,2,1,0:T(8,128)S(1)} %get-tuple-element.208.refs_0_, ...), custom_call_target="tpu_custom_call" | custom-call | flops 1750000000 | tf_op jit(solution)/shard_map/next3_3/pallas_call | solution.py:87
  148.6 2.5 %collective-permute-start.37 = (f32[2,17,8,256]{3,2,1,0:T(8,128)S(1)}, f32[2,17,8,256]{3,2,1,0:T(8,128)S(1)}, u32[]{:S(2)}, u32[]{:S(2)}) collective-permute-start(f32[2,17,8,256]{3,2,1,0:T(8,128)S(1)} %get-tuple-element.223), channel_id=1, source_target_pairs={{1,2},{2,1},{5,6},{6,5},{9,10},{10,9},{13,14},{14,13},{17,18},{18,... | collective-permute-start | bytes 835592 | tf_op jit(solution)/shard_map/ppermute | solution.py:647
  153.1 2.4 %next3_4.1 = (f32[8,17,8,256]{3,2,1,0:T(8,128)S(1)}, f32[2,17,8,256]{3,2,1,0:T(8,128)S(1)}, f32[2,17,8,256]{3,2,1,0:T(8,128)S(1)}, f32[8,128]{1,0:T(8,128)S(1)}) custom-call(f32[8,128]{1,0:T(8,128)S(1)} %get-tuple-element.216.before, f32[8,17,8,256]{3,2,1,0:T(8,128)S(1)} %get-tuple-element.217.refs_0_, ...), custom_call_target="tpu_custom_call" | custom-call | flops 1750000000 | tf_op jit(solution)/shard_map/next3_4/pallas_call | solution.py:87
  155.6 2.7 %collective-permute-start.39 = (f32[2,17,8,256]{3,2,1,0:T(8,128)S(1)}, f32[2,17,8,256]{3,2,1,0:T(8,128)S(1)}, u32[]{:S(2)}, u32[]{:S(2)}) collective-permute-start(f32[2,17,8,256]{3,2,1,0:T(8,128)S(1)} %get-tuple-element.228), channel_id=1, source_target_pairs={{1,2},{2,1},{5,6},{6,5},{9,10},{10,9},{13,14},{14,13},{17,18},{18,... | collective-permute-start | bytes 835592 | tf_op jit(solution)/shard_map/ppermute | solution.py:647
  159.2 3.3 %last2.1 = (f32[1,2,8,256,256]{4,3,2,1,0:T(8,128)}, f32[8,128]{1,0:T(8,128)S(1)}) custom-call(f32[8,128]{1,0:T(8,128)S(1)} %get-tuple-element.220.before, f32[8,17,8,256]{3,2,1,0:T(8,128)S(1)} %get-tuple-element.221.refs_0_, f32[2,17,8,256]{3,2,1,0:T(8,128)S(1)} %collective-permute-done.36.refs_1_, ...), custom_call_target="tpu_custom_call", output_to_operand_aliasing={{0}: (9, {})} | custom-call | flops 2449999872 | tf_op jit(solution)/shard_map/last2/pallas_call | solution.py:87
  164.1 4.1 %last3.1 = (f32[1,2,8,256,256]{4,3,2,1,0:T(8,128)}, f32[8,128]{1,0:T(8,128)}) custom-call(f32[8,128]{1,0:T(8,128)S(1)} %get-tuple-element.225.before, f32[8,17,8,256]{3,2,1,0:T(8,128)S(1)} %get-tuple-element.226.refs_0_, f32[2,17,8,256]{3,2,1,0:T(8,128)S(1)} %collective-permute-done.38.refs_1_, ...), custom_call_target="tpu_custom_call", output_to_operand_aliasing={{0}: (9, {})} | custom-call | flops 2449999872 | tf_op jit(solution)/shard_map/last3/pallas_call | solution.py:87
  (78 shorter events, 60.8 us)
Async XLA Ops:
  0.0 34.9 %collective-permute-start.2 = (f32[8,256,256]{2,1,0:T(8,128)}, f32[8,256,256]{2,1,0:T(8,128)S(1)}, u32[]{:S(2)}, u32[]{:S(2)}) collective-permute-start(f32[8,256,256]{2,1,0:T(8,128)} %bitcast.1), channel_id=1, source_target_pairs={{0,4},{4,8},{8,12},{12,16},{16,20},{20,24},{24,28},{28,96},{32,36}... | collective-permute-start | bytes 6291464 | tf_op jit(solution)/shard_map/ppermute | solution.py:677
  3.3 21.5 %collective-permute-start = (f32[3,256,256]{2,1,0:T(8,128)S(1)}, f32[3,256,256]{2,1,0:T(8,128)S(1)}, u32[]{:S(2)}, u32[]{:S(2)}) collective-permute-start(f32[3,256,256]{2,1,0:T(8,128)S(1)} %get-tuple-element.124), channel_id=1, source_target_pairs={{0,1},{1,0},{2,3},{3,2},{4,5},{5,4},{6,7},{7,6},{8,9},{9,8},{10,11... | collective-permute-start | bytes 2359304 | tf_op jit(solution)/shard_map/ppermute | solution.py:643
  3.9 22.9 %collective-permute-start.1 = (f32[3,256,256]{2,1,0:T(8,128)S(1)}, f32[3,256,256]{2,1,0:T(8,128)S(1)}, u32[]{:S(2)}, u32[]{:S(2)}) collective-permute-start(f32[3,256,256]{2,1,0:T(8,128)S(1)} %get-tuple-element.125), channel_id=1, source_target_pairs={{1,2},{2,1},{5,6},{6,5},{9,10},{10,9},{13,14},{14,13},{17,18},{18,... | collective-permute-start | bytes 2359304 | tf_op jit(solution)/shard_map/ppermute | solution.py:647
  14.8 20.1 %collective-permute-start.3 = (f32[6,17,8,256]{3,2,1,0:T(8,128)S(1)}, f32[6,17,8,256]{3,2,1,0:T(8,128)S(1)}, u32[]{:S(2)}, u32[]{:S(2)}) collective-permute-start(f32[6,17,8,256]{3,2,1,0:T(8,128)S(1)} %get-tuple-element.132), channel_id=1, source_target_pairs={{0,64},{64,0},{1,65},{65,1},{2,66},{66,2},{3,67},{67,3},{4,68},{68... | collective-permute-start | bytes 2506760 | tf_op jit(solution)/shard_map/ppermute | solution.py:651
  24.7 20.8 %collective-permute-start.5 = (f32[3,256,256]{2,1,0:T(8,128)S(1)}, f32[3,256,256]{2,1,0:T(8,128)S(1)}, u32[]{:S(2)}, u32[]{:S(2)}) collective-permute-start(f32[3,256,256]{2,1,0:T(8,128)S(1)} %get-tuple-element.137), channel_id=1, source_target_pairs={{0,1},{1,0},{2,3},{3,2},{4,5},{5,4},{6,7},{7,6},{8,9},{9,8},{10,11... | collective-permute-start | bytes 2359304 | tf_op jit(solution)/shard_map/ppermute | solution.py:643
  24.8 21.7 %collective-permute-start.6 = (f32[3,256,256]{2,1,0:T(8,128)S(1)}, f32[3,256,256]{2,1,0:T(8,128)S(1)}, u32[]{:S(2)}, u32[]{:S(2)}) collective-permute-start(f32[3,256,256]{2,1,0:T(8,128)S(1)} %get-tuple-element.138), channel_id=1, source_target_pairs={{1,2},{2,1},{5,6},{6,5},{9,10},{10,9},{13,14},{14,13},{17,18},{18,... | collective-permute-start | bytes 2359304 | tf_op jit(solution)/shard_map/ppermute | solution.py:647
  29.3 11.6 %collective-permute-start.4 = (f32[2,17,8,256]{3,2,1,0:T(8,128)S(1)}, f32[2,17,8,256]{3,2,1,0:T(8,128)S(1)}, u32[]{:S(2)}, u32[]{:S(2)}) collective-permute-start(f32[2,17,8,256]{3,2,1,0:T(8,128)S(1)} %get-tuple-element.134), channel_id=1, source_target_pairs={{0,64},{64,0},{1,65},{65,1},{2,66},{66,2},{3,67},{67,3},{4,68},{68... | collective-permute-start | bytes 835592 | tf_op jit(solution)/shard_map/ppermute | solution.py:651
  41.0 10.1 %collective-permute-start.7 = (f32[1,17,8,256]{3,2,1,0:T(8,128)S(1)}, f32[1,17,8,256]{3,2,1,0:T(8,128)S(1)}, u32[]{:S(2)}, u32[]{:S(2)}) collective-permute-start(f32[1,17,8,256]{3,2,1,0:T(8,128)S(1)} %get-tuple-element.143), channel_id=1, source_target_pairs={{0,1},{1,0},{2,3},{3,2},{4,5},{5,4},{6,7},{7,6},{8,9},{9,8},{10,11... | collective-permute-start | bytes 417800 | tf_op jit(solution)/shard_map/ppermute | solution.py:643
  41.1 10.0 %collective-permute-start.8 = (f32[1,17,8,256]{3,2,1,0:T(8,128)S(1)}, f32[1,17,8,256]{3,2,1,0:T(8,128)S(1)}, u32[]{:S(2)}, u32[]{:S(2)}) collective-permute-start(f32[1,17,8,256]{3,2,1,0:T(8,128)S(1)} %get-tuple-element.144), channel_id=1, source_target_pairs={{1,2},{2,1},{5,6},{6,5},{9,10},{10,9},{13,14},{14,13},{17,18},{18,... | collective-permute-start | bytes 417800 | tf_op jit(solution)/shard_map/ppermute | solution.py:647
  43.1 27.6 %collective-permute-start.11 = (f32[8,17,8,256]{3,2,1,0:T(8,128)S(1)}, f32[8,17,8,256]{3,2,1,0:T(8,128)S(1)}, u32[]{:S(2)}, u32[]{:S(2)}) collective-permute-start(f32[8,17,8,256]{3,2,1,0:T(8,128)S(1)} %get-tuple-element.155), channel_id=1, source_target_pairs={{0,64},{64,0},{1,65},{65,1},{2,66},{66,2},{3,67},{67,3},{4,68},{68... | collective-permute-start | bytes 3342344 | tf_op jit(solution)/shard_map/ppermute | solution.py:651
  54.2 11.1 %collective-permute-start.10 = (f32[2,17,8,256]{3,2,1,0:T(8,128)S(1)}, f32[2,17,8,256]{3,2,1,0:T(8,128)S(1)}, u32[]{:S(2)}, u32[]{:S(2)}) collective-permute-start(f32[2,17,8,256]{3,2,1,0:T(8,128)S(1)} %get-tuple-element.152), channel_id=1, source_target_pairs={{1,2},{2,1},{5,6},{6,5},{9,10},{10,9},{13,14},{14,13},{17,18},{18,... | collective-permute-start | bytes 835592 | tf_op jit(solution)/shard_map/ppermute | solution.py:647
  57.1 45.5 %collective-permute-start.20 = (f32[10,17,8,256]{3,2,1,0:T(8,128)S(1)}, f32[10,17,8,256]{3,2,1,0:T(8,128)S(1)}, u32[]{:S(2)}, u32[]{:S(2)}) collective-permute-start(f32[10,17,8,256]{3,2,1,0:T(8,128)S(1)} %get-tuple-element.180), channel_id=1, source_target_pairs={{0,64},{64,0},{1,65},{65,1},{2,66},{66,2},{3,67},{67,3},{4,68},{68... | collective-permute-start | bytes 4177928 | tf_op jit(solution)/shard_map/ppermute | solution.py:651
  67.6 9.5 %collective-permute-start.12 = (f32[2,17,8,256]{3,2,1,0:T(8,128)S(1)}, f32[2,17,8,256]{3,2,1,0:T(8,128)S(1)}, u32[]{:S(2)}, u32[]{:S(2)}) collective-permute-start(f32[2,17,8,256]{3,2,1,0:T(8,128)S(1)} %get-tuple-element.159), channel_id=1, source_target_pairs={{0,1},{1,0},{2,3},{3,2},{4,5},{5,4},{6,7},{7,6},{8,9},{9,8},{10,11... | collective-permute-start | bytes 835592 | tf_op jit(solution)/shard_map/ppermute | solution.py:643
  67.7 11.4 %collective-permute-start.13 = (f32[2,17,8,256]{3,2,1,0:T(8,128)S(1)}, f32[2,17,8,256]{3,2,1,0:T(8,128)S(1)}, u32[]{:S(2)}, u32[]{:S(2)}) collective-permute-start(f32[2,17,8,256]{3,2,1,0:T(8,128)S(1)} %get-tuple-element.160), channel_id=1, source_target_pairs={{1,2},{2,1},{5,6},{6,5},{9,10},{10,9},{13,14},{14,13},{17,18},{18,... | collective-permute-start | bytes 835592 | tf_op jit(solution)/shard_map/ppermute | solution.py:647
  70.8 13.3 %collective-permute-start.14 = (f32[1,17,8,256]{3,2,1,0:T(8,128)S(1)}, f32[1,17,8,256]{3,2,1,0:T(8,128)S(1)}, u32[]{:S(2)}, u32[]{:S(2)}) collective-permute-start(f32[1,17,8,256]{3,2,1,0:T(8,128)S(1)} %get-tuple-element.164), channel_id=1, source_target_pairs={{0,1},{1,0},{2,3},{3,2},{4,5},{5,4},{6,7},{7,6},{8,9},{9,8},{10,11... | collective-permute-start | bytes 417800 | tf_op jit(solution)/shard_map/ppermute | solution.py:643
  71.9 12.2 %collective-permute-start.15 = (f32[1,17,8,256]{3,2,1,0:T(8,128)S(1)}, f32[1,17,8,256]{3,2,1,0:T(8,128)S(1)}, u32[]{:S(2)}, u32[]{:S(2)}) collective-permute-start(f32[1,17,8,256]{3,2,1,0:T(8,128)S(1)} %get-tuple-element.165), channel_id=1, source_target_pairs={{1,2},{2,1},{5,6},{6,5},{9,10},{10,9},{13,14},{14,13},{17,18},{18,... | collective-permute-start | bytes 417800 | tf_op jit(solution)/shard_map/ppermute | solution.py:647
  81.5 10.1 %collective-permute-start.17 = (f32[2,17,8,256]{3,2,1,0:T(8,128)S(1)}, f32[2,17,8,256]{3,2,1,0:T(8,128)S(1)}, u32[]{:S(2)}, u32[]{:S(2)}) collective-permute-start(f32[2,17,8,256]{3,2,1,0:T(8,128)S(1)} %get-tuple-element.173), channel_id=1, source_target_pairs={{1,2},{2,1},{5,6},{6,5},{9,10},{10,9},{13,14},{14,13},{17,18},{18,... | collective-permute-start | bytes 835592 | tf_op jit(solution)/shard_map/ppermute | solution.py:647
  87.5 9.6 %collective-permute-start.19 = (f32[2,17,8,256]{3,2,1,0:T(8,128)S(1)}, f32[2,17,8,256]{3,2,1,0:T(8,128)S(1)}, u32[]{:S(2)}, u32[]{:S(2)}) collective-permute-start(f32[2,17,8,256]{3,2,1,0:T(8,128)S(1)} %get-tuple-element.177), channel_id=1, source_target_pairs={{1,2},{2,1},{5,6},{6,5},{9,10},{10,9},{13,14},{14,13},{17,18},{18,... | collective-permute-start | bytes 835592 | tf_op jit(solution)/shard_map/ppermute | solution.py:647
  99.5 10.6 %collective-permute-start.22 = (f32[2,17,8,256]{3,2,1,0:T(8,128)S(1)}, f32[2,17,8,256]{3,2,1,0:T(8,128)S(1)}, u32[]{:S(2)}, u32[]{:S(2)}) collective-permute-start(f32[2,17,8,256]{3,2,1,0:T(8,128)S(1)} %get-tuple-element.186), channel_id=1, source_target_pairs={{1,2},{2,1},{5,6},{6,5},{9,10},{10,9},{13,14},{14,13},{17,18},{18,... | collective-permute-start | bytes 835592 | tf_op jit(solution)/shard_map/ppermute | solution.py:647
  102.5 23.1 %collective-permute-start.27 = (f32[6,17,8,256]{3,2,1,0:T(8,128)S(1)}, f32[6,17,8,256]{3,2,1,0:T(8,128)S(1)}, u32[]{:S(2)}, u32[]{:S(2)}) collective-permute-start(f32[6,17,8,256]{3,2,1,0:T(8,128)S(1)} %get-tuple-element.199), channel_id=1, source_target_pairs={{0,64},{64,0},{1,65},{65,1},{2,66},{66,2},{3,67},{67,3},{4,68},{68... | collective-permute-start | bytes 2506760 | tf_op jit(solution)/shard_map/ppermute | solution.py:651
  102.9 11.7 %collective-permute-start.23 = (f32[2,17,8,256]{3,2,1,0:T(8,128)S(1)}, f32[2,17,8,256]{3,2,1,0:T(8,128)S(1)}, u32[]{:S(2)}, u32[]{:S(2)}) collective-permute-start(f32[2,17,8,256]{3,2,1,0:T(8,128)S(1)} %get-tuple-element.190), channel_id=1, source_target_pairs={{0,1},{1,0},{2,3},{3,2},{4,5},{5,4},{6,7},{7,6},{8,9},{9,8},{10,11... | collective-permute-start | bytes 835592 | tf_op jit(solution)/shard_map/ppermute | solution.py:643
  103.0 12.8 %collective-permute-start.24 = (f32[2,17,8,256]{3,2,1,0:T(8,128)S(1)}, f32[2,17,8,256]{3,2,1,0:T(8,128)S(1)}, u32[]{:S(2)}, u32[]{:S(2)}) collective-permute-start(f32[2,17,8,256]{3,2,1,0:T(8,128)S(1)} %get-tuple-element.191), channel_id=1, source_target_pairs={{1,2},{2,1},{5,6},{6,5},{9,10},{10,9},{13,14},{14,13},{17,18},{18,... | collective-permute-start | bytes 835592 | tf_op jit(solution)/shard_map/ppermute | solution.py:647
  112.6 9.6 %collective-permute-start.26 = (f32[2,17,8,256]{3,2,1,0:T(8,128)S(1)}, f32[2,17,8,256]{3,2,1,0:T(8,128)S(1)}, u32[]{:S(2)}, u32[]{:S(2)}) collective-permute-start(f32[2,17,8,256]{3,2,1,0:T(8,128)S(1)} %get-tuple-element.196), channel_id=1, source_target_pairs={{1,2},{2,1},{5,6},{6,5},{9,10},{10,9},{13,14},{14,13},{17,18},{18,... | collective-permute-start | bytes 835592 | tf_op jit(solution)/shard_map/ppermute | solution.py:647
  118.7 12.6 %collective-permute-start.28 = (f32[2,17,8,256]{3,2,1,0:T(8,128)S(1)}, f32[2,17,8,256]{3,2,1,0:T(8,128)S(1)}, u32[]{:S(2)}, u32[]{:S(2)}) collective-permute-start(f32[2,17,8,256]{3,2,1,0:T(8,128)S(1)} %get-tuple-element.204), channel_id=1, source_target_pairs={{0,1},{1,0},{2,3},{3,2},{4,5},{5,4},{6,7},{7,6},{8,9},{9,8},{10,11... | collective-permute-start | bytes 835592 | tf_op jit(solution)/shard_map/ppermute | solution.py:643
  118.8 12.5 %collective-permute-start.29 = (f32[2,17,8,256]{3,2,1,0:T(8,128)S(1)}, f32[2,17,8,256]{3,2,1,0:T(8,128)S(1)}, u32[]{:S(2)}, u32[]{:S(2)}) collective-permute-start(f32[2,17,8,256]{3,2,1,0:T(8,128)S(1)} %get-tuple-element.205), channel_id=1, source_target_pairs={{1,2},{2,1},{5,6},{6,5},{9,10},{10,9},{13,14},{14,13},{17,18},{18,... | collective-permute-start | bytes 835592 | tf_op jit(solution)/shard_map/ppermute | solution.py:647
  128.7 9.6 %collective-permute-start.30 = (f32[2,17,8,256]{3,2,1,0:T(8,128)S(1)}, f32[2,17,8,256]{3,2,1,0:T(8,128)S(1)}, u32[]{:S(2)}, u32[]{:S(2)}) collective-permute-start(f32[2,17,8,256]{3,2,1,0:T(8,128)S(1)} %get-tuple-element.209), channel_id=1, source_target_pairs={{0,1},{1,0},{2,3},{3,2},{4,5},{5,4},{6,7},{7,6},{8,9},{9,8},{10,11... | collective-permute-start | bytes 835592 | tf_op jit(solution)/shard_map/ppermute | solution.py:643
  128.8 11.4 %collective-permute-start.31 = (f32[2,17,8,256]{3,2,1,0:T(8,128)S(1)}, f32[2,17,8,256]{3,2,1,0:T(8,128)S(1)}, u32[]{:S(2)}, u32[]{:S(2)}) collective-permute-start(f32[2,17,8,256]{3,2,1,0:T(8,128)S(1)} %get-tuple-element.210), channel_id=1, source_target_pairs={{1,2},{2,1},{5,6},{6,5},{9,10},{10,9},{13,14},{14,13},{17,18},{18,... | collective-permute-start | bytes 835592 | tf_op jit(solution)/shard_map/ppermute | solution.py:647
  133.7 11.0 %collective-permute-start.32 = (f32[2,17,8,256]{3,2,1,0:T(8,128)S(1)}, f32[2,17,8,256]{3,2,1,0:T(8,128)S(1)}, u32[]{:S(2)}, u32[]{:S(2)}) collective-permute-start(f32[2,17,8,256]{3,2,1,0:T(8,128)S(1)} %get-tuple-element.214), channel_id=1, source_target_pairs={{0,1},{1,0},{2,3},{3,2},{4,5},{5,4},{6,7},{7,6},{8,9},{9,8},{10,11... | collective-permute-start | bytes 835592 | tf_op jit(solution)/shard_map/ppermute | solution.py:643
  133.9 12.2 %collective-permute-start.33 = (f32[2,17,8,256]{3,2,1,0:T(8,128)S(1)}, f32[2,17,8,256]{3,2,1,0:T(8,128)S(1)}, u32[]{:S(2)}, u32[]{:S(2)}) collective-permute-start(f32[2,17,8,256]{3,2,1,0:T(8,128)S(1)} %get-tuple-element.215), channel_id=1, source_target_pairs={{1,2},{2,1},{5,6},{6,5},{9,10},{10,9},{13,14},{14,13},{17,18},{18,... | collective-permute-start | bytes 835592 | tf_op jit(solution)/shard_map/ppermute | solution.py:647
  142.8 10.3 %collective-permute-start.35 = (f32[2,17,8,256]{3,2,1,0:T(8,128)S(1)}, f32[2,17,8,256]{3,2,1,0:T(8,128)S(1)}, u32[]{:S(2)}, u32[]{:S(2)}) collective-permute-start(f32[2,17,8,256]{3,2,1,0:T(8,128)S(1)} %get-tuple-element.219), channel_id=1, source_target_pairs={{1,2},{2,1},{5,6},{6,5},{9,10},{10,9},{13,14},{14,13},{17,18},{18,... | collective-permute-start | bytes 835592 | tf_op jit(solution)/shard_map/ppermute | solution.py:647
  148.5 9.9 %collective-permute-start.36 = (f32[2,17,8,256]{3,2,1,0:T(8,128)S(1)}, f32[2,17,8,256]{3,2,1,0:T(8,128)S(1)}, u32[]{:S(2)}, u32[]{:S(2)}) collective-permute-start(f32[2,17,8,256]{3,2,1,0:T(8,128)S(1)} %get-tuple-element.222), channel_id=1, source_target_pairs={{0,1},{1,0},{2,3},{3,2},{4,5},{5,4},{6,7},{7,6},{8,9},{9,8},{10,11... | collective-permute-start | bytes 835592 | tf_op jit(solution)/shard_map/ppermute | solution.py:643
  148.6 10.6 %collective-permute-start.37 = (f32[2,17,8,256]{3,2,1,0:T(8,128)S(1)}, f32[2,17,8,256]{3,2,1,0:T(8,128)S(1)}, u32[]{:S(2)}, u32[]{:S(2)}) collective-permute-start(f32[2,17,8,256]{3,2,1,0:T(8,128)S(1)} %get-tuple-element.223), channel_id=1, source_target_pairs={{1,2},{2,1},{5,6},{6,5},{9,10},{10,9},{13,14},{14,13},{17,18},{18,... | collective-permute-start | bytes 835592 | tf_op jit(solution)/shard_map/ppermute | solution.py:647
  (9 other events, 75.0 us)

commit v3 on v2

--- a/solution.py
+++ b/solution.py
@@ -820,7 +820,7 @@
     C, R, S, N, M, L = range(6)
     plan = (
         (R, 0), (C, 0), (C, 1), (S, 0), (N, 0), (R, 1), (M, 0), (S, 1), (L, 0), (N, 1), (R, 2),
-        (M, 1), (S, 2), (L, 1), (S, 3), (N, 2), (N, 3), (M, 2), (M, 3), (L, 2), (L, 3),
+        (M, 1), (S, 2), (S, 3), (L, 1), (N, 2), (N, 3), (M, 2), (M, 3), (L, 2), (L, 3),
     )
     for kind, unit in plan:
         if kind == C:

time: 169 us -> 166 us (0.982)
  waiting for transfers between devices: 38.7 us -> 34.5 us
    ppermute x17, waiting for transfers between devices: 18.2 us -> 15.8 us  [to_b(): return lax.ppermute(x, 'space', SWAP_B)]
    ppermute x17, waiting for transfers between devices: 12.9 us -> 11 us  [to_a(): return lax.ppermute(x, 'space', SWAP_A)]
  transfers between devices with their start and end apart: 40 -> 40, of which waited for: 22 -> 19; matrix products, arithmetic and copies ran while one was open for 0% -> 0% of each run, Pallas kernels for 40% -> 41%
where the time goes in v3:
time: 166 us; the launch traced here: 165 us
  Pallas kernels  71 us (43%)
  starting transfers between devices  58.8 us (35%)
  waiting for transfers between devices  34.5 us (21%)
    pallas_call x27, Pallas kernels, call(): pl.pallas_call(run, out_shape=[o if s is VM else jax.ShapeDtypeStruct(o,...  71 us
    ppermute x17, starting transfers between devices, to_b(): return lax.ppermute(x, 'space', SWAP_B)  47.4 us
    ppermute x17, waiting for transfers between devices, to_b(): return lax.ppermute(x, 'space', SWAP_B)  15.8 us
    ppermute x17, waiting for transfers between devices, to_a(): return lax.ppermute(x, 'space', SWAP_A)  11 us
    ppermute x5, waiting for transfers between devices, swap_nodes(): return lax.ppermute(x, 'node', [(0, 1), (1, 0)])  7.72 us
    ppermute x5, starting transfers between devices, swap_nodes(): return lax.ppermute(x, 'node', [(0, 1), (1, 0)])  6.21 us
  transfers between devices with their start and end apart: 40, of which 19 were waited for; matrix products, arithmetic and copies ran while one was open for 0% of the time, Pallas kernels for 41%

profile of v3, /device:TPU:14, one launch (start us, length us, event | category | flops | bytes accessed | tf_op | source)
XLA Modules:
  0.0 165.1 jit_solution(5710650199006977490)
XLA Ops:
  3.9 4.3 %collective-permute-start.1 = (f32[3,256,256]{2,1,0:T(8,128)S(1)}, f32[3,256,256]{2,1,0:T(8,128)S(1)}, u32[]{:S(2)}, u32[]{:S(2)}) collective-permute-start(f32[3,256,256]{2,1,0:T(8,128)S(1)} %get-tuple-element.125), channel_id=1, source_target_pairs={{1,2},{2,1},{5,6},{6,5},{9,10},{10,9},{13,14},{14,13},{17,18},{18,... | collective-permute-start | bytes 2359304 | tf_op jit(solution)/shard_map/ppermute | solution.py:647
  8.2 6.6 %inner0.1 = (f32[16,17,8,256]{3,2,1,0:T(8,128)S(1)}, f32[8,17,8,256]{3,2,1,0:T(8,128)S(1)}, f32[6,17,8,256]{3,2,1,0:T(8,128)S(1)}, f32[10,17,8,256]{3,2,1,0:T(8,...) custom-call(f32[8,128]{1,0:T(8,128)S(1)} %get-tuple-element.118.before, ...), custom_call_target="tpu_custom_call" | custom-call | flops 3500000000 | tf_op jit(solution)/shard_map/inner0/pallas_call | solution.py:87
  16.8 6.5 %inner1.1 = (f32[16,17,8,256]{3,2,1,0:T(8,128)S(1)}, f32[8,17,8,256]{3,2,1,0:T(8,128)S(1)}, f32[8,17,8,256]{3,2,1,0:T(8,128)S(1)}, f32[6,17,8,256]{3,2,1,0:T(8,1...) custom-call(f32[8,128]{1,0:T(8,128)S(1)} %get-tuple-element.119.before, ...), custom_call_target="tpu_custom_call" | custom-call | flops 3500000000 | tf_op jit(solution)/shard_map/inner1/pallas_call | solution.py:87
  26.8 2.5 %edge0.1 = (f32[2,17,8,256]{3,2,1,0:T(8,128)S(1)}, f32[10,17,8,256]{3,2,1,0:T(8,128)S(1)}, f32[2,17,8,256]{3,2,1,0:T(8,128)S(1)}, f32[2,17,8,256]{3,2,1,0:T(8,128)S(1)}, f32[8,128]{1,0:T(8,128)S(1)}) custom-call(f32[8,128]{1,0:T(8,128)S(1)} %get-tuple-element.121.before, ...), custom_call_target="tpu_custom_call", output_to_operand_aliasing={{1}: (5, {})} | custom-call | flops 1750000000 | tf_op jit(solution)/shard_map/edge0/pallas_call | solution.py:87
  30.9 4.0 %collective-permute-done.3.refs_7_.refs_0_ = f32[6,17,8,256]{3,2,1,0:T(8,128)S(1)} collective-permute-done((f32[6,17,8,256]{3,2,1,0:T(8,128)S(1)}, f32[6,17,8,256]{3,2,1,0:T(8,128)S(1)}, u32[]{:S(2)}, u32[]{:S(2)}) %collective-permute-start.3) | collective-permute-done | bytes 835616 | tf_op jit(solution)/shard_map/ppermute | solution.py:651
  34.9 2.5 %edge1.1 = (f32[8,17,8,256]{3,2,1,0:T(8,128)S(1)}, f32[10,17,8,256]{3,2,1,0:T(8,128)S(1)}, f32[2,17,8,256]{3,2,1,0:T(8,128)S(1)}, f32[2,17,8,256]{3,2,1,0:T(8,128)S(1)}, f32[8,128]{1,0:T(8,128)S(1)}) custom-call(f32[8,128]{1,0:T(8,128)S(1)} %get-tuple-element.127.before, ...), custom_call_target="tpu_custom_call", output_to_operand_aliasing={{0}: (5, {}), {1}: (6, {})} | custom-call | flops 1750000000 | tf_op jit(solution)/shard_map/edge1/pallas_call | solution.py:87
  37.4 3.5 %collective-permute-done.4.refs_0_ = f32[2,17,8,256]{3,2,1,0:T(8,128)S(1)} collective-permute-done((f32[2,17,8,256]{3,2,1,0:T(8,128)S(1)}, f32[2,17,8,256]{3,2,1,0:T(8,128)S(1)}, u32[]{:S(2)}, u32[]{:S(2)}) %collective-permute-start.4) | collective-permute-done | bytes 278560 | tf_op jit(solution)/shard_map/ppermute | solution.py:651
  43.2 2.4 %collective-permute-start.11 = (f32[8,17,8,256]{3,2,1,0:T(8,128)S(1)}, f32[8,17,8,256]{3,2,1,0:T(8,128)S(1)}, u32[]{:S(2)}, u32[]{:S(2)}) collective-permute-start(f32[8,17,8,256]{3,2,1,0:T(8,128)S(1)} %get-tuple-element.155), channel_id=1, source_target_pairs={{0,64},{64,0},{1,65},{65,1},{2,66},{66,2},{3,67},{67,3},{4,68},{68... | collective-permute-start | bytes 3342344 | tf_op jit(solution)/shard_map/ppermute | solution.py:651
  51.1 2.9 %first0.1 = (f32[10,17,8,256]{3,2,1,0:T(8,128)S(1)}, f32[8,17,8,256]{3,2,1,0:T(8,128)S(1)}, f32[2,17,8,256]{3,2,1,0:T(8,128)S(1)}, f32[2,17,8,256]{3,2,1,0:T(8,128)S(1)}, f32[8,128]{1,0:T(8,128)S(1)}) custom-call(f32[8,128]{1,0:T(8,128)S(1)} %get-tuple-element.140.before, f32[6,17,8,256]{3,2,1,0:T(8,128)S(1)} %collective-permute-done.3.refs_7_.refs_0_, ...), custom_call_target="tpu_custom_call" | custom-call | flops 2100000000 | tf_op jit(solution)/shard_map/first0/pallas_call | solution.py:87
  54.1 2.9 %collective-permute-start.10 = (f32[2,17,8,256]{3,2,1,0:T(8,128)S(1)}, f32[2,17,8,256]{3,2,1,0:T(8,128)S(1)}, u32[]{:S(2)}, u32[]{:S(2)}) collective-permute-start(f32[2,17,8,256]{3,2,1,0:T(8,128)S(1)} %get-tuple-element.152), channel_id=1, source_target_pairs={{1,2},{2,1},{5,6},{6,5},{9,10},{10,9},{13,14},{14,13},{17,18},{18,... | collective-permute-start | bytes 835592 | tf_op jit(solution)/shard_map/ppermute | solution.py:647
  57.2 6.1 %collective-permute-done.9.refs_1_ = f32[2,17,8,256]{3,2,1,0:T(8,128)S(1)} collective-permute-done((f32[2,17,8,256]{3,2,1,0:T(8,128)S(1)}, f32[2,17,8,256]{3,2,1,0:T(8,128)S(1)}, u32[]{:S(2)}, u32[]{:S(2)}) %collective-permute-start.9) | collective-permute-done | bytes 278560 | tf_op jit(solution)/shard_map/ppermute | solution.py:643
  67.7 2.8 %collective-permute-start.13 = (f32[2,17,8,256]{3,2,1,0:T(8,128)S(1)}, f32[2,17,8,256]{3,2,1,0:T(8,128)S(1)}, u32[]{:S(2)}, u32[]{:S(2)}) collective-permute-start(f32[2,17,8,256]{3,2,1,0:T(8,128)S(1)} %get-tuple-element.160), channel_id=1, source_target_pairs={{1,2},{2,1},{5,6},{6,5},{9,10},{10,9},{13,14},{14,13},{17,18},{18,... | collective-permute-start | bytes 835592 | tf_op jit(solution)/shard_map/ppermute | solution.py:647
  72.0 3.2 %collective-permute-start.15 = (f32[1,17,8,256]{3,2,1,0:T(8,128)S(1)}, f32[1,17,8,256]{3,2,1,0:T(8,128)S(1)}, u32[]{:S(2)}, u32[]{:S(2)}) collective-permute-start(f32[1,17,8,256]{3,2,1,0:T(8,128)S(1)} %get-tuple-element.165), channel_id=1, source_target_pairs={{1,2},{2,1},{5,6},{6,5},{9,10},{10,9},{13,14},{14,13},{17,18},{18,... | collective-permute-start | bytes 417800 | tf_op jit(solution)/shard_map/ppermute | solution.py:647
  81.4 2.6 %collective-permute-start.17 = (f32[2,17,8,256]{3,2,1,0:T(8,128)S(1)}, f32[2,17,8,256]{3,2,1,0:T(8,128)S(1)}, u32[]{:S(2)}, u32[]{:S(2)}) collective-permute-start(f32[2,17,8,256]{3,2,1,0:T(8,128)S(1)} %get-tuple-element.173), channel_id=1, source_target_pairs={{1,2},{2,1},{5,6},{6,5},{9,10},{10,9},{13,14},{14,13},{17,18},{18,... | collective-permute-start | bytes 835592 | tf_op jit(solution)/shard_map/ppermute | solution.py:647
  84.1 3.1 %first1.1 = (f32[10,17,8,256]{3,2,1,0:T(8,128)S(1)}, f32[8,17,8,256]{3,2,1,0:T(8,128)S(1)}, f32[2,17,8,256]{3,2,1,0:T(8,128)S(1)}, f32[2,17,8,256]{3,2,1,0:T(8,128)S(1)}, f32[8,128]{1,0:T(8,128)S(1)}) custom-call(f32[8,128]{1,0:T(8,128)S(1)} %get-tuple-element.161.before, f32[8,17,8,256]{3,2,1,0:T(8,128)S(1)} %collective-permute-done.11.refs_0_, ...), custom_call_target="tpu_custom_call" | custom-call | flops 2100000000 | tf_op jit(solution)/shard_map/first1/pallas_call | solution.py:87
  87.5 3.2 %collective-permute-start.19 = (f32[2,17,8,256]{3,2,1,0:T(8,128)S(1)}, f32[2,17,8,256]{3,2,1,0:T(8,128)S(1)}, u32[]{:S(2)}, u32[]{:S(2)}) collective-permute-start(f32[2,17,8,256]{3,2,1,0:T(8,128)S(1)} %get-tuple-element.177), channel_id=1, source_target_pairs={{1,2},{2,1},{5,6},{6,5},{9,10},{10,9},{13,14},{14,13},{17,18},{18,... | collective-permute-start | bytes 835592 | tf_op jit(solution)/shard_map/ppermute | solution.py:647
  91.5 3.3 %last0.1 = (f32[1,2,8,256,256]{4,3,2,1,0:T(8,128)}, f32[8,128]{1,0:T(8,128)S(1)}) custom-call(f32[8,128]{1,0:T(8,128)S(1)} %get-tuple-element.170.before, f32[8,17,8,256]{3,2,1,0:T(8,128)S(1)} %get-tuple-element.171.refs_0_, f32[2,17,8,256]{3,2,1,0:T(8,128)S(1)} %collective-permute-done.16.refs_1_, f32[2,17,8,256]{3,2,1,0:T(8,128)S(1)} %collective-permute-done.17.refs_2_, ...), custom_call_target="tpu_custom_call" | custom-call | flops 2449999872 | tf_op jit(solution)/shard_map/last0/pallas_call | solution.py:87
  99.5 3.0 %collective-permute-start.22 = (f32[2,17,8,256]{3,2,1,0:T(8,128)S(1)}, f32[2,17,8,256]{3,2,1,0:T(8,128)S(1)}, u32[]{:S(2)}, u32[]{:S(2)}) collective-permute-start(f32[2,17,8,256]{3,2,1,0:T(8,128)S(1)} %get-tuple-element.186), channel_id=1, source_target_pairs={{1,2},{2,1},{5,6},{6,5},{9,10},{10,9},{13,14},{14,13},{17,18},{18,... | collective-permute-start | bytes 835592 | tf_op jit(solution)/shard_map/ppermute | solution.py:647
  102.9 2.9 %collective-permute-start.24 = (f32[2,17,8,256]{3,2,1,0:T(8,128)S(1)}, f32[2,17,8,256]{3,2,1,0:T(8,128)S(1)}, u32[]{:S(2)}, u32[]{:S(2)}) collective-permute-start(f32[2,17,8,256]{3,2,1,0:T(8,128)S(1)} %get-tuple-element.191), channel_id=1, source_target_pairs={{1,2},{2,1},{5,6},{6,5},{9,10},{10,9},{13,14},{14,13},{17,18},{18,... | collective-permute-start | bytes 835592 | tf_op jit(solution)/shard_map/ppermute | solution.py:647
  105.8 2.5 %collective-permute-done.21.refs_1_ = f32[2,17,8,256]{3,2,1,0:T(8,128)S(1)} collective-permute-done((f32[2,17,8,256]{3,2,1,0:T(8,128)S(1)}, f32[2,17,8,256]{3,2,1,0:T(8,128)S(1)}, u32[]{:S(2)}, u32[]{:S(2)}) %collective-permute-start.21) | collective-permute-done | bytes 278560 | tf_op jit(solution)/shard_map/ppermute | solution.py:643
  115.8 2.9 %first2.1 = (f32[10,17,8,256]{3,2,1,0:T(8,128)S(1)}, f32[8,17,8,256]{3,2,1,0:T(8,128)S(1)}, f32[2,17,8,256]{3,2,1,0:T(8,128)S(1)}, f32[2,17,8,256]{3,2,1,0:T(8,128)S(1)}, f32[8,128]{1,0:T(8,128)S(1)}) custom-call(f32[8,128]{1,0:T(8,128)S(1)} %get-tuple-element.187.before, f32[10,17,8,256]{3,2,1,0:T(8,128)S(1)} %collective-permute-done.20.refs_0_.refs_1_, ...), custom_call_target="tpu_custom_call" | custom-call | flops 2100000000 | tf_op jit(solution)/shard_map/first2/pallas_call | solution.py:87
  118.8 2.6 %collective-permute-start.29 = (f32[2,17,8,256]{3,2,1,0:T(8,128)S(1)}, f32[2,17,8,256]{3,2,1,0:T(8,128)S(1)}, u32[]{:S(2)}, u32[]{:S(2)}) collective-permute-start(f32[2,17,8,256]{3,2,1,0:T(8,128)S(1)} %get-tuple-element.205), channel_id=1, source_target_pairs={{1,2},{2,1},{5,6},{6,5},{9,10},{10,9},{13,14},{14,13},{17,18},{18,... | collective-permute-start | bytes 835592 | tf_op jit(solution)/shard_map/ppermute | solution.py:647
  121.4 3.1 %first3.1 = (f32[10,17,8,256]{3,2,1,0:T(8,128)S(1)}, f32[8,17,8,256]{3,2,1,0:T(8,128)S(1)}, f32[2,17,8,256]{3,2,1,0:T(8,128)S(1)}, f32[2,17,8,256]{3,2,1,0:T(8,128)S(1)}, f32[8,128]{1,0:T(8,128)S(1)}) custom-call(f32[8,128]{1,0:T(8,128)S(1)} %get-tuple-element.193.before, f32[6,17,8,256]{3,2,1,0:T(8,128)S(1)} %collective-permute-done.25.refs_0_, ...), custom_call_target="tpu_custom_call" | custom-call | flops 2100000000 | tf_op jit(solution)/shard_map/first3/pallas_call | solution.py:87
  124.6 3.2 %collective-permute-start.31 = (f32[2,17,8,256]{3,2,1,0:T(8,128)S(1)}, f32[2,17,8,256]{3,2,1,0:T(8,128)S(1)}, u32[]{:S(2)}, u32[]{:S(2)}) collective-permute-start(f32[2,17,8,256]{3,2,1,0:T(8,128)S(1)} %get-tuple-element.210), channel_id=1, source_target_pairs={{1,2},{2,1},{5,6},{6,5},{9,10},{10,9},{13,14},{14,13},{17,18},{18,... | collective-permute-start | bytes 835592 | tf_op jit(solution)/shard_map/ppermute | solution.py:647
  127.9 3.4 %last1.1 = (f32[1,2,8,256,256]{4,3,2,1,0:T(8,128)}, f32[8,128]{1,0:T(8,128)S(1)}) custom-call(f32[8,128]{1,0:T(8,128)S(1)} %get-tuple-element.197.before, f32[8,17,8,256]{3,2,1,0:T(8,128)S(1)} %get-tuple-element.198.refs_0_, f32[2,17,8,256]{3,2,1,0:T(8,128)S(1)} %collective-permute-done.26.refs_1_, ...), custom_call_target="tpu_custom_call", output_to_operand_aliasing={{0}: (9, {})} | custom-call | flops 2449999872 | tf_op jit(solution)/shard_map/last1/pallas_call | solution.py:87
  133.7 2.6 %collective-permute-start.33 = (f32[2,17,8,256]{3,2,1,0:T(8,128)S(1)}, f32[2,17,8,256]{3,2,1,0:T(8,128)S(1)}, u32[]{:S(2)}, u32[]{:S(2)}) collective-permute-start(f32[2,17,8,256]{3,2,1,0:T(8,128)S(1)} %get-tuple-element.215), channel_id=1, source_target_pairs={{1,2},{2,1},{5,6},{6,5},{9,10},{10,9},{13,14},{14,13},{17,18},{18,... | collective-permute-start | bytes 835592 | tf_op jit(solution)/shard_map/ppermute | solution.py:647
  136.4 2.5 %next3_3.1 = (f32[8,17,8,256]{3,2,1,0:T(8,128)S(1)}, f32[2,17,8,256]{3,2,1,0:T(8,128)S(1)}, f32[2,17,8,256]{3,2,1,0:T(8,128)S(1)}, f32[8,128]{1,0:T(8,128)S(1)}) custom-call(f32[8,128]{1,0:T(8,128)S(1)} %get-tuple-element.207.before, f32[8,17,8,256]{3,2,1,0:T(8,128)S(1)} %get-tuple-element.208.refs_0_, ...), custom_call_target="tpu_custom_call" | custom-call | flops 1750000000 | tf_op jit(solution)/shard_map/next3_3/pallas_call | solution.py:87
  139.0 3.2 %collective-permute-start.35 = (f32[2,17,8,256]{3,2,1,0:T(8,128)S(1)}, f32[2,17,8,256]{3,2,1,0:T(8,128)S(1)}, u32[]{:S(2)}, u32[]{:S(2)}) collective-permute-start(f32[2,17,8,256]{3,2,1,0:T(8,128)S(1)} %get-tuple-element.219), channel_id=1, source_target_pairs={{1,2},{2,1},{5,6},{6,5},{9,10},{10,9},{13,14},{14,13},{17,18},{18,... | collective-permute-start | bytes 835592 | tf_op jit(solution)/shard_map/ppermute | solution.py:647
  149.9 2.4 %next3_4.1 = (f32[8,17,8,256]{3,2,1,0:T(8,128)S(1)}, f32[2,17,8,256]{3,2,1,0:T(8,128)S(1)}, f32[2,17,8,256]{3,2,1,0:T(8,128)S(1)}, f32[8,128]{1,0:T(8,128)S(1)}) custom-call(f32[8,128]{1,0:T(8,128)S(1)} %get-tuple-element.216.before, f32[8,17,8,256]{3,2,1,0:T(8,128)S(1)} %get-tuple-element.217.refs_0_, ...), custom_call_target="tpu_custom_call" | custom-call | flops 1750000000 | tf_op jit(solution)/shard_map/next3_4/pallas_call | solution.py:87
  152.4 3.0 %collective-permute-start.39 = (f32[2,17,8,256]{3,2,1,0:T(8,128)S(1)}, f32[2,17,8,256]{3,2,1,0:T(8,128)S(1)}, u32[]{:S(2)}, u32[]{:S(2)}) collective-permute-start(f32[2,17,8,256]{3,2,1,0:T(8,128)S(1)} %get-tuple-element.228), channel_id=1, source_target_pairs={{1,2},{2,1},{5,6},{6,5},{9,10},{10,9},{13,14},{14,13},{17,18},{18,... | collective-permute-start | bytes 835592 | tf_op jit(solution)/shard_map/ppermute | solution.py:647
  155.8 3.3 %last2.1 = (f32[1,2,8,256,256]{4,3,2,1,0:T(8,128)}, f32[8,128]{1,0:T(8,128)S(1)}) custom-call(f32[8,128]{1,0:T(8,128)S(1)} %get-tuple-element.220.before, f32[8,17,8,256]{3,2,1,0:T(8,128)S(1)} %get-tuple-element.221.refs_0_, f32[2,17,8,256]{3,2,1,0:T(8,128)S(1)} %collective-permute-done.36.refs_1_, ...), custom_call_target="tpu_custom_call", output_to_operand_aliasing={{0}: (9, {})} | custom-call | flops 2449999872 | tf_op jit(solution)/shard_map/last2/pallas_call | solution.py:87
  160.8 4.1 %last3.1 = (f32[1,2,8,256,256]{4,3,2,1,0:T(8,128)}, f32[8,128]{1,0:T(8,128)}) custom-call(f32[8,128]{1,0:T(8,128)S(1)} %get-tuple-element.225.before, f32[8,17,8,256]{3,2,1,0:T(8,128)S(1)} %get-tuple-element.226.refs_0_, f32[2,17,8,256]{3,2,1,0:T(8,128)S(1)} %collective-permute-done.38.refs_1_, ...), custom_call_target="tpu_custom_call", output_to_operand_aliasing={{0}: (9, {})} | custom-call | flops 2449999872 | tf_op jit(solution)/shard_map/last3/pallas_call | solution.py:87
  (78 shorter events, 57.1 us)
Async XLA Ops:
  0.0 34.9 %collective-permute-start.2 = (f32[8,256,256]{2,1,0:T(8,128)}, f32[8,256,256]{2,1,0:T(8,128)S(1)}, u32[]{:S(2)}, u32[]{:S(2)}) collective-permute-start(f32[8,256,256]{2,1,0:T(8,128)} %bitcast.1), channel_id=1, source_target_pairs={{0,4},{4,8},{8,12},{12,16},{16,20},{20,24},{24,28},{28,96},{32,36}... | collective-permute-start | bytes 6291464 | tf_op jit(solution)/shard_map/ppermute | solution.py:677
  3.3 21.5 %collective-permute-start = (f32[3,256,256]{2,1,0:T(8,128)S(1)}, f32[3,256,256]{2,1,0:T(8,128)S(1)}, u32[]{:S(2)}, u32[]{:S(2)}) collective-permute-start(f32[3,256,256]{2,1,0:T(8,128)S(1)} %get-tuple-element.124), channel_id=1, source_target_pairs={{0,1},{1,0},{2,3},{3,2},{4,5},{5,4},{6,7},{7,6},{8,9},{9,8},{10,11... | collective-permute-start | bytes 2359304 | tf_op jit(solution)/shard_map/ppermute | solution.py:643
  3.9 22.9 %collective-permute-start.1 = (f32[3,256,256]{2,1,0:T(8,128)S(1)}, f32[3,256,256]{2,1,0:T(8,128)S(1)}, u32[]{:S(2)}, u32[]{:S(2)}) collective-permute-start(f32[3,256,256]{2,1,0:T(8,128)S(1)} %get-tuple-element.125), channel_id=1, source_target_pairs={{1,2},{2,1},{5,6},{6,5},{9,10},{10,9},{13,14},{14,13},{17,18},{18,... | collective-permute-start | bytes 2359304 | tf_op jit(solution)/shard_map/ppermute | solution.py:647
  14.8 20.1 %collective-permute-start.3 = (f32[6,17,8,256]{3,2,1,0:T(8,128)S(1)}, f32[6,17,8,256]{3,2,1,0:T(8,128)S(1)}, u32[]{:S(2)}, u32[]{:S(2)}) collective-permute-start(f32[6,17,8,256]{3,2,1,0:T(8,128)S(1)} %get-tuple-element.132), channel_id=1, source_target_pairs={{0,64},{64,0},{1,65},{65,1},{2,66},{66,2},{3,67},{67,3},{4,68},{68... | collective-permute-start | bytes 2506760 | tf_op jit(solution)/shard_map/ppermute | solution.py:651
  24.8 20.8 %collective-permute-start.5 = (f32[3,256,256]{2,1,0:T(8,128)S(1)}, f32[3,256,256]{2,1,0:T(8,128)S(1)}, u32[]{:S(2)}, u32[]{:S(2)}) collective-permute-start(f32[3,256,256]{2,1,0:T(8,128)S(1)} %get-tuple-element.137), channel_id=1, source_target_pairs={{0,1},{1,0},{2,3},{3,2},{4,5},{5,4},{6,7},{7,6},{8,9},{9,8},{10,11... | collective-permute-start | bytes 2359304 | tf_op jit(solution)/shard_map/ppermute | solution.py:643
  24.9 21.7 %collective-permute-start.6 = (f32[3,256,256]{2,1,0:T(8,128)S(1)}, f32[3,256,256]{2,1,0:T(8,128)S(1)}, u32[]{:S(2)}, u32[]{:S(2)}) collective-permute-start(f32[3,256,256]{2,1,0:T(8,128)S(1)} %get-tuple-element.138), channel_id=1, source_target_pairs={{1,2},{2,1},{5,6},{6,5},{9,10},{10,9},{13,14},{14,13},{17,18},{18,... | collective-permute-start | bytes 2359304 | tf_op jit(solution)/shard_map/ppermute | solution.py:647
  29.3 11.5 %collective-permute-start.4 = (f32[2,17,8,256]{3,2,1,0:T(8,128)S(1)}, f32[2,17,8,256]{3,2,1,0:T(8,128)S(1)}, u32[]{:S(2)}, u32[]{:S(2)}) collective-permute-start(f32[2,17,8,256]{3,2,1,0:T(8,128)S(1)} %get-tuple-element.134), channel_id=1, source_target_pairs={{0,64},{64,0},{1,65},{65,1},{2,66},{66,2},{3,67},{67,3},{4,68},{68... | collective-permute-start | bytes 835592 | tf_op jit(solution)/shard_map/ppermute | solution.py:651
  41.0 10.1 %collective-permute-start.7 = (f32[1,17,8,256]{3,2,1,0:T(8,128)S(1)}, f32[1,17,8,256]{3,2,1,0:T(8,128)S(1)}, u32[]{:S(2)}, u32[]{:S(2)}) collective-permute-start(f32[1,17,8,256]{3,2,1,0:T(8,128)S(1)} %get-tuple-element.143), channel_id=1, source_target_pairs={{0,1},{1,0},{2,3},{3,2},{4,5},{5,4},{6,7},{7,6},{8,9},{9,8},{10,11... | collective-permute-start | bytes 417800 | tf_op jit(solution)/shard_map/ppermute | solution.py:643
  41.1 10.0 %collective-permute-start.8 = (f32[1,17,8,256]{3,2,1,0:T(8,128)S(1)}, f32[1,17,8,256]{3,2,1,0:T(8,128)S(1)}, u32[]{:S(2)}, u32[]{:S(2)}) collective-permute-start(f32[1,17,8,256]{3,2,1,0:T(8,128)S(1)} %get-tuple-element.144), channel_id=1, source_target_pairs={{1,2},{2,1},{5,6},{6,5},{9,10},{10,9},{13,14},{14,13},{17,18},{18,... | collective-permute-start | bytes 417800 | tf_op jit(solution)/shard_map/ppermute | solution.py:647
  43.2 27.5 %collective-permute-start.11 = (f32[8,17,8,256]{3,2,1,0:T(8,128)S(1)}, f32[8,17,8,256]{3,2,1,0:T(8,128)S(1)}, u32[]{:S(2)}, u32[]{:S(2)}) collective-permute-start(f32[8,17,8,256]{3,2,1,0:T(8,128)S(1)} %get-tuple-element.155), channel_id=1, source_target_pairs={{0,64},{64,0},{1,65},{65,1},{2,66},{66,2},{3,67},{67,3},{4,68},{68... | collective-permute-start | bytes 3342344 | tf_op jit(solution)/shard_map/ppermute | solution.py:651
  54.1 11.1 %collective-permute-start.10 = (f32[2,17,8,256]{3,2,1,0:T(8,128)S(1)}, f32[2,17,8,256]{3,2,1,0:T(8,128)S(1)}, u32[]{:S(2)}, u32[]{:S(2)}) collective-permute-start(f32[2,17,8,256]{3,2,1,0:T(8,128)S(1)} %get-tuple-element.152), channel_id=1, source_target_pairs={{1,2},{2,1},{5,6},{6,5},{9,10},{10,9},{13,14},{14,13},{17,18},{18,... | collective-permute-start | bytes 835592 | tf_op jit(solution)/shard_map/ppermute | solution.py:647
  57.1 45.4 %collective-permute-start.20 = (f32[10,17,8,256]{3,2,1,0:T(8,128)S(1)}, f32[10,17,8,256]{3,2,1,0:T(8,128)S(1)}, u32[]{:S(2)}, u32[]{:S(2)}) collective-permute-start(f32[10,17,8,256]{3,2,1,0:T(8,128)S(1)} %get-tuple-element.180), channel_id=1, source_target_pairs={{0,64},{64,0},{1,65},{65,1},{2,66},{66,2},{3,67},{67,3},{4,68},{68... | collective-permute-start | bytes 4177928 | tf_op jit(solution)/shard_map/ppermute | solution.py:651
  67.6 9.5 %collective-permute-start.12 = (f32[2,17,8,256]{3,2,1,0:T(8,128)S(1)}, f32[2,17,8,256]{3,2,1,0:T(8,128)S(1)}, u32[]{:S(2)}, u32[]{:S(2)}) collective-permute-start(f32[2,17,8,256]{3,2,1,0:T(8,128)S(1)} %get-tuple-element.159), channel_id=1, source_target_pairs={{0,1},{1,0},{2,3},{3,2},{4,5},{5,4},{6,7},{7,6},{8,9},{9,8},{10,11... | collective-permute-start | bytes 835592 | tf_op jit(solution)/shard_map/ppermute | solution.py:643
  67.7 11.4 %collective-permute-start.13 = (f32[2,17,8,256]{3,2,1,0:T(8,128)S(1)}, f32[2,17,8,256]{3,2,1,0:T(8,128)S(1)}, u32[]{:S(2)}, u32[]{:S(2)}) collective-permute-start(f32[2,17,8,256]{3,2,1,0:T(8,128)S(1)} %get-tuple-element.160), channel_id=1, source_target_pairs={{1,2},{2,1},{5,6},{6,5},{9,10},{10,9},{13,14},{14,13},{17,18},{18,... | collective-permute-start | bytes 835592 | tf_op jit(solution)/shard_map/ppermute | solution.py:647
  70.8 13.2 %collective-permute-start.14 = (f32[1,17,8,256]{3,2,1,0:T(8,128)S(1)}, f32[1,17,8,256]{3,2,1,0:T(8,128)S(1)}, u32[]{:S(2)}, u32[]{:S(2)}) collective-permute-start(f32[1,17,8,256]{3,2,1,0:T(8,128)S(1)} %get-tuple-element.164), channel_id=1, source_target_pairs={{0,1},{1,0},{2,3},{3,2},{4,5},{5,4},{6,7},{7,6},{8,9},{9,8},{10,11... | collective-permute-start | bytes 417800 | tf_op jit(solution)/shard_map/ppermute | solution.py:643
  72.0 12.1 %collective-permute-start.15 = (f32[1,17,8,256]{3,2,1,0:T(8,128)S(1)}, f32[1,17,8,256]{3,2,1,0:T(8,128)S(1)}, u32[]{:S(2)}, u32[]{:S(2)}) collective-permute-start(f32[1,17,8,256]{3,2,1,0:T(8,128)S(1)} %get-tuple-element.165), channel_id=1, source_target_pairs={{1,2},{2,1},{5,6},{6,5},{9,10},{10,9},{13,14},{14,13},{17,18},{18,... | collective-permute-start | bytes 417800 | tf_op jit(solution)/shard_map/ppermute | solution.py:647
  81.4 10.1 %collective-permute-start.17 = (f32[2,17,8,256]{3,2,1,0:T(8,128)S(1)}, f32[2,17,8,256]{3,2,1,0:T(8,128)S(1)}, u32[]{:S(2)}, u32[]{:S(2)}) collective-permute-start(f32[2,17,8,256]{3,2,1,0:T(8,128)S(1)} %get-tuple-element.173), channel_id=1, source_target_pairs={{1,2},{2,1},{5,6},{6,5},{9,10},{10,9},{13,14},{14,13},{17,18},{18,... | collective-permute-start | bytes 835592 | tf_op jit(solution)/shard_map/ppermute | solution.py:647
  87.5 9.6 %collective-permute-start.19 = (f32[2,17,8,256]{3,2,1,0:T(8,128)S(1)}, f32[2,17,8,256]{3,2,1,0:T(8,128)S(1)}, u32[]{:S(2)}, u32[]{:S(2)}) collective-permute-start(f32[2,17,8,256]{3,2,1,0:T(8,128)S(1)} %get-tuple-element.177), channel_id=1, source_target_pairs={{1,2},{2,1},{5,6},{6,5},{9,10},{10,9},{13,14},{14,13},{17,18},{18,... | collective-permute-start | bytes 835592 | tf_op jit(solution)/shard_map/ppermute | solution.py:647
  90.7 30.7 %collective-permute-start.25 = (f32[6,17,8,256]{3,2,1,0:T(8,128)S(1)}, f32[6,17,8,256]{3,2,1,0:T(8,128)S(1)}, u32[]{:S(2)}, u32[]{:S(2)}) collective-permute-start(f32[6,17,8,256]{3,2,1,0:T(8,128)S(1)} %get-tuple-element.194), channel_id=1, source_target_pairs={{0,64},{64,0},{1,65},{65,1},{2,66},{66,2},{3,67},{67,3},{4,68},{68... | collective-permute-start | bytes 2506760 | tf_op jit(solution)/shard_map/ppermute | solution.py:651
  99.5 10.5 %collective-permute-start.22 = (f32[2,17,8,256]{3,2,1,0:T(8,128)S(1)}, f32[2,17,8,256]{3,2,1,0:T(8,128)S(1)}, u32[]{:S(2)}, u32[]{:S(2)}) collective-permute-start(f32[2,17,8,256]{3,2,1,0:T(8,128)S(1)} %get-tuple-element.186), channel_id=1, source_target_pairs={{1,2},{2,1},{5,6},{6,5},{9,10},{10,9},{13,14},{14,13},{17,18},{18,... | collective-permute-start | bytes 835592 | tf_op jit(solution)/shard_map/ppermute | solution.py:647
  102.8 11.7 %collective-permute-start.23 = (f32[2,17,8,256]{3,2,1,0:T(8,128)S(1)}, f32[2,17,8,256]{3,2,1,0:T(8,128)S(1)}, u32[]{:S(2)}, u32[]{:S(2)}) collective-permute-start(f32[2,17,8,256]{3,2,1,0:T(8,128)S(1)} %get-tuple-element.190), channel_id=1, source_target_pairs={{0,1},{1,0},{2,3},{3,2},{4,5},{5,4},{6,7},{7,6},{8,9},{9,8},{10,11... | collective-permute-start | bytes 835592 | tf_op jit(solution)/shard_map/ppermute | solution.py:643
  102.9 12.9 %collective-permute-start.24 = (f32[2,17,8,256]{3,2,1,0:T(8,128)S(1)}, f32[2,17,8,256]{3,2,1,0:T(8,128)S(1)}, u32[]{:S(2)}, u32[]{:S(2)}) collective-permute-start(f32[2,17,8,256]{3,2,1,0:T(8,128)S(1)} %get-tuple-element.191), channel_id=1, source_target_pairs={{1,2},{2,1},{5,6},{6,5},{9,10},{10,9},{13,14},{14,13},{17,18},{18,... | collective-permute-start | bytes 835592 | tf_op jit(solution)/shard_map/ppermute | solution.py:647
  112.4 12.3 %collective-permute-start.26 = (f32[2,17,8,256]{3,2,1,0:T(8,128)S(1)}, f32[2,17,8,256]{3,2,1,0:T(8,128)S(1)}, u32[]{:S(2)}, u32[]{:S(2)}) collective-permute-start(f32[2,17,8,256]{3,2,1,0:T(8,128)S(1)} %get-tuple-element.199), channel_id=1, source_target_pairs={{0,1},{1,0},{2,3},{3,2},{4,5},{5,4},{6,7},{7,6},{8,9},{9,8},{10,11... | collective-permute-start | bytes 835592 | tf_op jit(solution)/shard_map/ppermute | solution.py:643
  112.5 15.4 %collective-permute-start.27 = (f32[2,17,8,256]{3,2,1,0:T(8,128)S(1)}, f32[2,17,8,256]{3,2,1,0:T(8,128)S(1)}, u32[]{:S(2)}, u32[]{:S(2)}) collective-permute-start(f32[2,17,8,256]{3,2,1,0:T(8,128)S(1)} %get-tuple-element.200), channel_id=1, source_target_pairs={{1,2},{2,1},{5,6},{6,5},{9,10},{10,9},{13,14},{14,13},{17,18},{18,... | collective-permute-start | bytes 835592 | tf_op jit(solution)/shard_map/ppermute | solution.py:647
  118.7 12.6 %collective-permute-start.28 = (f32[2,17,8,256]{3,2,1,0:T(8,128)S(1)}, f32[2,17,8,256]{3,2,1,0:T(8,128)S(1)}, u32[]{:S(2)}, u32[]{:S(2)}) collective-permute-start(f32[2,17,8,256]{3,2,1,0:T(8,128)S(1)} %get-tuple-element.204), channel_id=1, source_target_pairs={{0,1},{1,0},{2,3},{3,2},{4,5},{5,4},{6,7},{7,6},{8,9},{9,8},{10,11... | collective-permute-start | bytes 835592 | tf_op jit(solution)/shard_map/ppermute | solution.py:643
  118.8 12.5 %collective-permute-start.29 = (f32[2,17,8,256]{3,2,1,0:T(8,128)S(1)}, f32[2,17,8,256]{3,2,1,0:T(8,128)S(1)}, u32[]{:S(2)}, u32[]{:S(2)}) collective-permute-start(f32[2,17,8,256]{3,2,1,0:T(8,128)S(1)} %get-tuple-element.205), channel_id=1, source_target_pairs={{1,2},{2,1},{5,6},{6,5},{9,10},{10,9},{13,14},{14,13},{17,18},{18,... | collective-permute-start | bytes 835592 | tf_op jit(solution)/shard_map/ppermute | solution.py:647
  124.5 11.9 %collective-permute-start.30 = (f32[2,17,8,256]{3,2,1,0:T(8,128)S(1)}, f32[2,17,8,256]{3,2,1,0:T(8,128)S(1)}, u32[]{:S(2)}, u32[]{:S(2)}) collective-permute-start(f32[2,17,8,256]{3,2,1,0:T(8,128)S(1)} %get-tuple-element.209), channel_id=1, source_target_pairs={{0,1},{1,0},{2,3},{3,2},{4,5},{5,4},{6,7},{7,6},{8,9},{9,8},{10,11... | collective-permute-start | bytes 835592 | tf_op jit(solution)/shard_map/ppermute | solution.py:643
  124.6 11.8 %collective-permute-start.31 = (f32[2,17,8,256]{3,2,1,0:T(8,128)S(1)}, f32[2,17,8,256]{3,2,1,0:T(8,128)S(1)}, u32[]{:S(2)}, u32[]{:S(2)}) collective-permute-start(f32[2,17,8,256]{3,2,1,0:T(8,128)S(1)} %get-tuple-element.210), channel_id=1, source_target_pairs={{1,2},{2,1},{5,6},{6,5},{9,10},{10,9},{13,14},{14,13},{17,18},{18,... | collective-permute-start | bytes 835592 | tf_op jit(solution)/shard_map/ppermute | solution.py:647
  133.7 9.8 %collective-permute-start.33 = (f32[2,17,8,256]{3,2,1,0:T(8,128)S(1)}, f32[2,17,8,256]{3,2,1,0:T(8,128)S(1)}, u32[]{:S(2)}, u32[]{:S(2)}) collective-permute-start(f32[2,17,8,256]{3,2,1,0:T(8,128)S(1)} %get-tuple-element.215), channel_id=1, source_target_pairs={{1,2},{2,1},{5,6},{6,5},{9,10},{10,9},{13,14},{14,13},{17,18},{18,... | collective-permute-start | bytes 835592 | tf_op jit(solution)/shard_map/ppermute | solution.py:647
  139.0 10.9 %collective-permute-start.35 = (f32[2,17,8,256]{3,2,1,0:T(8,128)S(1)}, f32[2,17,8,256]{3,2,1,0:T(8,128)S(1)}, u32[]{:S(2)}, u32[]{:S(2)}) collective-permute-start(f32[2,17,8,256]{3,2,1,0:T(8,128)S(1)} %get-tuple-element.219), channel_id=1, source_target_pairs={{1,2},{2,1},{5,6},{6,5},{9,10},{10,9},{13,14},{14,13},{17,18},{18,... | collective-permute-start | bytes 835592 | tf_op jit(solution)/shard_map/ppermute | solution.py:647
  145.9 9.5 %collective-permute-start.36 = (f32[2,17,8,256]{3,2,1,0:T(8,128)S(1)}, f32[2,17,8,256]{3,2,1,0:T(8,128)S(1)}, u32[]{:S(2)}, u32[]{:S(2)}) collective-permute-start(f32[2,17,8,256]{3,2,1,0:T(8,128)S(1)} %get-tuple-element.222), channel_id=1, source_target_pairs={{0,1},{1,0},{2,3},{3,2},{4,5},{5,4},{6,7},{7,6},{8,9},{9,8},{10,11... | collective-permute-start | bytes 835592 | tf_op jit(solution)/shard_map/ppermute | solution.py:643
  146.0 9.8 %collective-permute-start.37 = (f32[2,17,8,256]{3,2,1,0:T(8,128)S(1)}, f32[2,17,8,256]{3,2,1,0:T(8,128)S(1)}, u32[]{:S(2)}, u32[]{:S(2)}) collective-permute-start(f32[2,17,8,256]{3,2,1,0:T(8,128)S(1)} %get-tuple-element.223), channel_id=1, source_target_pairs={{1,2},{2,1},{5,6},{6,5},{9,10},{10,9},{13,14},{14,13},{17,18},{18,... | collective-permute-start | bytes 835592 | tf_op jit(solution)/shard_map/ppermute | solution.py:647
  (9 other events, 74.3 us)
